TPU v7x, 256 devices: a whole 4x4x8 slice. The times are simulated.
256 devices in a mesh: gx: 16 (over z, core), gy: 16 (over x, y).
Axes of the slice: x: 4, y: 4, z: 8, core: 2. Of those that a mesh axis runs over, the one named last changes fastest.
Arguments:
- state: float32 [5, 1, 4096, 4096], P(None, None, 'gx', 'gy'), may hold values from -1.6 to 6.4, as said below
- viscous: float32 [1, 4096, 4096], P(None, 'gx', 'gy'), may hold values from 0.5 to 2000000
Outputs:
- new_state: float32 [5, 1, 4096, 4096], P(None, None, 'gx', 'gy')
Inputs may be any that keep to these rules, and one draw needn't show every extreme that they name: state[0] and 0.4 (state[4] - 0.5 (state[1]^2 + state[2]^2 + state[3]^2) / state[0]) lie between 0.6 and 1.6 in every cell.
All inputs are finite; a program needn't handle non-finite values.
Results may differ from a plain program's by a relative error of at most 0.00055.
Values sent between devices are 32-bit elements; how exact they have to be, the bound alone decides.
No kernel may reach another device: no remote copies, remote signals or barrier semaphores. Data moves between devices by JAX's collectives and lax.ppermute only.
A program may use at most 128 MiB of HBM per device.

v0:
```python
import jax
import jax.numpy as jnp
from jax import lax
from jax.sharding import PartitionSpec as P

STEP_RATIO = 0.25
ONE_THIRD = 1.0 / 3.0
NEAR_WEIGHT = 7.0 / 9.0
FAR_WEIGHT = 1.0 / 36.0
GAMMA_MINUS = 0.4
block_rows = 8


def shifted(value, axis, steps):
    count = lax.axis_size(axis)
    first, last = (max(0, -steps), min(count, count - steps))
    return lax.ppermute(value, axis, [(source, source + steps) for source in range(first, last)])


def with_halo(array, sides, width):
    for axis, dim in sides:
        devices, length = (lax.axis_size(axis), array.shape[dim])
        up = [(i, (i + 1) % devices) for i in range(devices - 1)]
        down = [(j, i) for i, j in up]
        last = lax.slice_in_dim(array, length - width, length, axis=dim)
        first = lax.slice_in_dim(array, 0, width, axis=dim)
        before = lax.ppermute(last, axis, up)
        after = lax.ppermute(first, axis, down)
        array = jnp.concatenate([before, array, after], axis=dim)
    return array


def pressure(fields, density):
    kinetic = fields[1] * fields[1] + fields[2] * fields[2] + fields[3] * fields[3]
    return GAMMA_MINUS * (fields[4] - 0.5 * kinetic / density)


def shifted_slice(extended, along_dim, extent, offset):
    return lax.slice_in_dim(extended, 2 + offset, 2 + offset + extent, axis=along_dim)


def mass_rows(extended, along_dim, extent):
    return shifted_slice(extended, along_dim, extent, 0) + ONE_THIRD * (
        shifted_slice(extended, along_dim, extent, -1)
        + shifted_slice(extended, along_dim, extent, 1)
    )


def central_rows(extended, along_dim, extent):
    return NEAR_WEIGHT * (
        shifted_slice(extended, along_dim, extent, 1)
        - shifted_slice(extended, along_dim, extent, -1)
    ) + FAR_WEIGHT * (
        shifted_slice(extended, along_dim, extent, 2)
        - shifted_slice(extended, along_dim, extent, -2)
    )


def face_rows(extended, along_dim, extent):
    middle = shifted_slice(extended, along_dim, extent, 0)
    face_low = 0.5 * (shifted_slice(extended, along_dim, extent, -1) + middle)
    face_high = 0.5 * (middle + shifted_slice(extended, along_dim, extent, 1))
    return (ONE_THIRD - face_low, 1.0 + face_low + face_high, ONE_THIRD - face_high)


def eliminate(lower, diagonal, upper):
    extent = len(diagonal)
    inverse = [None] * extent
    slopes = [None] * extent
    for position in range(1, extent - 1):
        if position == 1:
            pivot = diagonal[position]
        else:
            pivot = diagonal[position] - lower[position] * slopes[position - 1]
        inverse[position] = 1.0 / pivot
        slopes[position] = upper[position] * inverse[position]
    return (inverse, slopes)


def substitute(lower, inverse, slopes, source):
    extent = len(inverse)
    forward = [None] * extent
    for position in range(1, extent - 1):
        if position == 1:
            carried = source[position]
        else:
            carried = source[position] - lower[position] * forward[position - 1]
        forward[position] = carried * inverse[position]
    solution = [None] * extent
    solution[extent - 2] = forward[extent - 2]
    for position in range(extent - 3, 0, -1):
        solution[position] = forward[position] - slopes[position] * solution[position + 1]
    return solution


def couplings(lower, diagonal, upper):
    extent = len(diagonal)
    inverse, slopes = eliminate(lower, diagonal, upper)
    left_source = [0.0] * extent
    left_source[1] = -lower[1]
    right_source = [0.0] * extent
    right_source[extent - 2] = -upper[extent - 2]
    left_part = substitute(lower, inverse, slopes, left_source)
    right_part = substitute(lower, inverse, slopes, right_source)
    condensed = (
        lower[0],
        diagonal[0] + upper[0] * left_part[1],
        upper[0] * right_part[1],
        lower[extent - 1] * left_part[extent - 2],
        diagonal[extent - 1] + lower[extent - 1] * right_part[extent - 2],
        upper[extent - 1],
    )
    return (inverse, slopes, left_part, right_part, condensed)


def condense(lower, upper, inverse, slopes, source):
    extent = len(source)
    particular = substitute(lower, inverse, slopes, source)
    source_first = source[0] - upper[0] * particular[1]
    source_last = source[extent - 1] - lower[extent - 1] * particular[extent - 2]
    return (particular, source_first, source_last)


def expand(particular, left_part, right_part, first_row, last_row, along_dim):
    extent = len(particular)
    inner = [
        particular[position] + left_part[position] * first_row + right_part[position] * last_row
        for position in range(1, extent - 1)
    ]
    return jnp.stack([first_row] + inner + [last_row], along_dim)


def split_level(lower, diagonal, upper, source):
    extent = diagonal.shape[-2]
    lane_count = diagonal.shape[-1]
    sub_rows = block_rows if extent % block_rows == 0 else extent
    groups = extent // sub_rows

    def rows_of(values):
        shaped = values.reshape(values.shape[:-2] + (groups, sub_rows, lane_count))
        return [shaped[..., :, position, :] for position in range(sub_rows)]

    lower_rows = rows_of(lower)
    upper_rows = rows_of(upper)
    inverse, slopes, left_part, right_part, condensed = couplings(
        lower_rows, rows_of(diagonal), upper_rows
    )
    particular, source_first, source_last = condense(
        lower_rows, upper_rows, inverse, slopes, rows_of(source)
    )

    def pair_rows(first_row, last_row):
        paired = jnp.stack([first_row, last_row], -2)
        return paired.reshape(paired.shape[:-3] + (2 * groups, lane_count))

    reduced = (
        pair_rows(condensed[0], condensed[3]),
        pair_rows(condensed[1], condensed[4]),
        pair_rows(condensed[2], condensed[5]),
        pair_rows(source_first, source_last),
    )
    return ((particular, left_part, right_part), reduced)


def rebuild_level(retained, reduced_solution):
    particular, left_part, right_part = retained
    lane_count = reduced_solution.shape[-1]
    groups = reduced_solution.shape[-2] // 2
    paired = reduced_solution.reshape(reduced_solution.shape[:-2] + (groups, 2, lane_count))
    expanded = expand(particular, left_part, right_part, paired[..., 0, :], paired[..., 1, :], -2)
    return expanded.reshape(expanded.shape[:-3] + (groups * expanded.shape[-2], lane_count))


def reduce_lines(lower, diagonal, upper, source):
    levels = []
    while diagonal.shape[-2] > 2:
        retained, reduced = split_level(lower, diagonal, upper, source)
        lower, diagonal, upper, source = reduced
        levels.append(retained)
    condensed = (
        lower[..., 0, :],
        diagonal[..., 0, :],
        upper[..., 0, :],
        lower[..., 1, :],
        diagonal[..., 1, :],
        upper[..., 1, :],
    )
    return (levels, condensed, source[..., 0, :], source[..., 1, :])


def rebuild_lines(levels, first_row, last_row):
    solution = jnp.stack([first_row, last_row], -2)
    for retained in reversed(levels):
        solution = rebuild_level(retained, solution)
    return solution


def sweep_pair(condensed, source_first, source_last, incoming):
    lower_first, diag_first, upper_first, lower_last, diag_last, upper_last = condensed
    pivot_first = 1.0 / (diag_first - lower_first * incoming[0])
    slope_first = upper_first * pivot_first
    value_first = (source_first - lower_first * incoming[1:]) * pivot_first
    pivot_last = 1.0 / (diag_last - lower_last * slope_first)
    slope_last = upper_last * pivot_last
    value_last = (source_last - lower_last * value_first) * pivot_last
    return (slope_first, value_first, slope_last, value_last)


def relay_chain(condensed, source_first, source_last):
    initial = jnp.zeros((6,) + condensed[1].shape, jnp.float32)

    def forward_turn(turn, incoming):
        slope_first, value_first, slope_last, value_last = sweep_pair(
            condensed, source_first, source_last, incoming
        )
        outgoing = jnp.concatenate([slope_last[None], value_last], 0)
        return shifted(outgoing, "gx", 1)

    incoming = lax.fori_loop(0, lax.axis_size("gx") - 1, forward_turn, initial)
    slope_first, value_first, slope_last, value_last = sweep_pair(
        condensed, source_first, source_last, incoming
    )

    def backward_turn(turn, following):
        x_last = value_last - slope_last * following
        return shifted(value_first - slope_first * x_last, "gx", -1)

    following = lax.fori_loop(
        0, lax.axis_size("gx") - 1, backward_turn, jnp.zeros_like(value_first)
    )
    x_last = value_last - slope_last * following
    return (value_first - slope_first * x_last, x_last)


def chained_solve(lower, diagonal, upper, source, chain):
    levels, condensed, source_first, source_last = reduce_lines(lower, diagonal, upper, source)
    first_row, last_row = chain(condensed, source_first, source_last)
    return rebuild_lines(levels, first_row, last_row)


def entries(row_table, start_at, stop_at):
    return row_table[..., start_at:stop_at, :, :]


def protect(row_table, is_valid):
    return jnp.concatenate(
        [
            entries(row_table, 0, 1),
            jnp.where(is_valid, entries(row_table, 1, 2), 1.0),
            entries(row_table, 2, 8),
        ],
        -3,
    )


def combine_rows(center, lower_row, upper_row):
    weight_low = -entries(center, 0, 1) / entries(lower_row, 1, 2)
    weight_high = -entries(center, 2, 3) / entries(upper_row, 1, 2)
    return jnp.concatenate(
        [
            weight_low * entries(lower_row, 0, 1),
            entries(center, 1, 2)
            + weight_low * entries(lower_row, 2, 3)
            + weight_high * entries(upper_row, 0, 1),
            weight_high * entries(upper_row, 2, 3),
            entries(center, 3, 8)
            + weight_low * entries(lower_row, 3, 8)
            + weight_high * entries(upper_row, 3, 8),
        ],
        -3,
    )


def pack_slot(lower, diagonal, upper, source):
    return jnp.concatenate([lower[None], diagonal[None], upper[None], source], 0)


def cyclic_rows(boundary):
    my_index = lax.axis_index("gy")
    extent = lax.axis_size("gy")
    from_below = protect(shifted(boundary[1], "gy", 1), my_index >= 1)
    from_above = protect(shifted(boundary[0], "gy", -1), my_index + 1 < extent)
    boundary = jnp.stack(
        [
            combine_rows(boundary[0], from_below, boundary[1]),
            combine_rows(boundary[1], boundary[0], from_above),
        ],
        0,
    )
    for bit_level in range(extent.bit_length() - 1):
        offset = 1 << bit_level
        lower_pair = protect(shifted(boundary, "gy", offset), my_index >= offset)
        upper_pair = protect(shifted(boundary, "gy", -offset), my_index + offset < extent)
        boundary = combine_rows(boundary, lower_pair, upper_pair)
    return boundary


def shards(state, viscous):
    cells_x = state.shape[2]
    cells_y = state.shape[3]
    stacked = jnp.concatenate([state, viscous[None]], 0)
    padded = with_halo(stacked, (("gx", 2), ("gy", 3)), 2)
    x_strip = padded[:, :, :, 2 : cells_y + 2]
    y_strip = padded[:, :, 2 : cells_x + 2]
    x_cells = (
        lax.axis_index("gx") * cells_x - 2 + lax.broadcasted_iota(jnp.int32, (1, cells_x + 4, 1), 1)
    )
    x_inside = jnp.logical_and(x_cells >= 0, x_cells < cells_x * lax.axis_size("gx"))
    density_x = jnp.where(x_inside, x_strip[0], 1.0)
    velocity_x = x_strip[1] / density_x
    pressure_x = pressure(x_strip, density_x)
    flux_x = jnp.stack(
        [
            x_strip[1],
            x_strip[1] * velocity_x + pressure_x,
            x_strip[2] * velocity_x,
            x_strip[3] * velocity_x,
            (x_strip[4] + pressure_x) * velocity_x,
        ]
    )
    source_x = mass_rows(x_strip[:5], 2, cells_x) - STEP_RATIO * central_rows(flux_x, 2, cells_x)
    lower_x, diag_x, upper_x = face_rows(x_strip[5], 1, cells_x)
    y_cells = (
        lax.axis_index("gy") * cells_y - 2 + lax.broadcasted_iota(jnp.int32, (1, 1, cells_y + 4), 2)
    )
    y_inside = jnp.logical_and(y_cells >= 0, y_cells < cells_y * lax.axis_size("gy"))
    density_y = jnp.where(y_inside, y_strip[0], 1.0)
    velocity_y = y_strip[2] / density_y
    pressure_y = pressure(y_strip, density_y)
    lower_y, diag_y, upper_y = face_rows(y_strip[5], 2, cells_y)
    x_section = chained_solve(lower_x, diag_x, upper_x, source_x, relay_chain)
    x_extended = with_halo(x_section, (("gy", 3),), 2)
    flux_y = jnp.stack(
        [
            velocity_y * x_extended[0],
            velocity_y * x_extended[1],
            velocity_y * x_extended[2] + pressure_y,
            velocity_y * x_extended[3],
            velocity_y * x_extended[4] + pressure_y * velocity_y,
        ]
    )
    source_y = mass_rows(x_extended, 3, cells_y) - STEP_RATIO * central_rows(flux_y, 3, cells_y)
    y_levels, y_condensed, source_first, source_last = reduce_lines(
        jnp.swapaxes(lower_y, 1, 2),
        jnp.swapaxes(diag_y, 1, 2),
        jnp.swapaxes(upper_y, 1, 2),
        jnp.swapaxes(source_y, 2, 3),
    )
    boundary = jnp.stack(
        [
            pack_slot(y_condensed[0], y_condensed[1], y_condensed[2], source_first),
            pack_slot(y_condensed[3], y_condensed[4], y_condensed[5], source_last),
        ],
        0,
    )
    boundary = cyclic_rows(boundary)
    solved = entries(boundary, 3, 8) / entries(boundary, 1, 2)
    return jnp.swapaxes(rebuild_lines(y_levels, solved[0], solved[1]), 2, 3)


def solution(mesh):
    placed = (P(None, None, "gx", "gy"), P(None, "gx", "gy"))
    return jax.shard_map(
        shards, mesh=mesh, in_specs=placed, out_specs=P(None, None, "gx", "gy"), check_vma=False
    )
```

profile of v0, /device:TPU:134, one launch (start us, length us, event | category | flops | bytes accessed | tf_op | source)
XLA Modules:
  0.0 441.4 jit_solution(4641683138847617568)
XLA Ops:
  46.9 6.7 %slice_subtract_fusion.17 = (f32[5,1,32,1,256]{4,3,2,0,1:T(1,128)S(1)}, f32[5,1,32,1,256]{4,3,2,0,1:T(1,128)}, f32[5,1,32,1,256]{4,3,2,0,1:T(1,128)}, f32[5,1,32...) fusion(f32[5,1,32,8,256]{4,3,2,0,1:T(8,128)} %bitcast.1144, ...), kind=kLoop, calls=%fused_computation.126 | loop fusion | flops 1146880 | bytes 2686976 | tf_op jit(solution)/shard_map/sub | solution.py:119
  68.7 126.6 %while.20 = (s32[]{:T(128)}, f32[6,1,256]{2,1,0:T(1,128)S(1)}, f32[1,256]{1,0:T(1,128)}, f32[1,256]{1,0:T(1,128)}, f32[1,256]{1,0:T(1,128)}, /*index=5*/f32[1,25...) while((s32[]{:T(128)}, f32[6,1,256]{2,1,0:T(1,128)S(1)}, ...), condition=%wide.region_1.2_spmd, body=%wide.region_0.1_spmd.sunk | while | flops 11266 | bytes 96449 | solution.py:219
  199.2 111.9 %while.21 = (s32[]{:T(128)}, f32[5,1,256]{2,1,0:T(1,128)S(1)}, f32[1,256]{1,0:T(1,128)}, f32[1,256]{1,0:T(1,128)S(1)}, f32[5,1,256]{2,1,0:T(1,128)}, /*index=5*/f32[5,1,256]{2,1,0:T(1,128)}, s32[]{:T(128)}) while((s32[]{:T(128)}, f32[5,1,256]{2,1,0:T(1,128)S(1)}, f32[1,256]{1,0:T(1,128)}, f32[1,256]{1,0:T(1,128)S(1)}, f32[5,1,256]{2,1,0:T(1,128)}, ...), condition=%wide.region_3.4_spmd, body=%wide.region_2.3_spmd.sunk | while | flops 5122 | bytes 43125 | solution.py:228
  205.3 4.8 %collective-permute-start.1 = (f32[5,1,256]{2,1,0:T(1,128)}, f32[5,1,256]{2,1,0:T(1,128)S(1)}, u32[]{:S(2)}, u32[]{:S(2)}) collective-permute-start(f32[5,1,256]{2,1,0:T(1,128)} %multiply_subtract_fusion.162), channel_id=1, source_target_pairs={{16,0},{32,16},{48,32},{64,48},{80,64},{96,80},{112,96},{128,112},... | collective-permute-start | bytes 15368 | tf_op jit(solution)/shard_map/while/body/eval_jaxpr/ppermute | solution.py:17
  212.9 4.8 %collective-permute-start.1 = (f32[5,1,256]{2,1,0:T(1,128)}, f32[5,1,256]{2,1,0:T(1,128)S(1)}, u32[]{:S(2)}, u32[]{:S(2)}) collective-permute-start(f32[5,1,256]{2,1,0:T(1,128)} %multiply_subtract_fusion.162), channel_id=1, source_target_pairs={{16,0},{32,16},{48,32},{64,48},{80,64},{96,80},{112,96},{128,112},... | collective-permute-start | bytes 15368 | tf_op jit(solution)/shard_map/while/body/eval_jaxpr/ppermute | solution.py:17
  220.6 4.8 %collective-permute-start.1 = (f32[5,1,256]{2,1,0:T(1,128)}, f32[5,1,256]{2,1,0:T(1,128)S(1)}, u32[]{:S(2)}, u32[]{:S(2)}) collective-permute-start(f32[5,1,256]{2,1,0:T(1,128)} %multiply_subtract_fusion.162), channel_id=1, source_target_pairs={{16,0},{32,16},{48,32},{64,48},{80,64},{96,80},{112,96},{128,112},... | collective-permute-start | bytes 15368 | tf_op jit(solution)/shard_map/while/body/eval_jaxpr/ppermute | solution.py:17
  228.2 4.8 %collective-permute-start.1 = (f32[5,1,256]{2,1,0:T(1,128)}, f32[5,1,256]{2,1,0:T(1,128)S(1)}, u32[]{:S(2)}, u32[]{:S(2)}) collective-permute-start(f32[5,1,256]{2,1,0:T(1,128)} %multiply_subtract_fusion.162), channel_id=1, source_target_pairs={{16,0},{32,16},{48,32},{64,48},{80,64},{96,80},{112,96},{128,112},... | collective-permute-start | bytes 15368 | tf_op jit(solution)/shard_map/while/body/eval_jaxpr/ppermute | solution.py:17
  235.9 4.8 %collective-permute-start.1 = (f32[5,1,256]{2,1,0:T(1,128)}, f32[5,1,256]{2,1,0:T(1,128)S(1)}, u32[]{:S(2)}, u32[]{:S(2)}) collective-permute-start(f32[5,1,256]{2,1,0:T(1,128)} %multiply_subtract_fusion.162), channel_id=1, source_target_pairs={{16,0},{32,16},{48,32},{64,48},{80,64},{96,80},{112,96},{128,112},... | collective-permute-start | bytes 15368 | tf_op jit(solution)/shard_map/while/body/eval_jaxpr/ppermute | solution.py:17
  243.5 4.8 %collective-permute-start.1 = (f32[5,1,256]{2,1,0:T(1,128)}, f32[5,1,256]{2,1,0:T(1,128)S(1)}, u32[]{:S(2)}, u32[]{:S(2)}) collective-permute-start(f32[5,1,256]{2,1,0:T(1,128)} %multiply_subtract_fusion.162), channel_id=1, source_target_pairs={{16,0},{32,16},{48,32},{64,48},{80,64},{96,80},{112,96},{128,112},... | collective-permute-start | bytes 15368 | tf_op jit(solution)/shard_map/while/body/eval_jaxpr/ppermute | solution.py:17
  251.2 4.8 %collective-permute-start.1 = (f32[5,1,256]{2,1,0:T(1,128)}, f32[5,1,256]{2,1,0:T(1,128)S(1)}, u32[]{:S(2)}, u32[]{:S(2)}) collective-permute-start(f32[5,1,256]{2,1,0:T(1,128)} %multiply_subtract_fusion.162), channel_id=1, source_target_pairs={{16,0},{32,16},{48,32},{64,48},{80,64},{96,80},{112,96},{128,112},... | collective-permute-start | bytes 15368 | tf_op jit(solution)/shard_map/while/body/eval_jaxpr/ppermute | solution.py:17
  258.8 4.8 %collective-permute-start.1 = (f32[5,1,256]{2,1,0:T(1,128)}, f32[5,1,256]{2,1,0:T(1,128)S(1)}, u32[]{:S(2)}, u32[]{:S(2)}) collective-permute-start(f32[5,1,256]{2,1,0:T(1,128)} %multiply_subtract_fusion.162), channel_id=1, source_target_pairs={{16,0},{32,16},{48,32},{64,48},{80,64},{96,80},{112,96},{128,112},... | collective-permute-start | bytes 15368 | tf_op jit(solution)/shard_map/while/body/eval_jaxpr/ppermute | solution.py:17
  266.5 4.8 %collective-permute-start.1 = (f32[5,1,256]{2,1,0:T(1,128)}, f32[5,1,256]{2,1,0:T(1,128)S(1)}, u32[]{:S(2)}, u32[]{:S(2)}) collective-permute-start(f32[5,1,256]{2,1,0:T(1,128)} %multiply_subtract_fusion.162), channel_id=1, source_target_pairs={{16,0},{32,16},{48,32},{64,48},{80,64},{96,80},{112,96},{128,112},... | collective-permute-start | bytes 15368 | tf_op jit(solution)/shard_map/while/body/eval_jaxpr/ppermute | solution.py:17
  274.1 4.8 %collective-permute-start.1 = (f32[5,1,256]{2,1,0:T(1,128)}, f32[5,1,256]{2,1,0:T(1,128)S(1)}, u32[]{:S(2)}, u32[]{:S(2)}) collective-permute-start(f32[5,1,256]{2,1,0:T(1,128)} %multiply_subtract_fusion.162), channel_id=1, source_target_pairs={{16,0},{32,16},{48,32},{64,48},{80,64},{96,80},{112,96},{128,112},... | collective-permute-start | bytes 15368 | tf_op jit(solution)/shard_map/while/body/eval_jaxpr/ppermute | solution.py:17
  281.8 4.8 %collective-permute-start.1 = (f32[5,1,256]{2,1,0:T(1,128)}, f32[5,1,256]{2,1,0:T(1,128)S(1)}, u32[]{:S(2)}, u32[]{:S(2)}) collective-permute-start(f32[5,1,256]{2,1,0:T(1,128)} %multiply_subtract_fusion.162), channel_id=1, source_target_pairs={{16,0},{32,16},{48,32},{64,48},{80,64},{96,80},{112,96},{128,112},... | collective-permute-start | bytes 15368 | tf_op jit(solution)/shard_map/while/body/eval_jaxpr/ppermute | solution.py:17
  289.5 4.8 %collective-permute-start.1 = (f32[5,1,256]{2,1,0:T(1,128)}, f32[5,1,256]{2,1,0:T(1,128)S(1)}, u32[]{:S(2)}, u32[]{:S(2)}) collective-permute-start(f32[5,1,256]{2,1,0:T(1,128)} %multiply_subtract_fusion.162), channel_id=1, source_target_pairs={{16,0},{32,16},{48,32},{64,48},{80,64},{96,80},{112,96},{128,112},... | collective-permute-start | bytes 15368 | tf_op jit(solution)/shard_map/while/body/eval_jaxpr/ppermute | solution.py:17
  338.8 5.2 %collective-permute-start.7 = (f32[5,1,256,2]{2,3,1,0:T(2,128)S(1)}, f32[5,1,256,2]{2,3,1,0:T(2,128)S(1)}, u32[]{:S(2)}, u32[]{:S(2)}) collective-permute-start(f32[5,1,256,2]{2,3,1,0:T(2,128)S(1)} %get-tuple-element.432), channel_id=1, source_target_pairs={{1,0},{2,1},{3,2},{4,3},{5,4},{6,5},{7,6},{8,7},{9,8},{10,9},{11,1... | collective-permute-start | bytes 30728 | tf_op jit(solution)/shard_map/ppermute | solution.py:28
  346.1 6.0 %collective-permute-start.5 = (f32[6,1,260,2]{2,3,1,0:T(2,128)S(1)}, f32[6,1,260,2]{2,3,1,0:T(2,128)S(1)}, u32[]{:S(2)}, u32[]{:S(2)}) collective-permute-start(f32[6,1,260,2]{2,3,1,0:T(2,128)S(1)} %get-tuple-element.426), channel_id=1, source_target_pairs={{1,0},{2,1},{3,2},{4,3},{5,4},{6,5},{7,6},{8,7},{9,8},{10,9},{11,1... | collective-permute-start | bytes 37448 | tf_op jit(solution)/shard_map/ppermute | solution.py:28
  354.3 5.7 %collective-permute-done.4 = f32[6,1,260,2]{2,3,1,0:T(2,128)S(1)} collective-permute-done((f32[6,1,260,2]{2,3,1,0:T(2,128)S(1)}, f32[6,1,260,2]{2,3,1,0:T(2,128)S(1)}, u32[]{:S(2)}, u32[]{:S(2)}) %collective-permute-start.4) | collective-permute-done | bytes 12512 | tf_op jit(solution)/shard_map/ppermute | solution.py:27
  385.1 6.0 %collective-permute-start.9 = (f32[8,1,256]{2,0,1:T(8,128)S(1)}, f32[8,1,256]{2,0,1:T(8,128)S(1)}, u32[]{:S(2)}, u32[]{:S(2)}) collective-permute-start(f32[8,1,256]{2,0,1:T(8,128)S(1)} %pad_maximum_fusion.43), channel_id=1, source_target_pairs={{1,0},{2,1},{3,2},{4,3},{5,4},{6,5},{7,6},{8,7},{9,8},{10,9},{11,1... | collective-permute-start | bytes 24584 | tf_op jit(solution)/shard_map/ppermute | solution.py:17
  394.5 6.3 %collective-permute-start.11 = (f32[2,8,1,256]{3,1,2,0:T(8,128)S(1)}, f32[2,8,1,256]{3,1,2,0:T(8,128)S(1)}, u32[]{:S(2)}, u32[]{:S(2)}) collective-permute-start(f32[2,8,1,256]{3,1,2,0:T(8,128)S(1)} %pad_maximum_fusion.28), channel_id=1, source_target_pairs={{1,0},{2,1},{3,2},{4,3},{5,4},{6,5},{7,6},{8,7},{9,8},{10,9},{11,1... | collective-permute-start | bytes 49160 | tf_op jit(solution)/shard_map/ppermute | solution.py:17
  404.4 6.5 %collective-permute-start.13 = (f32[2,8,1,256]{3,1,2,0:T(8,128)S(1)}, f32[2,8,1,256]{3,1,2,0:T(8,128)S(1)}, u32[]{:S(2)}, u32[]{:S(2)}) collective-permute-start(f32[2,8,1,256]{3,1,2,0:T(8,128)S(1)} %pad_maximum_fusion.39), channel_id=1, source_target_pairs={{2,0},{3,1},{4,2},{5,3},{6,4},{7,5},{8,6},{9,7},{10,8},{11,9},{12,... | collective-permute-start | bytes 49160 | tf_op jit(solution)/shard_map/ppermute | solution.py:17
  413.7 6.2 %collective-permute-start.15 = (f32[2,8,1,256]{3,1,2,0:T(8,128)S(1)}, f32[2,8,1,256]{3,1,2,0:T(8,128)S(1)}, u32[]{:S(2)}, u32[]{:S(2)}) collective-permute-start(f32[2,8,1,256]{3,1,2,0:T(8,128)S(1)} %pad_maximum_fusion.40), channel_id=1, source_target_pairs={{4,0},{5,1},{6,2},{7,3},{8,4},{9,5},{10,6},{11,7},{12,8},{13,9},{1... | collective-permute-start | bytes 49160 | tf_op jit(solution)/shard_map/ppermute | solution.py:17
  421.5 6.3 %collective-permute-start.17 = (f32[2,8,1,256]{3,1,2,0:T(8,128)S(1)}, f32[2,8,1,256]{3,1,2,0:T(8,128)S(1)}, u32[]{:S(2)}, u32[]{:S(2)}) collective-permute-start(f32[2,8,1,256]{3,1,2,0:T(8,128)S(1)} %pad_maximum_fusion.41), channel_id=1, source_target_pairs={{8,0},{9,1},{10,2},{11,3},{12,4},{13,5},{14,6},{15,7},{24,16},{25,... | collective-permute-start | bytes 49160 | tf_op jit(solution)/shard_map/ppermute | solution.py:17
  429.2 5.7 %collective-permute-done.16 = f32[2,8,1,256]{3,1,2,0:T(8,128)S(1)} collective-permute-done((f32[2,8,1,256]{3,1,2,0:T(8,128)S(1)}, f32[2,8,1,256]{3,1,2,0:T(8,128)S(1)}, u32[]{:S(2)}, u32[]{:S(2)}) %collective-permute-start.16) | collective-permute-done | bytes 16416 | tf_op jit(solution)/shard_map/ppermute | solution.py:17
  (839 shorter events, 318.2 us)
Async XLA Ops:
  70.8 6.4 %collective-permute-start = (f32[6,1,256]{2,1,0:T(1,128)}, f32[6,1,256]{2,1,0:T(1,128)S(1)}, u32[]{:S(2)}, u32[]{:S(2)}) collective-permute-start(f32[6,1,256]{2,1,0:T(1,128)} %pad_maximum_fusion.51), channel_id=1, source_target_pairs={{0,16},{16,32},{32,48},{48,64},{64,80},{80,96},{96,112},{112,128},... | collective-permute-start | bytes 18440 | tf_op jit(solution)/shard_map/while/body/eval_jaxpr/ppermute | solution.py:17
  79.2 6.4 %collective-permute-start = (f32[6,1,256]{2,1,0:T(1,128)}, f32[6,1,256]{2,1,0:T(1,128)S(1)}, u32[]{:S(2)}, u32[]{:S(2)}) collective-permute-start(f32[6,1,256]{2,1,0:T(1,128)} %pad_maximum_fusion.51), channel_id=1, source_target_pairs={{0,16},{16,32},{32,48},{48,64},{64,80},{80,96},{96,112},{112,128},... | collective-permute-start | bytes 18440 | tf_op jit(solution)/shard_map/while/body/eval_jaxpr/ppermute | solution.py:17
  87.7 6.4 %collective-permute-start = (f32[6,1,256]{2,1,0:T(1,128)}, f32[6,1,256]{2,1,0:T(1,128)S(1)}, u32[]{:S(2)}, u32[]{:S(2)}) collective-permute-start(f32[6,1,256]{2,1,0:T(1,128)} %pad_maximum_fusion.51), channel_id=1, source_target_pairs={{0,16},{16,32},{32,48},{48,64},{64,80},{80,96},{96,112},{112,128},... | collective-permute-start | bytes 18440 | tf_op jit(solution)/shard_map/while/body/eval_jaxpr/ppermute | solution.py:17
  96.1 6.4 %collective-permute-start = (f32[6,1,256]{2,1,0:T(1,128)}, f32[6,1,256]{2,1,0:T(1,128)S(1)}, u32[]{:S(2)}, u32[]{:S(2)}) collective-permute-start(f32[6,1,256]{2,1,0:T(1,128)} %pad_maximum_fusion.51), channel_id=1, source_target_pairs={{0,16},{16,32},{32,48},{48,64},{64,80},{80,96},{96,112},{112,128},... | collective-permute-start | bytes 18440 | tf_op jit(solution)/shard_map/while/body/eval_jaxpr/ppermute | solution.py:17
  104.5 6.4 %collective-permute-start = (f32[6,1,256]{2,1,0:T(1,128)}, f32[6,1,256]{2,1,0:T(1,128)S(1)}, u32[]{:S(2)}, u32[]{:S(2)}) collective-permute-start(f32[6,1,256]{2,1,0:T(1,128)} %pad_maximum_fusion.51), channel_id=1, source_target_pairs={{0,16},{16,32},{32,48},{48,64},{64,80},{80,96},{96,112},{112,128},... | collective-permute-start | bytes 18440 | tf_op jit(solution)/shard_map/while/body/eval_jaxpr/ppermute | solution.py:17
  113.0 6.4 %collective-permute-start = (f32[6,1,256]{2,1,0:T(1,128)}, f32[6,1,256]{2,1,0:T(1,128)S(1)}, u32[]{:S(2)}, u32[]{:S(2)}) collective-permute-start(f32[6,1,256]{2,1,0:T(1,128)} %pad_maximum_fusion.51), channel_id=1, source_target_pairs={{0,16},{16,32},{32,48},{48,64},{64,80},{80,96},{96,112},{112,128},... | collective-permute-start | bytes 18440 | tf_op jit(solution)/shard_map/while/body/eval_jaxpr/ppermute | solution.py:17
  121.4 6.4 %collective-permute-start = (f32[6,1,256]{2,1,0:T(1,128)}, f32[6,1,256]{2,1,0:T(1,128)S(1)}, u32[]{:S(2)}, u32[]{:S(2)}) collective-permute-start(f32[6,1,256]{2,1,0:T(1,128)} %pad_maximum_fusion.51), channel_id=1, source_target_pairs={{0,16},{16,32},{32,48},{48,64},{64,80},{80,96},{96,112},{112,128},... | collective-permute-start | bytes 18440 | tf_op jit(solution)/shard_map/while/body/eval_jaxpr/ppermute | solution.py:17
  129.9 6.4 %collective-permute-start = (f32[6,1,256]{2,1,0:T(1,128)}, f32[6,1,256]{2,1,0:T(1,128)S(1)}, u32[]{:S(2)}, u32[]{:S(2)}) collective-permute-start(f32[6,1,256]{2,1,0:T(1,128)} %pad_maximum_fusion.51), channel_id=1, source_target_pairs={{0,16},{16,32},{32,48},{48,64},{64,80},{80,96},{96,112},{112,128},... | collective-permute-start | bytes 18440 | tf_op jit(solution)/shard_map/while/body/eval_jaxpr/ppermute | solution.py:17
  138.3 6.4 %collective-permute-start = (f32[6,1,256]{2,1,0:T(1,128)}, f32[6,1,256]{2,1,0:T(1,128)S(1)}, u32[]{:S(2)}, u32[]{:S(2)}) collective-permute-start(f32[6,1,256]{2,1,0:T(1,128)} %pad_maximum_fusion.51), channel_id=1, source_target_pairs={{0,16},{16,32},{32,48},{48,64},{64,80},{80,96},{96,112},{112,128},... | collective-permute-start | bytes 18440 | tf_op jit(solution)/shard_map/while/body/eval_jaxpr/ppermute | solution.py:17
  146.7 6.4 %collective-permute-start = (f32[6,1,256]{2,1,0:T(1,128)}, f32[6,1,256]{2,1,0:T(1,128)S(1)}, u32[]{:S(2)}, u32[]{:S(2)}) collective-permute-start(f32[6,1,256]{2,1,0:T(1,128)} %pad_maximum_fusion.51), channel_id=1, source_target_pairs={{0,16},{16,32},{32,48},{48,64},{64,80},{80,96},{96,112},{112,128},... | collective-permute-start | bytes 18440 | tf_op jit(solution)/shard_map/while/body/eval_jaxpr/ppermute | solution.py:17
  338.8 15.4 %collective-permute-start.7 = (f32[5,1,256,2]{2,3,1,0:T(2,128)S(1)}, f32[5,1,256,2]{2,3,1,0:T(2,128)S(1)}, u32[]{:S(2)}, u32[]{:S(2)}) collective-permute-start(f32[5,1,256,2]{2,3,1,0:T(2,128)S(1)} %get-tuple-element.432), channel_id=1, source_target_pairs={{1,0},{2,1},{3,2},{4,3},{5,4},{6,5},{7,6},{8,7},{9,8},{10,9},{11,1... | collective-permute-start | bytes 30728 | tf_op jit(solution)/shard_map/ppermute | solution.py:28
  344.0 10.2 %collective-permute-start.6 = (f32[5,1,256,2]{2,3,1,0:T(2,128)S(1)}, f32[5,1,256,2]{2,3,1,0:T(2,128)S(1)}, u32[]{:S(2)}, u32[]{:S(2)}) collective-permute-start(f32[5,1,256,2]{2,3,1,0:T(2,128)S(1)} %get-tuple-element.431), channel_id=1, source_target_pairs={{0,1},{1,2},{2,3},{3,4},{4,5},{5,6},{6,7},{7,8},{8,9},{9,10},{10,1... | collective-permute-start | bytes 30728 | tf_op jit(solution)/shard_map/ppermute | solution.py:27
  346.1 8.1 %collective-permute-start.5 = (f32[6,1,260,2]{2,3,1,0:T(2,128)S(1)}, f32[6,1,260,2]{2,3,1,0:T(2,128)S(1)}, u32[]{:S(2)}, u32[]{:S(2)}) collective-permute-start(f32[6,1,260,2]{2,3,1,0:T(2,128)S(1)} %get-tuple-element.426), channel_id=1, source_target_pairs={{1,0},{2,1},{3,2},{4,3},{5,4},{6,5},{7,6},{8,7},{9,8},{10,9},{11,1... | collective-permute-start | bytes 37448 | tf_op jit(solution)/shard_map/ppermute | solution.py:28
  352.2 7.8 %collective-permute-start.4 = (f32[6,1,260,2]{2,3,1,0:T(2,128)S(1)}, f32[6,1,260,2]{2,3,1,0:T(2,128)S(1)}, u32[]{:S(2)}, u32[]{:S(2)}) collective-permute-start(f32[6,1,260,2]{2,3,1,0:T(2,128)S(1)} %get-tuple-element.425), channel_id=1, source_target_pairs={{0,1},{1,2},{2,3},{3,4},{4,5},{5,6},{6,7},{7,8},{8,9},{9,10},{10,1... | collective-permute-start | bytes 37448 | tf_op jit(solution)/shard_map/ppermute | solution.py:27
  383.1 8.0 %collective-permute-start.8 = (f32[8,1,256]{2,0,1:T(8,128)S(1)}, f32[8,1,256]{2,0,1:T(8,128)S(1)}, u32[]{:S(2)}, u32[]{:S(2)}) collective-permute-start(f32[8,1,256]{2,0,1:T(8,128)S(1)} %pad_maximum_fusion.42), channel_id=1, source_target_pairs={{0,1},{1,2},{2,3},{3,4},{4,5},{5,6},{6,7},{7,8},{8,9},{9,10},{10,1... | collective-permute-start | bytes 24584 | tf_op jit(solution)/shard_map/ppermute | solution.py:17
  385.1 7.4 %collective-permute-start.9 = (f32[8,1,256]{2,0,1:T(8,128)S(1)}, f32[8,1,256]{2,0,1:T(8,128)S(1)}, u32[]{:S(2)}, u32[]{:S(2)}) collective-permute-start(f32[8,1,256]{2,0,1:T(8,128)S(1)} %pad_maximum_fusion.43), channel_id=1, source_target_pairs={{1,0},{2,1},{3,2},{4,3},{5,4},{6,5},{7,6},{8,7},{9,8},{10,9},{11,1... | collective-permute-start | bytes 24584 | tf_op jit(solution)/shard_map/ppermute | solution.py:17
  392.6 8.3 %collective-permute-start.10 = (f32[2,8,1,256]{3,1,2,0:T(8,128)S(1)}, f32[2,8,1,256]{3,1,2,0:T(8,128)S(1)}, u32[]{:S(2)}, u32[]{:S(2)}) collective-permute-start(f32[2,8,1,256]{3,1,2,0:T(8,128)S(1)} %pad_maximum_fusion.28), channel_id=1, source_target_pairs={{0,1},{1,2},{2,3},{3,4},{4,5},{5,6},{6,7},{7,8},{8,9},{9,10},{10,1... | collective-permute-start | bytes 49160 | tf_op jit(solution)/shard_map/ppermute | solution.py:17
  394.5 7.7 %collective-permute-start.11 = (f32[2,8,1,256]{3,1,2,0:T(8,128)S(1)}, f32[2,8,1,256]{3,1,2,0:T(8,128)S(1)}, u32[]{:S(2)}, u32[]{:S(2)}) collective-permute-start(f32[2,8,1,256]{3,1,2,0:T(8,128)S(1)} %pad_maximum_fusion.28), channel_id=1, source_target_pairs={{1,0},{2,1},{3,2},{4,3},{5,4},{6,5},{7,6},{8,7},{9,8},{10,9},{11,1... | collective-permute-start | bytes 49160 | tf_op jit(solution)/shard_map/ppermute | solution.py:17
  402.3 8.5 %collective-permute-start.12 = (f32[2,8,1,256]{3,1,2,0:T(8,128)S(1)}, f32[2,8,1,256]{3,1,2,0:T(8,128)S(1)}, u32[]{:S(2)}, u32[]{:S(2)}) collective-permute-start(f32[2,8,1,256]{3,1,2,0:T(8,128)S(1)} %pad_maximum_fusion.39), channel_id=1, source_target_pairs={{0,2},{1,3},{2,4},{3,5},{4,6},{5,7},{6,8},{7,9},{8,10},{9,11},{10,... | collective-permute-start | bytes 49160 | tf_op jit(solution)/shard_map/ppermute | solution.py:17
  404.4 7.9 %collective-permute-start.13 = (f32[2,8,1,256]{3,1,2,0:T(8,128)S(1)}, f32[2,8,1,256]{3,1,2,0:T(8,128)S(1)}, u32[]{:S(2)}, u32[]{:S(2)}) collective-permute-start(f32[2,8,1,256]{3,1,2,0:T(8,128)S(1)} %pad_maximum_fusion.39), channel_id=1, source_target_pairs={{2,0},{3,1},{4,2},{5,3},{6,4},{7,5},{8,6},{9,7},{10,8},{11,9},{12,... | collective-permute-start | bytes 49160 | tf_op jit(solution)/shard_map/ppermute | solution.py:17
  412.4 7.6 %collective-permute-start.14 = (f32[2,8,1,256]{3,1,2,0:T(8,128)S(1)}, f32[2,8,1,256]{3,1,2,0:T(8,128)S(1)}, u32[]{:S(2)}, u32[]{:S(2)}) collective-permute-start(f32[2,8,1,256]{3,1,2,0:T(8,128)S(1)} %pad_maximum_fusion.40), channel_id=1, source_target_pairs={{0,4},{1,5},{2,6},{3,7},{4,8},{5,9},{6,10},{7,11},{8,12},{9,13},{1... | collective-permute-start | bytes 49160 | tf_op jit(solution)/shard_map/ppermute | solution.py:17
  413.7 7.6 %collective-permute-start.15 = (f32[2,8,1,256]{3,1,2,0:T(8,128)S(1)}, f32[2,8,1,256]{3,1,2,0:T(8,128)S(1)}, u32[]{:S(2)}, u32[]{:S(2)}) collective-permute-start(f32[2,8,1,256]{3,1,2,0:T(8,128)S(1)} %pad_maximum_fusion.40), channel_id=1, source_target_pairs={{4,0},{5,1},{6,2},{7,3},{8,4},{9,5},{10,6},{11,7},{12,8},{13,9},{1... | collective-permute-start | bytes 49160 | tf_op jit(solution)/shard_map/ppermute | solution.py:17
  421.5 7.7 %collective-permute-start.17 = (f32[2,8,1,256]{3,1,2,0:T(8,128)S(1)}, f32[2,8,1,256]{3,1,2,0:T(8,128)S(1)}, u32[]{:S(2)}, u32[]{:S(2)}) collective-permute-start(f32[2,8,1,256]{3,1,2,0:T(8,128)S(1)} %pad_maximum_fusion.41), channel_id=1, source_target_pairs={{8,0},{9,1},{10,2},{11,3},{12,4},{13,5},{14,6},{15,7},{24,16},{25,... | collective-permute-start | bytes 49160 | tf_op jit(solution)/shard_map/ppermute | solution.py:17
  427.7 7.1 %collective-permute-start.16 = (f32[2,8,1,256]{3,1,2,0:T(8,128)S(1)}, f32[2,8,1,256]{3,1,2,0:T(8,128)S(1)}, u32[]{:S(2)}, u32[]{:S(2)}) collective-permute-start(f32[2,8,1,256]{3,1,2,0:T(8,128)S(1)} %pad_maximum_fusion.41), channel_id=1, source_target_pairs={{0,8},{1,9},{2,10},{3,11},{4,12},{5,13},{6,14},{7,15},{16,24},{17,... | collective-permute-start | bytes 49160 | tf_op jit(solution)/shard_map/ppermute | solution.py:17
  (237 other events, 2171.5 us)
where the time goes:
time: 447 us; the launch traced here: 441 us
  starting transfers between devices  157 us (35%)
  other arithmetic  130 us (29%)
  waiting for transfers between devices  109 us (24%)
  local copies, waits for them, and re-layouts  40.1 us (9%)
    ppermute x40, starting transfers between devices, shifted(): lax.ppermute(value, axis, [(source, source + steps) for source in range(f...  138 us
    ppermute x40, waiting for transfers between devices, shifted(): lax.ppermute(value, axis, [(source, source + steps) for source in range(f...  101 us
    sub x15, other arithmetic, backward_turn(): return shifted(value_first - slope_first * x_last, 'gx', -1)  19.6 us
    sub x8, other arithmetic, condense(): source_first = source[0] - upper[0] * particular[1]  15.1 us
    mul x17, other arithmetic, sweep_pair(): slope_last = upper_last * pivot_last  13.3 us
    ppermute x3, starting transfers between devices, with_halo(): after = lax.ppermute(first, axis, down)  13.1 us
    mul x16, other arithmetic, sweep_pair(): value_last = (source_last - lower_last * value_first) * pivot_last  12.5 us
    unnamed x31, other arithmetic  11.2 us
  transfers between devices with their start and end apart: 46, of which 37 were waited for; matrix products, arithmetic and copies ran while one was open for 0% of the time, Pallas kernels for 0%

commit v1 on v0

v1 whole, which is shorter than its diff:
```python
import functools
import jax
import jax.numpy as jnp
from jax import lax
from jax.experimental import pallas as pl
from jax.experimental.pallas import tpu as pltpu
from jax.sharding import PartitionSpec as P

STEP_RATIO = 0.25
ONE_THIRD = 1.0 / 3.0
NEAR_WEIGHT = 7.0 / 9.0
FAR_WEIGHT = 1.0 / 36.0
GAMMA_MINUS = 0.4
FAR_SCALED = STEP_RATIO * FAR_WEIGHT
FIELDS = 5
CHUNKS = 8
LANES = 128
PAY_ROWS = 40
ROW_RIGHT, ROW_HI, ROW_FLUX_RIGHT, ROW_LEFT, ROW_FLUX_LEFT, ROW_LO = 16, 21, 22, 27, 32, 37


def strided(ref, position, count):
    return ref[pl.ds(position, CHUNKS, stride=count), :]


def sublane_ids(shape):
    return lax.broadcasted_iota(jnp.int32, shape, 0)


def from_previous(value):
    return jnp.where(sublane_ids(value.shape) == 0, 0.0, pltpu.roll(value, 1, 0))


def from_next(value):
    return jnp.where(sublane_ids(value.shape) == CHUNKS - 1, 0.0, pltpu.roll(value, CHUNKS - 1, 0))


class Window:
    def __init__(self, make, count):
        self.make, self.count, self.known = make, count, {}

    def __call__(self, position):
        if position not in self.known:
            if position < 0:
                value = jax.tree.map(from_previous, self(position + self.count))
            elif position >= self.count:
                value = jax.tree.map(from_next, self(position - self.count))
            else:
                value = self.make(position)
            self.known[position] = value
        return self.known[position]


def local_solve(cells, viscous, count, part_ref, left_ref, right_ref, inner_ref, pay_ref, first_ref, last_ref):
    final = count - 1

    @functools.cache
    def face(j):
        return 0.5 * (viscous(j - 1) + viscous(j))

    @functools.cache
    def coupling(j):
        return ONE_THIRD - face(j)

    def diagonal(j):
        return 1.0 + face(j) + face(j + 1)

    def source(j, q):
        u_low, u_mid, u_high = cells(j - 1)[0][q], cells(j)[0][q], cells(j + 1)[0][q]
        f = [cells(j + o)[1][q] for o in (-2, -1, 1, 2)]
        central = NEAR_WEIGHT * (f[2] - f[1]) + FAR_WEIGHT * (f[3] - f[0])
        return u_mid + ONE_THIRD * (u_low + u_high) - STEP_RATIO * central

    rows = lambda j: pl.ds(j * CHUNKS, CHUNKS)
    slopes = {}
    forward = left = None
    ends = {}
    for j in range(count):
        values = [source(j, q) for q in range(FIELDS)]
        if j == 0 or j == final:
            ends[j] = values
            continue
        if j == 1:
            inverse = 1.0 / diagonal(j)
            left = -coupling(j) * inverse
            forward = [s * inverse for s in values]
        else:
            inverse = 1.0 / (diagonal(j) - coupling(j) * slopes[j - 1])
            tied = coupling(j) * inverse
            left = -tied * left
            forward = [s * inverse - tied * f for s, f in zip(values, forward)]
        slopes[j] = coupling(j + 1) * inverse
        left_ref[rows(j), :] = left
        right_ref[rows(j), :] = slopes[j]
        for q in range(FIELDS):
            part_ref[q, rows(j), :] = forward[q]
    last_part, last_left, last_right = forward, left, -slopes[final - 1]
    right = last_right
    right_ref[rows(final - 1), :] = right
    for j in range(final - 2, 0, -1):
        slope = right_ref[rows(j), :]
        left = left_ref[rows(j), :] - slope * left
        right = -slope * right
        forward = [part_ref[q, rows(j), :] - slope * f for q, f in enumerate(forward)]
        left_ref[rows(j), :] = left
        right_ref[rows(j), :] = right
        for q in range(FIELDS):
            part_ref[q, rows(j), :] = forward[q]
    zeros = jnp.zeros_like(left)
    up_first, low_last = coupling(1), coupling(final)
    first_diag = diagonal(0) + up_first * left
    first_up = up_first * right
    last_low = low_last * last_left
    last_diag = diagonal(final) + low_last * last_right
    first_low, last_up = coupling(0), coupling(count)
    for q in range(FIELDS):
        first_ref[pl.ds(q, CHUNKS, stride=8), :] = ends[0][q] - up_first * forward[q]
        last_ref[pl.ds(q, CHUNKS, stride=8), :] = ends[final][q] - low_last * last_part[q]
    ids = sublane_ids(zeros.shape)
    first_ref[pl.ds(5, CHUNKS, stride=8), :] = zeros
    first_ref[pl.ds(6, CHUNKS, stride=8), :] = jnp.where(ids == CHUNKS - 1, -first_up, zeros)
    first_ref[pl.ds(7, CHUNKS, stride=8), :] = zeros
    last_ref[pl.ds(5, CHUNKS, stride=8), :] = jnp.where(ids == 0, -last_low, zeros)
    last_ref[pl.ds(6, CHUNKS, stride=8), :] = zeros
    last_ref[pl.ds(7, CHUNKS, stride=8), :] = zeros

    def row(value, c):
        return value[c : c + 1]

    block = lambda ref, c: ref[pl.ds(8 * c, 8), :]
    chain = []
    for c in range(CHUNKS):
        if c > 0:
            chain.append((row(first_low, c), row(first_diag, c), row(first_up, c), block(first_ref, c)))
        if c < CHUNKS - 1:
            chain.append((row(last_low, c), row(last_diag, c), row(last_up, c), block(last_ref, c)))
    solved, chain_slopes = [], []
    for m, (low, diag, up, rhs) in enumerate(chain):
        if m == 0:
            inverse = 1.0 / diag
            solved.append(rhs * inverse)
        else:
            inverse = 1.0 / (diag - low * chain_slopes[-1])
            solved.append((rhs - low * solved[-1]) * inverse)
        chain_slopes.append(up * inverse)
    for m in range(len(chain) - 2, -1, -1):
        solved[m] = solved[m] - chain_slopes[m] * solved[m + 1]
    inner_ref[0:8, :] = jnp.zeros_like(solved[0])
    inner_ref[120:128, :] = jnp.zeros_like(solved[0])
    for m, value in enumerate(solved):
        inner_ref[8 * m + 8 : 8 * m + 16, :] = value

    for q in range(FIELDS):
        pay_ref[q : q + 1, :] = row(forward[q], 0)
        pay_ref[8 + q : 9 + q, :] = row(last_part[q], CHUNKS - 1)
    pay_ref[5:6, :] = row(left, 0)
    pay_ref[6:8, :] = jnp.zeros((2, zeros.shape[1]), jnp.float32)
    pay_ref[13:14, :] = jnp.zeros((1, zeros.shape[1]), jnp.float32)
    pay_ref[14:15, :] = row(last_right, CHUNKS - 1)
    pay_ref[15:16, :] = jnp.zeros((1, zeros.shape[1]), jnp.float32)
    eight = sublane_ids((8, zeros.shape[1]))
    second = pay_ref[0:8, :] + row(right, 0) * solved[0]
    pay_ref[0:8, :] = jnp.where(eight < FIELDS, -row(up_first, 0) * second, second)
    before = pay_ref[8:16, :] + row(last_left, CHUNKS - 1) * solved[-1]
    pay_ref[8:16, :] = jnp.where(eight < FIELDS, -row(low_last, CHUNKS - 1) * before, before)
    for q in range(FIELDS):
        pay_ref[q : q + 1, :] += row(ends[0][q], 0)
        pay_ref[8 + q : 9 + q, :] += row(ends[final][q], CHUNKS - 1)
    write_payload(cells, viscous, face, count, pay_ref)


def write_payload(cells, viscous, face, count, pay_ref):
    final = count - 1
    first = lambda value: value[0:1]
    last = lambda value: value[CHUNKS - 1 : CHUNKS]
    pay_ref[7:8, :] = first(viscous(0))
    pay_ref[15:16, :] = last(viscous(final))
    pay_ref[ROW_HI : ROW_HI + 1, :] = first(face(1))
    pay_ref[ROW_LO : ROW_LO + 1, :] = last(face(final))
    u_last, f_last = cells(final)
    f_before = cells(final - 1)[1]
    u_first, f_first = cells(0)
    f_second = cells(1)[1]
    for q in range(FIELDS):
        right = ONE_THIRD * last(u_last[q]) + STEP_RATIO * (
            NEAR_WEIGHT * last(f_last[q]) + FAR_WEIGHT * last(f_before[q])
        )
        left = ONE_THIRD * first(u_first[q]) - STEP_RATIO * (
            NEAR_WEIGHT * first(f_first[q]) + FAR_WEIGHT * first(f_second[q])
        )
        pay_ref[ROW_RIGHT + q : ROW_RIGHT + q + 1, :] = right
        pay_ref[ROW_FLUX_RIGHT + q : ROW_FLUX_RIGHT + q + 1, :] = last(f_last[q])
        pay_ref[ROW_LEFT + q : ROW_LEFT + q + 1, :] = left
        pay_ref[ROW_FLUX_LEFT + q : ROW_FLUX_LEFT + q + 1, :] = first(f_first[q])
    pay_ref[38:40, :] = jnp.zeros((2, pay_ref.shape[1]), jnp.float32)


def reduced_solve(me, devices, half, all_ref, coef_ref, out_ref):
    def quantity(row):
        return all_ref[pl.ds(half * PAY_ROWS + row, devices, stride=2 * PAY_ROWS), :]

    first_v, last_v = quantity(7), quantity(15)
    hi_first, lo_last = quantity(ROW_HI), quantity(ROW_LO)
    ids = sublane_ids(first_v.shape)
    at_start, at_end = ids == 0, ids == devices - 1
    v_below = jnp.where(at_start, 0.0, pltpu.roll(last_v, 1, 0))
    v_above = jnp.where(at_end, 0.0, pltpu.roll(first_v, devices - 1, 0))
    lo_first = 0.5 * (v_below + first_v)
    hi_last = 0.5 * (last_v + v_above)
    up_first = ONE_THIRD - hi_first
    low_last = ONE_THIRD - lo_last
    table = (
        jnp.where(at_start, 0.0, ONE_THIRD - lo_first),
        (1.0 + lo_first + hi_first) + up_first * quantity(5),
        up_first * quantity(6),
        low_last * quantity(13),
        (1.0 + lo_last + hi_last) + low_last * quantity(14),
        jnp.where(at_end, 0.0, ONE_THIRD - hi_last),
        1.0 / up_first,
        1.0 / low_last,
    )
    for i, value in enumerate(table):
        coef_ref[i * devices : (i + 1) * devices, :] = value

    def coef(i, d):
        return coef_ref[i * devices + d : i * devices + d + 1, :]

    def piece(d, row, size=8):
        return all_ref[pl.ds((2 * d + half) * PAY_ROWS + row, size), :]

    def one(d, row):
        return piece(d, row, 1)

    slope = value = None
    steps, deltas = [], []
    for d in range(devices):
        rhs_first, rhs_last = piece(d, 0), piece(d, 8)
        delta_second = delta_before = None
        if d > 0:
            delta_second = FAR_SCALED * piece(d - 1, ROW_FLUX_RIGHT)
            rhs_first = rhs_first + piece(d - 1, ROW_RIGHT) + one(d, 5) * delta_second
            rhs_last = rhs_last + one(d, 6) * delta_second
        if d < devices - 1:
            delta_before = -FAR_SCALED * piece(d + 1, ROW_FLUX_LEFT)
            rhs_first = rhs_first + one(d, 13) * delta_before
            rhs_last = rhs_last + piece(d + 1, ROW_LEFT) + one(d, 14) * delta_before
        deltas.append((delta_second, delta_before))
        for base, rhs in ((0, rhs_first), (3, rhs_last)):
            if slope is None:
                inverse = 1.0 / coef(base + 1, d)
                value = rhs * inverse
            else:
                inverse = 1.0 / (coef(base + 1, d) - coef(base, d) * slope)
                value = (rhs - coef(base, d) * value) * inverse
            slope = coef(base + 2, d) * inverse
            steps.append((slope, value))
    following = None
    for d in range(devices - 1, -1, -1):
        x_last = steps[2 * d + 1][1]
        if following is not None:
            x_last = x_last - steps[2 * d + 1][0] * following
        x_first = steps[2 * d][1] - steps[2 * d][0] * x_last
        following = x_first
        delta_second, delta_before = deltas[d]
        seen_first = x_first if delta_second is None else x_first - delta_second * coef(6, d)
        seen_last = x_last if delta_before is None else x_last - delta_before * coef(7, d)
        for i, value in enumerate((x_first, x_last, seen_first, seen_last)):
            out_ref[d * 32 + 8 * i : d * 32 + 8 * i + 8, :] = value
    start = pl.multiple_of(me * 32, 32)
    mine = out_ref[pl.ds(start, 32), :]
    return mine[0:8], mine[8:16], mine[16:24], mine[24:32]


def rebuild(ends, count, part_ref, left_ref, right_ref, inner_ref, sol_ref, store):
    x_first, x_last, seen_first, seen_last = ends
    for m in range(16):
        if m == 0:
            value = seen_first
        elif m == 15:
            value = seen_last
        else:
            inner = inner_ref[8 * m : 8 * m + 8, :]
            value = inner + inner[5:6] * seen_first + inner[6:7] * seen_last
        sol_ref[8 * m : 8 * m + 8, :] = value
    chunk_first = [sol_ref[pl.ds(q, CHUNKS, stride=16), :] for q in range(FIELDS)]
    chunk_last = [sol_ref[pl.ds(8 + q, CHUNKS, stride=16), :] for q in range(FIELDS)]
    ids = sublane_ids(chunk_first[0].shape)
    for q in range(FIELDS):
        store(q, 0, jnp.where(ids == 0, x_first[q : q + 1], chunk_first[q]))
        store(q, count - 1, jnp.where(ids == CHUNKS - 1, x_last[q : q + 1], chunk_last[q]))
    for j in range(1, count - 1):
        left, right = left_ref[pl.ds(j * CHUNKS, CHUNKS), :], right_ref[pl.ds(j * CHUNKS, CHUNKS), :]
        for q in range(FIELDS):
            part = part_ref[q, pl.ds(j * CHUNKS, CHUNKS), :]
            store(q, j, part + left * chunk_first[q] + right * chunk_last[q])


def turn(from_ref, to_ref):
    for i in range(2):
        for k in range(2):
            to_ref[k, i * LANES : (i + 1) * LANES, :] = from_ref[i, k * LANES : (k + 1) * LANES, :].T


def x_kernel(
    count, state_ref, viscous_ref, part_ref, left_ref, right_ref, inner_ref, pay_ref, aux_ref, first_ref, last_ref
):
    def make_cells(j):
        density, mom_x, mom_y, mom_z, energy = (strided(state_ref.at[q], j, count) for q in range(FIELDS))
        inverse = 1.0 / density
        vel_x = mom_x * inverse
        kinetic = mom_x * mom_x + mom_y * mom_y + mom_z * mom_z
        press = GAMMA_MINUS * (energy - 0.5 * kinetic * inverse)
        here = pl.ds(j * CHUNKS, CHUNKS)
        aux_ref[0, here, :] = mom_y * inverse
        aux_ref[1, here, :] = press
        flux = (mom_x, mom_x * vel_x + press, mom_y * vel_x, mom_z * vel_x, (energy + press) * vel_x)
        return (density, mom_x, mom_y, mom_z, energy), flux

    def make_viscous(j):
        value = strided(viscous_ref, j, count)
        aux_ref[2, pl.ds(j * CHUNKS, CHUNKS), :] = value
        return value

    local_solve(
        Window(make_cells, count), Window(make_viscous, count), count,
        part_ref, left_ref, right_ref, inner_ref, pay_ref, first_ref, last_ref,
    )


def y_kernel(
    count, devices, me_ref, all_ref, x_part_ref, x_left_ref, x_right_ref, x_inner_ref, aux_ref,
    part_ref, left_ref, right_ref, inner_ref, pay_ref,
    coef_ref, out_ref, sol_ref, section_ref, turned_ref, first_ref, last_ref,
):
    ends = [reduced_solve(me_ref[0], devices, h, all_ref, coef_ref.at[h], out_ref.at[h]) for h in range(2)]
    for h in range(2):
        def store(q, j, value):
            section_ref[q, h, pl.ds(j * CHUNKS, CHUNKS), :] = value

        rebuild(
            ends[h], count, x_part_ref.at[h], x_left_ref.at[h], x_right_ref.at[h], x_inner_ref.at[h],
            sol_ref.at[h], store,
        )
    for q in range(FIELDS):
        turn(section_ref.at[q], turned_ref.at[q])
    for i in range(3):
        turn(aux_ref.at[:, i], turned_ref.at[FIELDS + i])

    def half(h, _):
        def value(q, j):
            return strided(turned_ref.at[q, h], j, count)

        def make_cells(j):
            section = tuple(value(q, j) for q in range(FIELDS))
            vel_y, press = value(FIELDS, j), value(FIELDS + 1, j)
            flux = (
                vel_y * section[0], vel_y * section[1], vel_y * section[2] + press,
                vel_y * section[3], vel_y * section[4] + press * vel_y,
            )
            return section, flux

        local_solve(
            Window(make_cells, count), Window(lambda j: value(FIELDS + 2, j), count), count,
            part_ref.at[h], left_ref.at[h], right_ref.at[h], inner_ref.at[h], pay_ref.at[h], first_ref, last_ref,
        )
        return 0

    lax.fori_loop(0, 2, half, 0)


def last_kernel(
    count, devices, me_ref, all_ref, part_ref, left_ref, right_ref, inner_ref, new_ref,
    coef_ref, out_ref, sol_ref, section_ref, turned_ref,
):
    ends = [reduced_solve(me_ref[0], devices, h, all_ref, coef_ref.at[h], out_ref.at[h]) for h in range(2)]
    for h in range(2):
        def store(q, j, value):
            section_ref[q, h, pl.ds(j, CHUNKS, stride=count), :] = value

        rebuild(
            ends[h], count, part_ref.at[h], left_ref.at[h], right_ref.at[h], inner_ref.at[h], sol_ref.at[h], store
        )
    for q in range(FIELDS):
        turn(section_ref.at[q], turned_ref.at[q])
        for h in range(2):
            for c in range(CHUNKS):
                for k in range(count // 8):
                    rows = turned_ref[q, h, pl.ds(64 * k + c, 8, stride=CHUNKS), :]
                    new_ref[q, c * count + 8 * k : c * count + 8 * k + 8, h * LANES : (h + 1) * LANES] = rows


def shards(devices_x, devices_y, state, viscous):
    cells = state.shape[2]
    count = cells // CHUNKS
    float_of = lambda *shape: jax.ShapeDtypeStruct(shape, jnp.float32)
    memory = lambda *shape: pltpu.VMEM(shape, jnp.float32)
    params = pltpu.CompilerParams(vmem_limit_bytes=48 * 1024 * 1024)
    whole = pl.BlockSpec(memory_space=pltpu.VMEM)
    scalar = pl.BlockSpec(memory_space=pltpu.SMEM)
    solved_shapes = [
        float_of(2, FIELDS, cells, LANES), float_of(2, cells, LANES), float_of(2, cells, LANES),
        float_of(2, 128, LANES), float_of(2, PAY_ROWS, LANES),
    ]
    half_block = lambda *shape: pl.BlockSpec((None,) + shape, lambda h: (h,) + (0,) * len(shape))
    *x_parts, x_pay, aux = pl.pallas_call(
        functools.partial(x_kernel, count),
        grid=(2,),
        out_shape=solved_shapes + [float_of(2, 3, cells, LANES)],
        in_specs=[
            pl.BlockSpec((FIELDS, cells, LANES), lambda h: (0, 0, h)),
            pl.BlockSpec((cells, LANES), lambda h: (0, h)),
        ],
        out_specs=[half_block(*s.shape[1:]) for s in solved_shapes] + [half_block(3, cells, LANES)],
        scratch_shapes=[memory(64, LANES)] * 2,
        compiler_params=params,
        name="x_lines",
    )(state.reshape(FIELDS, cells, cells), viscous.reshape(cells, cells))
    x_all = lax.all_gather(x_pay, "gx").reshape(devices_x * 2 * PAY_ROWS, LANES)
    me_x = lax.axis_index("gx").astype(jnp.int32).reshape(1)
    me_y = lax.axis_index("gy").astype(jnp.int32).reshape(1)
    *y_parts, y_pay = pl.pallas_call(
        functools.partial(y_kernel, count, devices_x),
        out_shape=solved_shapes,
        in_specs=[scalar] + [whole] * 6,
        out_specs=[whole] * 5,
        scratch_shapes=[
            memory(2, 8 * devices_x, LANES), memory(2, 32 * devices_x, LANES), memory(2, 128, LANES),
            memory(FIELDS, 2, cells, LANES), memory(FIELDS + 3, 2, cells, LANES),
            memory(64, LANES), memory(64, LANES),
        ],
        compiler_params=params,
        name="y_lines",
    )(me_x, x_all, *x_parts, aux)
    copies = jnp.broadcast_to(y_pay[None], (devices_y,) + y_pay.shape)
    y_all = lax.all_to_all(copies, "gy", 0, 0).reshape(devices_y * 2 * PAY_ROWS, LANES)
    new = pl.pallas_call(
        functools.partial(last_kernel, count, devices_y),
        out_shape=float_of(FIELDS, cells, cells),
        in_specs=[scalar] + [whole] * 5,
        out_specs=whole,
        scratch_shapes=[
            memory(2, 8 * devices_y, LANES), memory(2, 32 * devices_y, LANES), memory(2, 128, LANES),
            memory(FIELDS, 2, cells, LANES), memory(FIELDS, 2, cells, LANES),
        ],
        compiler_params=params,
        name="new_state",
    )(me_y, y_all, *y_parts)
    return new.reshape(state.shape)


def solution(mesh):
    placed = (P(None, None, "gx", "gy"), P(None, "gx", "gy"))
    return jax.shard_map(
        functools.partial(shards, mesh.shape["gx"], mesh.shape["gy"]),
        mesh=mesh, in_specs=placed, out_specs=P(None, None, "gx", "gy"), check_vma=False,
    )
```

time: 447 us -> 53.1 us (0.12)
  the two profiles are of different devices: /device:TPU:134 before, /device:TPU:1 now
where the time goes in v1:
time: 53.1 us; the launch traced here: 52.8 us
  blocking collectives  23.1 us (44%)
  waiting for transfers between devices  11.3 us (21%)
  Pallas kernels  8.45 us (16%)
  starting transfers between devices  6.75 us (13%)
  local copies, waits for them, and re-layouts  3.15 us (6%)
    all_gather x1, blocking collectives, shards(): x_all = lax.all_gather(x_pay, 'gx').reshape(devices_x * 2 * PAY_ROWS, LANES)  23.1 us
    all_to_all x1, waiting for transfers between devices, shards(): lax.all_to_all(copies, 'gy', 0, 0).reshape(devices_y * 2 * PAY_ROWS, LANES)  11.3 us
    all_to_all x1, starting transfers between devices, shards(): lax.all_to_all(copies, 'gy', 0, 0).reshape(devices_y * 2 * PAY_ROWS, LANES)  6.75 us
    pallas_call x1, Pallas kernels, shards(): pl.pallas_call(functools.partial(y_kernel, count, devices_x), out_shape=s...  3.56 us
    pallas_call x1, Pallas kernels, shards(): pl.pallas_call(functools.partial(last_kernel, count, devices_y), out_shap...  2.75 us
    unnamed x4, local copies, waits for them, and re-layouts  2.27 us
    pallas_call x1, Pallas kernels, shards(): pl.pallas_call(functools.partial(x_kernel, count), grid=(2,), out_shape=s...  2.14 us
  transfers between devices with their start and end apart: 1, of which 1 were waited for; matrix products, arithmetic and copies ran while one was open for 0% of the time, Pallas kernels for 0%

profile of v1, /device:TPU:1, one launch (start us, length us, event | category | flops | bytes accessed | tf_op | source)
XLA Modules:
  0.0 52.8 jit_solution(3634150868303453990)
XLA Ops:
  0.0 0.0 copy-start
  0.0 1.3 %copy-done = f32[5,1,256,256]{3,2,1,0:T(8,128)S(1)} copy-done((f32[5,1,256,256]{3,2,1,0:T(8,128)S(1)}, f32[5,1,256,256]{3,2,1,0:T(8,128)}, u32[]{:S(2)}) %copy-start) | copy-done | bytes 1310744
  1.3 0.0 copy-start.1
  1.3 0.9 %copy-done.1 = f32[1,256,256]{2,1,0:T(8,128)S(1)} copy-done((f32[1,256,256]{2,1,0:T(8,128)S(1)}, f32[1,256,256]{2,1,0:T(8,128)}, u32[]{:S(2)}) %copy-start.1) | copy-done | bytes 262168
  2.3 2.1 %x_lines.1 = (f32[2,5,256,128]{3,2,1,0:T(8,128)S(1)}, f32[2,256,128]{2,1,0:T(8,128)S(1)}, f32[2,256,128]{2,1,0:T(8,128)S(1)}, f32[2,128,128]{2,1,0:T(8,128)S(1)}...) custom-call(f32[5,256,256]{2,1,0:T(8,128)S(1)} %bitcast.11, f32[256,256]{1,0:T(8,128)S(1)} %bitcast.12), custom_call_target="tpu_custom_call" | custom-call | tf_op jit(solution)/shard_map/x_lines/pallas_call | solution.py:405
  4.4 23.1 %all-gather = f32[32,40,128]{2,1,0:T(8,128)S(1)} all-gather(f32[2,40,128]{2,1,0:T(8,128)S(1)} %get-tuple-element.16), channel_id=2, replica_groups=mesh['gx'=16,'gy'=16] {'gx'}, dimensions={0}, use_global_device_ids=true | all-gather | bytes 696320 | tf_op jit(solution)/shard_map/all_gather | solution.py:418
  27.5 3.6 %y_lines.1 = (f32[2,5,256,128]{3,2,1,0:T(8,128)S(1)}, f32[2,256,128]{2,1,0:T(8,128)S(1)}, f32[2,256,128]{2,1,0:T(8,128)S(1)}, f32[2,128,128]{2,1,0:T(8,128)S(1)}, f32[2,40,128]{2,1,0:T(8,128)S(1)}) custom-call(s32[1]{0:T(128)} %bitcast.1.me_ref, f32[1280,128]{1,0:T(8,128)S(1)} %bitcast.10, f32[2,5,256,128]{3,2,1,0:T(8,128)S(1)} %get-tuple-element.17.x_part_ref, ...), custom_call_target="tpu_custom_call" | custom-call | tf_op jit(solution)/shard_map/y_lines/pallas_call | solution.py:421
  31.1 0.9 %broadcast_in_dim.2 = f32[16,2,40,128]{3,2,1,0:T(8,128)} broadcast(f32[2,40,128]{2,1,0:T(8,128)S(1)} %get-tuple-element.22), dimensions={1,2,3} | broadcast | bytes 696320 | tf_op jit(solution)/shard_map/broadcast_in_dim | solution.py:434
  32.0 6.8 %all-to-all-start = ((f32[16,2,40,128]{3,2,1,0:T(8,128)}), f32[16,2,40,128]{3,2,1,0:T(8,128)S(1)}, u32[]{:S(2)}, u32[]{:S(2)}) async-start(f32[16,2,40,128]{3,2,1,0:T(8,128)} %broadcast_in_dim.2), calls=%async_computation | async-start | bytes 1310720 | tf_op jit(solution)/shard_map/all_to_all | solution.py:435
  38.8 11.3 %all-to-all-done = f32[16,2,40,128]{3,2,1,0:T(8,128)S(1)} async-done(((f32[16,2,40,128]{3,2,1,0:T(8,128)}), f32[16,2,40,128]{3,2,1,0:T(8,128)S(1)}, u32[]{:S(2)}, u32[]{:S(2)}) %all-to-all-start) | async-done | bytes 655392 | tf_op jit(solution)/shard_map/all_to_all | solution.py:435
  50.1 2.7 %new_state.1 = f32[5,256,256]{2,1,0:T(8,128)} custom-call(s32[1]{0:T(128)} %bitcast.me_ref, f32[1280,128]{1,0:T(8,128)S(1)} %bitcast.9, f32[2,5,256,128]{3,2,1,0:T(8,128)S(1)} %get-tuple-element.23.part_ref, f32[2,256,128]{2,1,0:T(8,128)S(1)} %get-tuple-element.24.left_ref, f32[2,256,128]{2,1,0:T(8,128)S(1)} %get-tuple-element.25.right_ref, ...), custom_call_target="tpu_custom_call" | custom-call | tf_op jit(solution)/shard_map/new_state/pallas_call | solution.py:436
Async XLA Ops:
  0.0 1.3 %copy-start = (f32[5,1,256,256]{3,2,1,0:T(8,128)S(1)}, f32[5,1,256,256]{3,2,1,0:T(8,128)}, u32[]{:S(2)}) copy-start(f32[5,1,256,256]{3,2,1,0:T(8,128)} %param.2) | copy-start | bytes 3932164
  1.3 0.9 %copy-start.1 = (f32[1,256,256]{2,1,0:T(8,128)S(1)}, f32[1,256,256]{2,1,0:T(8,128)}, u32[]{:S(2)}) copy-start(f32[1,256,256]{2,1,0:T(8,128)} %param.3) | copy-start | bytes 786436
  32.0 18.1 %all-to-all-start = ((f32[16,2,40,128]{3,2,1,0:T(8,128)}), f32[16,2,40,128]{3,2,1,0:T(8,128)S(1)}, u32[]{:S(2)}, u32[]{:S(2)}) async-start(f32[16,2,40,128]{3,2,1,0:T(8,128)} %broadcast_in_dim.2), calls=%async_computation | async-start | bytes 1310720 | tf_op jit(solution)/shard_map/all_to_all | solution.py:435

commit v2 on v1

v2 whole, which is shorter than its diff:
```python
import functools
import jax
import jax.numpy as jnp
from jax import lax
from jax.experimental import pallas as pl
from jax.experimental.pallas import tpu as pltpu
from jax.sharding import PartitionSpec as P

STEP_RATIO = 0.25
ONE_THIRD = 1.0 / 3.0
NEAR_WEIGHT = 7.0 / 9.0
FAR_WEIGHT = 1.0 / 36.0
GAMMA_MINUS = 0.4
FAR_SCALED = STEP_RATIO * FAR_WEIGHT
FIELDS = 5
CHUNKS = 8
LANES = 128
PAY_ROWS = 40
ROW_RIGHT, ROW_HI, ROW_FLUX_RIGHT, ROW_LEFT, ROW_FLUX_LEFT, ROW_LO = 16, 21, 22, 27, 32, 37


def strided(ref, position, count):
    return ref[pl.ds(position, CHUNKS, stride=count), :]


def sublane_ids(shape):
    return lax.broadcasted_iota(jnp.int32, shape, len(shape) - 2)


def from_previous(value):
    return jnp.where(sublane_ids(value.shape) == 0, 0.0, pltpu.roll(value, 1, value.ndim - 2))


def from_next(value):
    return jnp.where(sublane_ids(value.shape) == CHUNKS - 1, 0.0, pltpu.roll(value, CHUNKS - 1, value.ndim - 2))


class Window:
    def __init__(self, make, count):
        self.make, self.count, self.known = make, count, {}

    def __call__(self, position):
        if position not in self.known:
            if position < 0:
                value = jax.tree.map(from_previous, self(position + self.count))
            elif position >= self.count:
                value = jax.tree.map(from_next, self(position - self.count))
            else:
                value = self.make(position)
            self.known[position] = value
        return self.known[position]


def local_solve(make_cells, make_viscous, count, part_ref, left_ref, right_ref, inner_ref, pay_ref, first_ref, last_ref):
    final, middle = count - 1, count // 2
    viscous = Window(make_viscous, count)
    face = functools.cache(lambda j: 0.5 * (viscous(j - 1) + viscous(j)))
    coupling = functools.cache(lambda j: ONE_THIRD - face(j))
    rows = lambda j: pl.ds(j * CHUNKS, CHUNKS)

    def diagonal(j):
        return 1.0 + face(j) + face(j + 1)

    inverse, tied, slope, reach = {}, {}, {}, {}
    for k in range(1, middle):
        for j, before, outer, inner in ((k, k - 1, k, k + 1), (final - k, final - k + 1, final - k + 1, final - k)):
            pivot = diagonal(j)
            if k > 1:
                pivot = pivot - coupling(outer) * slope[before]
            inverse[j] = 1.0 / pivot
            tied[j] = coupling(outer) * inverse[j]
            slope[j] = coupling(inner) * inverse[j]
            reach[j] = -tied[j] if k == 1 else -tied[j] * reach[before]
    low, high = middle - 1, middle
    meet = 1.0 / (1.0 - slope[low] * slope[high])
    left, right = {}, {}
    left[low], right[low] = reach[low] * meet, -(slope[low] * reach[high]) * meet
    left[high], right[high] = -slope[high] * left[low], reach[high] - slope[high] * right[low]
    for k in range(middle - 2, 0, -1):
        left[k], right[k] = reach[k] - slope[k] * left[k + 1], -slope[k] * right[k + 1]
        m = final - k
        left[m], right[m] = -slope[m] * left[m - 1], reach[m] - slope[m] * right[m - 1]
    for j in range(1, final):
        left_ref[:, rows(j), :] = left[j]
        right_ref[:, rows(j), :] = right[j]

    up_first, low_last = coupling(1), coupling(final)
    for h in range(2):
        cells = Window(functools.partial(make_cells, h), count)

        def source(j, q):
            u_low, u_mid, u_high = cells(j - 1)[0][q], cells(j)[0][q], cells(j + 1)[0][q]
            f = [cells(j + o)[1][q] for o in (-2, -1, 1, 2)]
            central = NEAR_WEIGHT * (f[2] - f[1]) + FAR_WEIGHT * (f[3] - f[0])
            return u_mid + ONE_THIRD * (u_low + u_high) - STEP_RATIO * central

        ends, carried = {}, {}
        for k in range(middle):
            for j, before in ((k, k - 1), (final - k, final - k + 1)):
                values = [source(j, q) for q in range(FIELDS)]
                if k == 0:
                    ends[j] = values
                    continue
                if k == 1:
                    carried[j] = [s * inverse[j][h] for s in values]
                else:
                    carried[j] = [s * inverse[j][h] - tied[j][h] * f for s, f in zip(values, carried[before])]
                if k < middle - 1:
                    for q in range(FIELDS):
                        part_ref[h, q, rows(j), :] = carried[j][q]
        solved_low = [(a - slope[low][h] * b) * meet[h] for a, b in zip(carried[low], carried[high])]
        solved_high = [b - slope[high][h] * a for a, b in zip(solved_low, carried[high])]
        for q in range(FIELDS):
            part_ref[h, q, rows(low), :] = solved_low[q]
            part_ref[h, q, rows(high), :] = solved_high[q]
        for k in range(middle - 2, 0, -1):
            solved_low = [part_ref[h, q, rows(k), :] - slope[k][h] * solved_low[q] for q in range(FIELDS)]
            m = final - k
            solved_high = [part_ref[h, q, rows(m), :] - slope[m][h] * solved_high[q] for q in range(FIELDS)]
            for q in range(FIELDS):
                part_ref[h, q, rows(k), :] = solved_low[q]
                part_ref[h, q, rows(m), :] = solved_high[q]
        for q in range(FIELDS):
            first_ref[h, pl.ds(q, CHUNKS, stride=8), :] = ends[0][q] - up_first[h] * solved_low[q]
            last_ref[h, pl.ds(q, CHUNKS, stride=8), :] = ends[final][q] - low_last[h] * solved_high[q]
            pay_ref[h, q : q + 1, :] = solved_low[q][0:1]
            pay_ref[h, 8 + q : 9 + q, :] = solved_high[q][CHUNKS - 1 : CHUNKS]
            pay_ref[h, ROW_RIGHT + q : ROW_RIGHT + q + 1, :] = ends[0][q][0:1]
            pay_ref[h, ROW_LEFT + q : ROW_LEFT + q + 1, :] = ends[final][q][CHUNKS - 1 : CHUNKS]
        zeros = jnp.zeros((CHUNKS, LANES), jnp.float32)
        ids = sublane_ids(zeros.shape)
        first_ref[h, pl.ds(5, CHUNKS, stride=8), :] = zeros
        first_ref[h, pl.ds(6, CHUNKS, stride=8), :] = jnp.where(ids == CHUNKS - 1, -up_first[h] * right[1][h], zeros)
        first_ref[h, pl.ds(7, CHUNKS, stride=8), :] = zeros
        last_ref[h, pl.ds(5, CHUNKS, stride=8), :] = jnp.where(ids == 0, -low_last[h] * left[final - 1][h], zeros)
        last_ref[h, pl.ds(6, CHUNKS, stride=8), :] = zeros
        last_ref[h, pl.ds(7, CHUNKS, stride=8), :] = zeros
        pay_ref[h, 5:6, :] = left[1][h][0:1]
        pay_ref[h, 6:8, :] = zeros[0:2]
        pay_ref[h, 13:14, :] = zeros[0:1]
        pay_ref[h, 14:15, :] = right[final - 1][h][CHUNKS - 1 : CHUNKS]
        pay_ref[h, 15:16, :] = zeros[0:1]

    def row(value, c):
        return value[:, c : c + 1, :]

    first_low, first_diag, first_up = coupling(0), diagonal(0) + up_first * left[1], up_first * right[1]
    last_low, last_diag = low_last * left[final - 1], diagonal(final) + low_last * right[final - 1]
    last_up = coupling(count)
    chain = []
    for c in range(CHUNKS):
        if c > 0:
            rhs = first_ref[:, 8 * c : 8 * c + 8, :]
            chain.append((row(first_low, c), row(first_diag, c), row(first_up, c), rhs))
        if c < CHUNKS - 1:
            rhs = last_ref[:, 8 * c : 8 * c + 8, :]
            chain.append((row(last_low, c), row(last_diag, c), row(last_up, c), rhs))
    solved = solve_chain(chain)
    inner_ref[:, 0:8, :] = jnp.zeros_like(solved[0])
    inner_ref[:, 120:128, :] = jnp.zeros_like(solved[0])
    for m, value in enumerate(solved):
        inner_ref[:, 8 * m + 8 : 8 * m + 16, :] = value

    eight = sublane_ids((2, 8, LANES))
    second = pay_ref[:, 0:8, :] + row(right[1], 0) * solved[0]
    end = pay_ref[:, ROW_RIGHT : ROW_RIGHT + 8, :]
    pay_ref[:, 0:8, :] = jnp.where(eight < FIELDS, end - row(up_first, 0) * second, second)
    second = pay_ref[:, 8:16, :] + row(left[final - 1], CHUNKS - 1) * solved[-1]
    end = pay_ref[:, ROW_LEFT : ROW_LEFT + 8, :]
    pay_ref[:, 8:16, :] = jnp.where(eight < FIELDS, end - row(low_last, CHUNKS - 1) * second, second)

    first = lambda value: value[..., 0:1, :]
    last = lambda value: value[..., CHUNKS - 1 : CHUNKS, :]
    pay_ref[:, 7:8, :] = first(viscous(0))
    pay_ref[:, 15:16, :] = last(viscous(final))
    pay_ref[:, ROW_HI : ROW_HI + 1, :] = first(face(1))
    pay_ref[:, ROW_LO : ROW_LO + 1, :] = last(face(final))
    pay_ref[:, 38:40, :] = jnp.zeros((2, 2, LANES), jnp.float32)
    for h in range(2):
        u_last, f_last = make_cells(h, final)
        f_before = make_cells(h, final - 1)[1]
        u_first, f_first = make_cells(h, 0)
        f_second = make_cells(h, 1)[1]
        for q in range(FIELDS):
            to_right = ONE_THIRD * u_last[q] + STEP_RATIO * (NEAR_WEIGHT * f_last[q] + FAR_WEIGHT * f_before[q])
            to_left = ONE_THIRD * u_first[q] - STEP_RATIO * (NEAR_WEIGHT * f_first[q] + FAR_WEIGHT * f_second[q])
            pay_ref[h, ROW_RIGHT + q : ROW_RIGHT + q + 1, :] = last(to_right)
            pay_ref[h, ROW_FLUX_RIGHT + q : ROW_FLUX_RIGHT + q + 1, :] = last(f_last[q])
            pay_ref[h, ROW_LEFT + q : ROW_LEFT + q + 1, :] = first(to_left)
            pay_ref[h, ROW_FLUX_LEFT + q : ROW_FLUX_LEFT + q + 1, :] = first(f_first[q])


def solve_chain(chain):
    size, middle = len(chain), len(chain) // 2
    slope, value = [None] * size, [None] * size
    for k in range(middle):
        for m, before in ((k, k - 1), (size - 1 - k, size - k)):
            low, diag, up, rhs = chain[m]
            outer, inner = (low, up) if m < middle else (up, low)
            if k > 0:
                diag = diag - outer * slope[before]
                rhs = rhs - outer * value[before]
            inverse = 1.0 / diag
            value[m] = rhs * inverse
            slope[m] = inner * inverse
    a, b = middle - 1, middle
    value[a] = (value[a] - slope[a] * value[b]) * (1.0 / (1.0 - slope[a] * slope[b]))
    value[b] = value[b] - slope[b] * value[a]
    for k in range(middle - 2, -1, -1):
        value[k] = value[k] - slope[k] * value[k + 1]
        m = size - 1 - k
        value[m] = value[m] - slope[m] * value[m - 1]
    return value


def reduced_solve(me, devices, all_ref, coef_ref, out_ref):
    def quantity(row):
        return jnp.stack(
            [all_ref[pl.ds(h * PAY_ROWS + row, devices, stride=2 * PAY_ROWS), :] for h in range(2)]
        )

    first_v, last_v = quantity(7), quantity(15)
    hi_first, lo_last = quantity(ROW_HI), quantity(ROW_LO)
    ids = sublane_ids(first_v.shape)
    at_start, at_end = ids == 0, ids == devices - 1
    v_below = jnp.where(at_start, 0.0, pltpu.roll(last_v, 1, 1))
    v_above = jnp.where(at_end, 0.0, pltpu.roll(first_v, devices - 1, 1))
    lo_first = 0.5 * (v_below + first_v)
    hi_last = 0.5 * (last_v + v_above)
    up_first = ONE_THIRD - hi_first
    low_last = ONE_THIRD - lo_last
    table = (
        jnp.where(at_start, 0.0, ONE_THIRD - lo_first),
        (1.0 + lo_first + hi_first) + up_first * quantity(5),
        up_first * quantity(6),
        low_last * quantity(13),
        (1.0 + lo_last + hi_last) + low_last * quantity(14),
        jnp.where(at_end, 0.0, ONE_THIRD - hi_last),
        1.0 / up_first,
        1.0 / low_last,
    )
    for i, value in enumerate(table):
        coef_ref[:, i * devices : (i + 1) * devices, :] = value

    def coef(i, d):
        return coef_ref[:, i * devices + d : i * devices + d + 1, :]

    def piece(d, row, size=8):
        return jnp.stack([all_ref[pl.ds((2 * d + h) * PAY_ROWS + row, size), :] for h in range(2)])

    def one(d, row):
        return piece(d, row, 1)

    chain, deltas = [], []
    for d in range(devices):
        rhs_first, rhs_last = piece(d, 0), piece(d, 8)
        delta_second = delta_before = None
        if d > 0:
            delta_second = FAR_SCALED * piece(d - 1, ROW_FLUX_RIGHT)
            rhs_first = rhs_first + piece(d - 1, ROW_RIGHT) + one(d, 5) * delta_second
            rhs_last = rhs_last + one(d, 6) * delta_second
        if d < devices - 1:
            delta_before = -FAR_SCALED * piece(d + 1, ROW_FLUX_LEFT)
            rhs_first = rhs_first + one(d, 13) * delta_before
            rhs_last = rhs_last + piece(d + 1, ROW_LEFT) + one(d, 14) * delta_before
        deltas.append((delta_second, delta_before))
        chain.append((coef(0, d), coef(1, d), coef(2, d), rhs_first))
        chain.append((coef(3, d), coef(4, d), coef(5, d), rhs_last))
    solved = solve_chain(chain)
    for d in range(devices):
        x_first, x_last = solved[2 * d], solved[2 * d + 1]
        delta_second, delta_before = deltas[d]
        seen_first = x_first if delta_second is None else x_first - delta_second * coef(6, d)
        seen_last = x_last if delta_before is None else x_last - delta_before * coef(7, d)
        for i, value in enumerate((x_first, x_last, seen_first, seen_last)):
            out_ref[:, d * 32 + 8 * i : d * 32 + 8 * i + 8, :] = value
    start = pl.multiple_of(me * 32, 32)
    mine = out_ref[:, pl.ds(start, 32), :]
    return [[mine[h, 8 * i : 8 * i + 8] for i in range(4)] for h in range(2)]


def rebuild(ends, count, part_ref, left_ref, right_ref, inner_ref, sol_ref, store):
    x_first, x_last, seen_first, seen_last = ends
    for m in range(16):
        if m == 0:
            value = seen_first
        elif m == 15:
            value = seen_last
        else:
            inner = inner_ref[8 * m : 8 * m + 8, :]
            value = inner + inner[5:6] * seen_first + inner[6:7] * seen_last
        sol_ref[8 * m : 8 * m + 8, :] = value
    chunk_first = [sol_ref[pl.ds(q, CHUNKS, stride=16), :] for q in range(FIELDS)]
    chunk_last = [sol_ref[pl.ds(8 + q, CHUNKS, stride=16), :] for q in range(FIELDS)]
    ids = sublane_ids(chunk_first[0].shape)
    for q in range(FIELDS):
        store(q, 0, jnp.where(ids == 0, x_first[q : q + 1], chunk_first[q]))
        store(q, count - 1, jnp.where(ids == CHUNKS - 1, x_last[q : q + 1], chunk_last[q]))
    for j in range(1, count - 1):
        left, right = left_ref[pl.ds(j * CHUNKS, CHUNKS), :], right_ref[pl.ds(j * CHUNKS, CHUNKS), :]
        for q in range(FIELDS):
            part = part_ref[q, pl.ds(j * CHUNKS, CHUNKS), :]
            store(q, j, part + left * chunk_first[q] + right * chunk_last[q])


def turn(from_ref, to_ref):
    for i in range(2):
        for k in range(2):
            to_ref[k, i * LANES : (i + 1) * LANES, :] = from_ref[i, k * LANES : (k + 1) * LANES, :].T


def lane_half(h):
    return pl.ds(h * LANES, LANES)


def x_kernel(
    count, state_ref, viscous_ref, part_ref, left_ref, right_ref, inner_ref, pay_ref, aux_ref,
    held_ref, first_ref, last_ref, sems,
):
    copies = [
        pltpu.make_async_copy(viscous_ref.at[:, lane_half(h)], held_ref.at[h, FIELDS], sems.at[h, FIELDS])
        for h in range(2)
    ] + [
        pltpu.make_async_copy(state_ref.at[q, :, lane_half(h)], held_ref.at[h, q], sems.at[h, q])
        for h in range(2)
        for q in range(FIELDS)
    ]
    for copy in copies:
        copy.start()
    for copy in copies:
        copy.wait()

    def make_cells(h, j):
        density, mom_x, mom_y, mom_z, energy = (strided(held_ref.at[h, q], j, count) for q in range(FIELDS))
        inverse = 1.0 / density
        vel_x = mom_x * inverse
        kinetic = mom_x * mom_x + mom_y * mom_y + mom_z * mom_z
        press = GAMMA_MINUS * (energy - 0.5 * kinetic * inverse)
        here = pl.ds(j * CHUNKS, CHUNKS)
        aux_ref[h, 0, here, :] = mom_y * inverse
        aux_ref[h, 1, here, :] = press
        flux = (mom_x, mom_x * vel_x + press, mom_y * vel_x, mom_z * vel_x, (energy + press) * vel_x)
        return (density, mom_x, mom_y, mom_z, energy), flux

    def make_viscous(j):
        value = jnp.stack([strided(held_ref.at[h, FIELDS], j, count) for h in range(2)])
        aux_ref[:, 2, pl.ds(j * CHUNKS, CHUNKS), :] = value
        return value

    local_solve(
        make_cells, make_viscous, count, part_ref, left_ref, right_ref, inner_ref, pay_ref, first_ref, last_ref
    )


def y_kernel(
    count, devices, devices_y, me_ref, all_ref, x_part_ref, x_left_ref, x_right_ref, x_inner_ref, aux_ref,
    part_ref, left_ref, right_ref, inner_ref, copies_ref,
    coef_ref, out_ref, sol_ref, section_ref, turned_ref, first_ref, last_ref, pay_ref, sems,
):
    ends = reduced_solve(me_ref[0] // devices_y, devices, all_ref, coef_ref, out_ref)
    for h in range(2):
        def store(q, j, value):
            section_ref[q, h, pl.ds(j * CHUNKS, CHUNKS), :] = value

        rebuild(
            ends[h], count, x_part_ref.at[h], x_left_ref.at[h], x_right_ref.at[h], x_inner_ref.at[h],
            sol_ref.at[h], store,
        )
    for i in range(3):
        turn(aux_ref.at[:, i], turned_ref.at[FIELDS + i])
    for q in range(FIELDS):
        turn(section_ref.at[q], turned_ref.at[q])

    def value(q, h, j):
        return strided(turned_ref.at[q, h], j, count)

    def make_cells(h, j):
        section = tuple(value(q, h, j) for q in range(FIELDS))
        vel_y, press = value(FIELDS, h, j), value(FIELDS + 1, h, j)
        flux = (
            vel_y * section[0], vel_y * section[1], vel_y * section[2] + press,
            vel_y * section[3], vel_y * section[4] + press * vel_y,
        )
        return section, flux

    def make_viscous(j):
        return jnp.stack([value(FIELDS + 2, h, j) for h in range(2)])

    local_solve(
        make_cells, make_viscous, count, part_ref, left_ref, right_ref, inner_ref, pay_ref, first_ref, last_ref
    )
    copies = [
        pltpu.make_async_copy(pay_ref, copies_ref.at[d], sems.at[d]) for d in range(copies_ref.shape[0])
    ]
    for copy in copies:
        copy.start()
    for copy in copies:
        copy.wait()


def last_kernel(
    count, devices, me_ref, all_ref, part_ref, left_ref, right_ref, inner_ref, new_ref,
    coef_ref, out_ref, sol_ref, section_ref, turned_ref, sems,
):
    ends = reduced_solve(lax.rem(me_ref[0], devices), devices, all_ref, coef_ref, out_ref)
    for h in range(2):
        def store(q, j, value):
            section_ref[q, h, pl.ds(j, CHUNKS, stride=count), :] = value

        rebuild(
            ends[h], count, part_ref.at[h], left_ref.at[h], right_ref.at[h], inner_ref.at[h], sol_ref.at[h], store
        )
    copies = []
    for q in range(FIELDS):
        turn(section_ref.at[q], turned_ref.at[q])
        for h in range(2):
            for c in range(CHUNKS):
                for k in range(count // 8):
                    rows = turned_ref[q, h, pl.ds(64 * k + c, 8, stride=CHUNKS), :]
                    section_ref[q, h, c * count + 8 * k : c * count + 8 * k + 8, :] = rows
            copies.append(
                pltpu.make_async_copy(section_ref.at[q, h], new_ref.at[q, :, lane_half(h)], sems.at[q, h])
            )
            copies[-1].start()
    for copy in copies:
        copy.wait()


def shards(devices_x, devices_y, state, viscous):
    cells = state.shape[2]
    count = cells // CHUNKS
    float_of = lambda *shape: jax.ShapeDtypeStruct(shape, jnp.float32)
    memory = lambda *shape: pltpu.VMEM(shape, jnp.float32)
    params = pltpu.CompilerParams(vmem_limit_bytes=48 * 1024 * 1024)
    whole = pl.BlockSpec(memory_space=pltpu.VMEM)
    far = pl.BlockSpec(memory_space=pltpu.HBM)
    scalar = pl.BlockSpec(memory_space=pltpu.SMEM)
    solved_shapes = [
        float_of(2, FIELDS, cells, LANES), float_of(2, cells, LANES), float_of(2, cells, LANES),
        float_of(2, 128, LANES),
    ]
    pay_shape = (2, PAY_ROWS, LANES)
    *x_parts, x_pay, aux = pl.pallas_call(
        functools.partial(x_kernel, count),
        out_shape=solved_shapes + [float_of(*pay_shape), float_of(2, 3, cells, LANES)],
        in_specs=[far] * 2,
        out_specs=[whole] * 6,
        scratch_shapes=[
            memory(2, FIELDS + 1, cells, LANES), memory(2, 64, LANES), memory(2, 64, LANES),
            pltpu.SemaphoreType.DMA((2, FIELDS + 1)),
        ],
        compiler_params=params,
        name="x_lines",
    )(
        pltpu.with_memory_space_constraint(state.reshape(FIELDS, cells, cells), pltpu.HBM),
        pltpu.with_memory_space_constraint(viscous.reshape(cells, cells), pltpu.HBM),
    )
    x_all = lax.all_gather(x_pay, "gx").reshape(devices_x * 2 * PAY_ROWS, LANES)
    me = (lax.axis_index("gx") * devices_y + lax.axis_index("gy")).astype(jnp.int32).reshape(1)

    def solve_scratch(devices):
        return [memory(2, 8 * devices, LANES), memory(2, 32 * devices, LANES), memory(2, 128, LANES)]

    *y_parts, copies = pl.pallas_call(
        functools.partial(y_kernel, count, devices_x, devices_y),
        out_shape=solved_shapes + [float_of(devices_y, *pay_shape)],
        in_specs=[scalar] + [whole] * 6,
        out_specs=[whole] * 4 + [far],
        scratch_shapes=solve_scratch(devices_x) + [
            memory(FIELDS, 2, cells, LANES), memory(FIELDS + 3, 2, cells, LANES),
            memory(2, 64, LANES), memory(2, 64, LANES), memory(*pay_shape),
            pltpu.SemaphoreType.DMA((devices_y,)),
        ],
        compiler_params=params,
        name="y_lines",
    )(me, x_all, *x_parts, aux)
    y_all = lax.all_to_all(copies, "gy", 0, 0).reshape(devices_y * 2 * PAY_ROWS, LANES)
    new = pl.pallas_call(
        functools.partial(last_kernel, count, devices_y),
        out_shape=float_of(FIELDS, cells, cells),
        in_specs=[scalar] + [whole] * 5,
        out_specs=far,
        scratch_shapes=solve_scratch(devices_y) + [
            memory(FIELDS, 2, cells, LANES), memory(FIELDS, 2, cells, LANES),
            pltpu.SemaphoreType.DMA((FIELDS, 2)),
        ],
        compiler_params=params,
        name="new_state",
    )(me, y_all, *y_parts)
    return new.reshape(state.shape)


def solution(mesh):
    placed = (P(None, None, "gx", "gy"), P(None, "gx", "gy"))
    return jax.shard_map(
        functools.partial(shards, mesh.shape["gx"], mesh.shape["gy"]),
        mesh=mesh, in_specs=placed, out_specs=P(None, None, "gx", "gy"), check_vma=False,
    )
```

time: 53.1 us -> 52.4 us (0.987)
  blocking collectives: 23.1 us -> 41.9 us
  waiting for transfers between devices: 11.3 us -> 0 us
  starting transfers between devices: 6.75 us -> 0 us
  local copies, waits for them, and re-layouts: 3.15 us -> 0 us
  Pallas kernels: 8.45 us -> 10.4 us
    all_to_all x0 -> x1, blocking collectives: none -> 18.8 us  [shards(): lax.all_to_all(copies, 'gy', 0, 0).reshape(devices_y * 2 * PAY_ROWS, LANES)]
    all_to_all x1 -> x0, waiting for transfers between devices: 11.3 us -> none  [shards(): lax.all_to_all(copies, 'gy', 0, 0).reshape(devices_y * 2 * PAY_ROWS, LANES)]
    all_to_all x1 -> x0, starting transfers between devices: 6.75 us -> none  [shards(): lax.all_to_all(copies, 'gy', 0, 0).reshape(devices_y * 2 * PAY_ROWS, LANES)]
    unnamed x4 -> x0, local copies, waits for them, and re-layouts: 2.27 us -> none
    pallas_call x2, Pallas kernels: 5.7 us -> 7.66 us  [the longest x1 4.15 us: shards(): pl.pallas_call(functools.partial(y_kernel, count, devices_x, devices_y),...]
    broadcast_in_dim x1 -> x0, local copies, waits for them, and re-layouts: 0.89 us -> none  [shards(): copies = jnp.broadcast_to(y_pay[None], (devices_y,) + y_pay.shape)]
  transfers between devices with their start and end apart: 1 -> 0, of which waited for: 1 -> 0; matrix products, arithmetic and copies ran while one was open for 0% -> 0% of each run, Pallas kernels for 0% -> 0%
where the time goes in v2:
time: 52.4 us; the launch traced here: 52.3 us
  blocking collectives  41.9 us (80%)
  Pallas kernels  10.4 us (20%)
    all_gather x1, blocking collectives, shards(): x_all = lax.all_gather(x_pay, 'gx').reshape(devices_x * 2 * PAY_ROWS, LANES)  23.1 us
    all_to_all x1, blocking collectives, shards(): lax.all_to_all(copies, 'gy', 0, 0).reshape(devices_y * 2 * PAY_ROWS, LANES)  18.8 us
    pallas_call x1, Pallas kernels, shards(): pl.pallas_call(functools.partial(y_kernel, count, devices_x, devices_y),...  4.15 us
    pallas_call x1, Pallas kernels, shards(): pl.pallas_call(functools.partial(x_kernel, count), out_shape=solved_shape...  3.51 us
    pallas_call x1, Pallas kernels, shards(): pl.pallas_call(functools.partial(last_kernel, count, devices_y), out_shap...  2.72 us

profile of v2, /device:TPU:1, one launch (start us, length us, event | category | flops | bytes accessed | tf_op | source)
XLA Modules:
  0.0 52.3 jit_solution(12650389877703378470)
XLA Ops:
  0.0 3.5 %x_lines.1 = (f32[2,5,256,128]{3,2,1,0:T(8,128)S(1)}, f32[2,256,128]{2,1,0:T(8,128)S(1)}, f32[2,256,128]{2,1,0:T(8,128)S(1)}, f32[2,128,128]{2,1,0:T(8,128)S(1)}...) custom-call(f32[5,256,256]{2,1,0:T(8,128)} %bitcast.10, f32[256,256]{1,0:T(8,128)} %bitcast.11), custom_call_target="tpu_custom_call" | custom-call | tf_op jit(solution)/shard_map/x_lines/pallas_call | solution.py:443
  3.5 23.1 %all-gather = f32[32,40,128]{2,1,0:T(8,128)S(1)} all-gather(f32[2,40,128]{2,1,0:T(8,128)S(1)} %get-tuple-element.16), channel_id=2, replica_groups=mesh['gx'=16,'gy'=16] {'gx'}, dimensions={0}, use_global_device_ids=true | all-gather | bytes 696320 | tf_op jit(solution)/shard_map/all_gather | solution.py:458
  26.6 4.1 %y_lines.1 = (f32[2,5,256,128]{3,2,1,0:T(8,128)S(1)}, f32[2,256,128]{2,1,0:T(8,128)S(1)}, f32[2,256,128]{2,1,0:T(8,128)S(1)}, f32[2,128,128]{2,1,0:T(8,128)S(1)}, f32[16,2,40,128]{3,2,1,0:T(8,128)S(1)}) custom-call(s32[1]{0:T(128)} %bitcast.me_ref, f32[1280,128]{1,0:T(8,128)S(1)} %bitcast.8, f32[2,5,256,128]{3,2,1,0:T(8,128)S(1)} %get-tuple-element.17.x_part_ref, ...), custom_call_target="tpu_custom_call" | custom-call | tf_op jit(solution)/shard_map/y_lines/pallas_call | solution.py:464
  30.8 18.8 %all_to_all.5 = f32[16,2,40,128]{3,2,1,0:T(8,128)S(1)} all-to-all(f32[16,2,40,128]{3,2,1,0:T(8,128)S(1)} %get-tuple-element.22), channel_id=1, replica_groups=mesh['gx'=16,'gy'=16] {'gy'}, dimensions={0} | all-to-all | bytes 1310720 | tf_op jit(solution)/shard_map/all_to_all | solution.py:477
  49.6 2.7 %new_state.1 = f32[5,256,256]{2,1,0:T(8,128)} custom-call(s32[1]{0:T(128)} %bitcast.me_ref, f32[1280,128]{1,0:T(8,128)S(1)} %bitcast.9, f32[2,5,256,128]{3,2,1,0:T(8,128)S(1)} %get-tuple-element.23.part_ref, f32[2,256,128]{2,1,0:T(8,128)S(1)} %get-tuple-element.24.left_ref, f32[2,256,128]{2,1,0:T(8,128)S(1)} %get-tuple-element.25.right_ref, ...), custom_call_target="tpu_custom_call" | custom-call | tf_op jit(solution)/shard_map/new_state/pallas_call | solution.py:478

commit v3 on v2

--- a/solution.py
+++ b/solution.py
@@ -11,7 +11,8 @@
 NEAR_WEIGHT = 7.0 / 9.0
 FAR_WEIGHT = 1.0 / 36.0
 GAMMA_MINUS = 0.4
-FAR_SCALED = STEP_RATIO * FAR_WEIGHT
+NEAR_SCALED = STEP_RATIO * NEAR_WEIGHT
+FAR_RATIO = FAR_WEIGHT / NEAR_WEIGHT
 FIELDS = 5
 CHUNKS = 8
 LANES = 128
@@ -35,28 +36,22 @@
     return jnp.where(sublane_ids(value.shape) == CHUNKS - 1, 0.0, pltpu.roll(value, CHUNKS - 1, value.ndim - 2))
 
 
-class Window:
-    def __init__(self, make, count):
-        self.make, self.count, self.known = make, count, {}
-
-    def __call__(self, position):
-        if position not in self.known:
-            if position < 0:
-                value = jax.tree.map(from_previous, self(position + self.count))
-            elif position >= self.count:
-                value = jax.tree.map(from_next, self(position - self.count))
-            else:
-                value = self.make(position)
-            self.known[position] = value
-        return self.known[position]
-
-
-def local_solve(make_cells, make_viscous, count, part_ref, left_ref, right_ref, inner_ref, pay_ref, first_ref, last_ref):
+def local_solve(
+    ready, make_terms, viscous_at, count, part_ref, left_ref, right_ref, inner_ref, pay_ref, first_ref, last_ref
+):
     final, middle = count - 1, count // 2
-    viscous = Window(make_viscous, count)
+    rows = lambda j: pl.ds(j * CHUNKS, CHUNKS)
+
+    @functools.cache
+    def viscous(j):
+        if j < 0:
+            return from_previous(viscous(j + count))
+        if j >= count:
+            return from_next(viscous(j - count))
+        return viscous_at(j)
+
     face = functools.cache(lambda j: 0.5 * (viscous(j - 1) + viscous(j)))
     coupling = functools.cache(lambda j: ONE_THIRD - face(j))
-    rows = lambda j: pl.ds(j * CHUNKS, CHUNKS)
 
     def diagonal(j):
         return 1.0 + face(j) + face(j + 1)
@@ -84,49 +79,90 @@
         left_ref[:, rows(j), :] = left[j]
         right_ref[:, rows(j), :] = right[j]
 
+    first = lambda value: value[..., 0:1, :]
+    last = lambda value: value[..., CHUNKS - 1 : CHUNKS, :]
     up_first, low_last = coupling(1), coupling(final)
+    fields = range(FIELDS)
     for h in range(2):
-        cells = Window(functools.partial(make_cells, h), count)
-
-        def source(j, q):
-            u_low, u_mid, u_high = cells(j - 1)[0][q], cells(j)[0][q], cells(j + 1)[0][q]
-            f = [cells(j + o)[1][q] for o in (-2, -1, 1, 2)]
-            central = NEAR_WEIGHT * (f[2] - f[1]) + FAR_WEIGHT * (f[3] - f[0])
-            return u_mid + ONE_THIRD * (u_low + u_high) - STEP_RATIO * central
-
-        ends, carried = {}, {}
-        for k in range(middle):
-            for j, before in ((k, k - 1), (final - k, final - k + 1)):
-                values = [source(j, q) for q in range(FIELDS)]
-                if k == 0:
-                    ends[j] = values
-                    continue
-                if k == 1:
-                    carried[j] = [s * inverse[j][h] for s in values]
+        ready(h)
+        ends, carried = {}, None
+
+        def take(j, sums):
+            nonlocal carried
+            if j == 0 or j == final:
+                ends[j] = sums
+                return
+            if j == 1:
+                carried = [s * inverse[j][h] for s in sums]
+            elif j < middle:
+                carried = [s * inverse[j][h] - tied[j][h] * f for s, f in zip(sums, carried)]
+            for q in fields:
+                part_ref[h, q, rows(j), :] = carried[q] if j < middle else sums[q]
+
+        before, end = make_terms(h, final - 1), make_terms(h, final)
+        for q in fields:
+            pay_ref[h, ROW_RIGHT + q : ROW_RIGHT + q + 1, :] = last(end[q][2] + before[q][3])
+            pay_ref[h, ROW_FLUX_RIGHT + q : ROW_FLUX_RIGHT + q + 1, :] = last(end[q][3])
+        sums = {
+            0: [from_previous(end[q][2] + before[q][3]) for q in fields],
+            1: [from_previous(end[q][3]) for q in fields],
+        }
+        for j in range(count):
+            terms = make_terms(h, j)
+            if j == 0:
+                zero = terms
+            if j == 1:
+                above_last = [from_next(zero[q][1] - terms[q][3]) for q in fields]
+                above_before = [from_next(zero[q][3]) for q in fields]
+                for q in fields:
+                    to_left = first(zero[q][1] - terms[q][3])
+                    pay_ref[h, ROW_LEFT + q : ROW_LEFT + q + 1, :] = to_left
+                    pay_ref[h, ROW_FLUX_LEFT + q : ROW_FLUX_LEFT + q + 1, :] = -first(zero[q][3])
+            if j >= 2:
+                take(j - 2, [sums[j - 2][q] - terms[q][3] for q in fields])
+                del sums[j - 2]
+            if j >= 1:
+                sums[j - 1] = [sums[j - 1][q] + terms[q][1] for q in fields]
+            sums[j] = [sums[j][q] + terms[q][0] for q in fields]
+            if j < final:
+                if j == 0:
+                    sums[1] = [sums[1][q] + terms[q][2] for q in fields]
                 else:
-                    carried[j] = [s * inverse[j][h] - tied[j][h] * f for s, f in zip(values, carried[before])]
-                if k < middle - 1:
-                    for q in range(FIELDS):
-                        part_ref[h, q, rows(j), :] = carried[j][q]
-        solved_low = [(a - slope[low][h] * b) * meet[h] for a, b in zip(carried[low], carried[high])]
-        solved_high = [b - slope[high][h] * a for a, b in zip(solved_low, carried[high])]
-        for q in range(FIELDS):
+                    sums[j + 1] = [sums[j + 1][q] + terms[q][2] for q in fields]
+            if j < final - 1:
+                sums[j + 2] = [terms[q][3] for q in fields]
+        take(final - 1, [sums[final - 1][q] - above_before[q] for q in fields])
+        take(final, [sums[final][q] + above_last[q] for q in fields])
+
+        upper = None
+        for j in range(final - 1, middle - 1, -1):
+            values = [part_ref[h, q, rows(j), :] for q in fields]
+            if upper is None:
+                upper = [s * inverse[j][h] for s in values]
+            else:
+                upper = [s * inverse[j][h] - tied[j][h] * f for s, f in zip(values, upper)]
+            if j > middle:
+                for q in fields:
+                    part_ref[h, q, rows(j), :] = upper[q]
+        solved_low = [(a - slope[low][h] * b) * meet[h] for a, b in zip(carried, upper)]
+        solved_high = [b - slope[high][h] * a for a, b in zip(solved_low, upper)]
+        for q in fields:
             part_ref[h, q, rows(low), :] = solved_low[q]
             part_ref[h, q, rows(high), :] = solved_high[q]
         for k in range(middle - 2, 0, -1):
-            solved_low = [part_ref[h, q, rows(k), :] - slope[k][h] * solved_low[q] for q in range(FIELDS)]
+            solved_low = [part_ref[h, q, rows(k), :] - slope[k][h] * solved_low[q] for q in fields]
             m = final - k
-            solved_high = [part_ref[h, q, rows(m), :] - slope[m][h] * solved_high[q] for q in range(FIELDS)]
-            for q in range(FIELDS):
+            solved_high = [part_ref[h, q, rows(m), :] - slope[m][h] * solved_high[q] for q in fields]
+            for q in fields:
                 part_ref[h, q, rows(k), :] = solved_low[q]
                 part_ref[h, q, rows(m), :] = solved_high[q]
-        for q in range(FIELDS):
+        for q in fields:
             first_ref[h, pl.ds(q, CHUNKS, stride=8), :] = ends[0][q] - up_first[h] * solved_low[q]
             last_ref[h, pl.ds(q, CHUNKS, stride=8), :] = ends[final][q] - low_last[h] * solved_high[q]
-            pay_ref[h, q : q + 1, :] = solved_low[q][0:1]
-            pay_ref[h, 8 + q : 9 + q, :] = solved_high[q][CHUNKS - 1 : CHUNKS]
-            pay_ref[h, ROW_RIGHT + q : ROW_RIGHT + q + 1, :] = ends[0][q][0:1]
-            pay_ref[h, ROW_LEFT + q : ROW_LEFT + q + 1, :] = ends[final][q][CHUNKS - 1 : CHUNKS]
+            pay_ref[h, q : q + 1, :] = first(solved_low[q])
+            pay_ref[h, 8 + q : 9 + q, :] = last(solved_high[q])
+            first_ref[h, 64 + q : 65 + q, :] = first(ends[0][q])
+            last_ref[h, 64 + q : 65 + q, :] = last(ends[final][q])
         zeros = jnp.zeros((CHUNKS, LANES), jnp.float32)
         ids = sublane_ids(zeros.shape)
         first_ref[h, pl.ds(5, CHUNKS, stride=8), :] = zeros
@@ -135,10 +171,10 @@
         last_ref[h, pl.ds(5, CHUNKS, stride=8), :] = jnp.where(ids == 0, -low_last[h] * left[final - 1][h], zeros)
         last_ref[h, pl.ds(6, CHUNKS, stride=8), :] = zeros
         last_ref[h, pl.ds(7, CHUNKS, stride=8), :] = zeros
-        pay_ref[h, 5:6, :] = left[1][h][0:1]
+        pay_ref[h, 5:6, :] = first(left[1][h])
         pay_ref[h, 6:8, :] = zeros[0:2]
         pay_ref[h, 13:14, :] = zeros[0:1]
-        pay_ref[h, 14:15, :] = right[final - 1][h][CHUNKS - 1 : CHUNKS]
+        pay_ref[h, 14:15, :] = last(right[final - 1][h])
         pay_ref[h, 15:16, :] = zeros[0:1]
 
     def row(value, c):
@@ -163,31 +199,16 @@
 
     eight = sublane_ids((2, 8, LANES))
     second = pay_ref[:, 0:8, :] + row(right[1], 0) * solved[0]
-    end = pay_ref[:, ROW_RIGHT : ROW_RIGHT + 8, :]
-    pay_ref[:, 0:8, :] = jnp.where(eight < FIELDS, end - row(up_first, 0) * second, second)
+    pay_ref[:, 0:8, :] = jnp.where(eight < FIELDS, first_ref[:, 64:72, :] - row(up_first, 0) * second, second)
     second = pay_ref[:, 8:16, :] + row(left[final - 1], CHUNKS - 1) * solved[-1]
-    end = pay_ref[:, ROW_LEFT : ROW_LEFT + 8, :]
-    pay_ref[:, 8:16, :] = jnp.where(eight < FIELDS, end - row(low_last, CHUNKS - 1) * second, second)
-
-    first = lambda value: value[..., 0:1, :]
-    last = lambda value: value[..., CHUNKS - 1 : CHUNKS, :]
+    pay_ref[:, 8:16, :] = jnp.where(
+        eight < FIELDS, last_ref[:, 64:72, :] - row(low_last, CHUNKS - 1) * second, second
+    )
     pay_ref[:, 7:8, :] = first(viscous(0))
     pay_ref[:, 15:16, :] = last(viscous(final))
     pay_ref[:, ROW_HI : ROW_HI + 1, :] = first(face(1))
     pay_ref[:, ROW_LO : ROW_LO + 1, :] = last(face(final))
     pay_ref[:, 38:40, :] = jnp.zeros((2, 2, LANES), jnp.float32)
-    for h in range(2):
-        u_last, f_last = make_cells(h, final)
-        f_before = make_cells(h, final - 1)[1]
-        u_first, f_first = make_cells(h, 0)
-        f_second = make_cells(h, 1)[1]
-        for q in range(FIELDS):
-            to_right = ONE_THIRD * u_last[q] + STEP_RATIO * (NEAR_WEIGHT * f_last[q] + FAR_WEIGHT * f_before[q])
-            to_left = ONE_THIRD * u_first[q] - STEP_RATIO * (NEAR_WEIGHT * f_first[q] + FAR_WEIGHT * f_second[q])
-            pay_ref[h, ROW_RIGHT + q : ROW_RIGHT + q + 1, :] = last(to_right)
-            pay_ref[h, ROW_FLUX_RIGHT + q : ROW_FLUX_RIGHT + q + 1, :] = last(f_last[q])
-            pay_ref[h, ROW_LEFT + q : ROW_LEFT + q + 1, :] = first(to_left)
-            pay_ref[h, ROW_FLUX_LEFT + q : ROW_FLUX_LEFT + q + 1, :] = first(f_first[q])
 
 
 def solve_chain(chain):
@@ -256,11 +277,11 @@
         rhs_first, rhs_last = piece(d, 0), piece(d, 8)
         delta_second = delta_before = None
         if d > 0:
-            delta_second = FAR_SCALED * piece(d - 1, ROW_FLUX_RIGHT)
+            delta_second = piece(d - 1, ROW_FLUX_RIGHT)
             rhs_first = rhs_first + piece(d - 1, ROW_RIGHT) + one(d, 5) * delta_second
             rhs_last = rhs_last + one(d, 6) * delta_second
         if d < devices - 1:
-            delta_before = -FAR_SCALED * piece(d + 1, ROW_FLUX_LEFT)
+            delta_before = piece(d + 1, ROW_FLUX_LEFT)
             rhs_first = rhs_first + one(d, 13) * delta_before
             rhs_last = rhs_last + piece(d + 1, ROW_LEFT) + one(d, 14) * delta_before
         deltas.append((delta_second, delta_before))
@@ -279,7 +300,7 @@
     return [[mine[h, 8 * i : 8 * i + 8] for i in range(4)] for h in range(2)]
 
 
-def rebuild(ends, count, part_ref, left_ref, right_ref, inner_ref, sol_ref, store):
+def rebuild(ends, count, part_ref, left_ref, right_ref, inner_ref, sol_ref):
     x_first, x_last, seen_first, seen_last = ends
     for m in range(16):
         if m == 0:
@@ -293,20 +314,24 @@
     chunk_first = [sol_ref[pl.ds(q, CHUNKS, stride=16), :] for q in range(FIELDS)]
     chunk_last = [sol_ref[pl.ds(8 + q, CHUNKS, stride=16), :] for q in range(FIELDS)]
     ids = sublane_ids(chunk_first[0].shape)
-    for q in range(FIELDS):
-        store(q, 0, jnp.where(ids == 0, x_first[q : q + 1], chunk_first[q]))
-        store(q, count - 1, jnp.where(ids == CHUNKS - 1, x_last[q : q + 1], chunk_last[q]))
-    for j in range(1, count - 1):
-        left, right = left_ref[pl.ds(j * CHUNKS, CHUNKS), :], right_ref[pl.ds(j * CHUNKS, CHUNKS), :]
-        for q in range(FIELDS):
-            part = part_ref[q, pl.ds(j * CHUNKS, CHUNKS), :]
-            store(q, j, part + left * chunk_first[q] + right * chunk_last[q])
-
-
-def turn(from_ref, to_ref):
-    for i in range(2):
-        for k in range(2):
-            to_ref[k, i * LANES : (i + 1) * LANES, :] = from_ref[i, k * LANES : (k + 1) * LANES, :].T
+
+    def solution_at(q, j):
+        if j == 0:
+            return jnp.where(ids == 0, x_first[q : q + 1], chunk_first[q])
+        if j == count - 1:
+            return jnp.where(ids == CHUNKS - 1, x_last[q : q + 1], chunk_last[q])
+        here = pl.ds(j * CHUNKS, CHUNKS)
+        return part_ref[q, here, :] + left_ref[here, :] * chunk_first[q] + right_ref[here, :] * chunk_last[q]
+
+    return solution_at
+
+
+def turn(count, from_ref, to_ref):
+    for k in range(2):
+        starts = [64 * t + c for c in range(4 * k, 4 * k + 4) for t in range(count // 8)]
+        for i in range(2):
+            tiles = [from_ref[i, pl.ds(start, 8, stride=CHUNKS), :] for start in starts]
+            to_ref[k, i * LANES : (i + 1) * LANES, :] = jnp.concatenate(tiles, 0).T
 
 
 def lane_half(h):
@@ -327,28 +352,46 @@
     ]
     for copy in copies:
         copy.start()
-    for copy in copies:
+    for copy in copies[:2]:
         copy.wait()
 
-    def make_cells(h, j):
+    def ready(h):
+        for copy in copies[2 + FIELDS * h : 2 + FIELDS * (h + 1)]:
+            copy.wait()
+
+    def make_terms(h, j):
         density, mom_x, mom_y, mom_z, energy = (strided(held_ref.at[h, q], j, count) for q in range(FIELDS))
         inverse = 1.0 / density
-        vel_x = mom_x * inverse
+        vel_x = (NEAR_SCALED * inverse) * mom_x
         kinetic = mom_x * mom_x + mom_y * mom_y + mom_z * mom_z
         press = GAMMA_MINUS * (energy - 0.5 * kinetic * inverse)
         here = pl.ds(j * CHUNKS, CHUNKS)
-        aux_ref[h, 0, here, :] = mom_y * inverse
+        aux_ref[h, 0, here, :] = (NEAR_SCALED * inverse) * mom_y
         aux_ref[h, 1, here, :] = press
-        flux = (mom_x, mom_x * vel_x + press, mom_y * vel_x, mom_z * vel_x, (energy + press) * vel_x)
-        return (density, mom_x, mom_y, mom_z, energy), flux
-
-    def make_viscous(j):
+        low, high, far = ONE_THIRD - vel_x, ONE_THIRD + vel_x, FAR_RATIO * vel_x
+
+        def general(u, flux):
+            third = ONE_THIRD * u
+            return u, third - flux, third + flux, FAR_RATIO * flux
+
+        def carried(u):
+            return u, low * u, high * u, far * u
+
+        return (
+            general(density, NEAR_SCALED * mom_x),
+            general(mom_x, mom_x * vel_x + NEAR_SCALED * press),
+            carried(mom_y),
+            carried(mom_z),
+            general(energy, (energy + press) * vel_x),
+        )
+
+    def viscous_at(j):
         value = jnp.stack([strided(held_ref.at[h, FIELDS], j, count) for h in range(2)])
         aux_ref[:, 2, pl.ds(j * CHUNKS, CHUNKS), :] = value
         return value
 
     local_solve(
-        make_cells, make_viscous, count, part_ref, left_ref, right_ref, inner_ref, pay_ref, first_ref, last_ref
+        ready, make_terms, viscous_at, count, part_ref, left_ref, right_ref, inner_ref, pay_ref, first_ref, last_ref
     )
 
 
@@ -358,36 +401,47 @@
     coef_ref, out_ref, sol_ref, section_ref, turned_ref, first_ref, last_ref, pay_ref, sems,
 ):
     ends = reduced_solve(me_ref[0] // devices_y, devices, all_ref, coef_ref, out_ref)
-    for h in range(2):
-        def store(q, j, value):
-            section_ref[q, h, pl.ds(j * CHUNKS, CHUNKS), :] = value
-
+    for i in range(3):
+        turn(count, aux_ref.at[:, i], turned_ref.at[FIELDS + i])
+    halves = [
         rebuild(
-            ends[h], count, x_part_ref.at[h], x_left_ref.at[h], x_right_ref.at[h], x_inner_ref.at[h],
-            sol_ref.at[h], store,
+            ends[h], count, x_part_ref.at[h], x_left_ref.at[h], x_right_ref.at[h], x_inner_ref.at[h], sol_ref.at[h]
         )
-    for i in range(3):
-        turn(aux_ref.at[:, i], turned_ref.at[FIELDS + i])
+        for h in range(2)
+    ]
     for q in range(FIELDS):
-        turn(section_ref.at[q], turned_ref.at[q])
+        for h in range(2):
+            for j in range(count):
+                section_ref[q, h, pl.ds(j * CHUNKS, CHUNKS), :] = halves[h](q, j)
+        turn(count, section_ref.at[q], turned_ref.at[q])
 
     def value(q, h, j):
         return strided(turned_ref.at[q, h], j, count)
 
-    def make_cells(h, j):
-        section = tuple(value(q, h, j) for q in range(FIELDS))
+    def make_terms(h, j):
         vel_y, press = value(FIELDS, h, j), value(FIELDS + 1, h, j)
-        flux = (
-            vel_y * section[0], vel_y * section[1], vel_y * section[2] + press,
-            vel_y * section[3], vel_y * section[4] + press * vel_y,
+        low, high, far = ONE_THIRD - vel_y, ONE_THIRD + vel_y, FAR_RATIO * vel_y
+
+        def carried(u):
+            return u, low * u, high * u, far * u
+
+        def pressed(u, flux):
+            return u, low * u - flux, high * u + flux, far * u + FAR_RATIO * flux
+
+        return (
+            carried(value(0, h, j)),
+            carried(value(1, h, j)),
+            pressed(value(2, h, j), NEAR_SCALED * press),
+            carried(value(3, h, j)),
+            pressed(value(4, h, j), press * vel_y),
         )
-        return section, flux
-
-    def make_viscous(j):
+
+    def viscous_at(j):
         return jnp.stack([value(FIELDS + 2, h, j) for h in range(2)])
 
     local_solve(
-        make_cells, make_viscous, count, part_ref, left_ref, right_ref, inner_ref, pay_ref, first_ref, last_ref
+        lambda h: None, make_terms, viscous_at, count,
+        part_ref, left_ref, right_ref, inner_ref, pay_ref, first_ref, last_ref,
     )
     copies = [
         pltpu.make_async_copy(pay_ref, copies_ref.at[d], sems.at[d]) for d in range(copies_ref.shape[0])
@@ -403,23 +457,19 @@
     coef_ref, out_ref, sol_ref, section_ref, turned_ref, sems,
 ):
     ends = reduced_solve(lax.rem(me_ref[0], devices), devices, all_ref, coef_ref, out_ref)
-    for h in range(2):
-        def store(q, j, value):
-            section_ref[q, h, pl.ds(j, CHUNKS, stride=count), :] = value
-
-        rebuild(
-            ends[h], count, part_ref.at[h], left_ref.at[h], right_ref.at[h], inner_ref.at[h], sol_ref.at[h], store
-        )
+    halves = [
+        rebuild(ends[h], count, part_ref.at[h], left_ref.at[h], right_ref.at[h], inner_ref.at[h], sol_ref.at[h])
+        for h in range(2)
+    ]
     copies = []
     for q in range(FIELDS):
-        turn(section_ref.at[q], turned_ref.at[q])
         for h in range(2):
-            for c in range(CHUNKS):
-                for k in range(count // 8):
-                    rows = turned_ref[q, h, pl.ds(64 * k + c, 8, stride=CHUNKS), :]
-                    section_ref[q, h, c * count + 8 * k : c * count + 8 * k + 8, :] = rows
+            for j in range(count):
+                section_ref[q, h, pl.ds(j * CHUNKS, CHUNKS), :] = halves[h](q, j)
+        turn(count, section_ref.at[q], turned_ref.at[q])
+        for h in range(2):
             copies.append(
-                pltpu.make_async_copy(section_ref.at[q, h], new_ref.at[q, :, lane_half(h)], sems.at[q, h])
+                pltpu.make_async_copy(turned_ref.at[q, h], new_ref.at[q, :, lane_half(h)], sems.at[q, h])
             )
             copies[-1].start()
     for copy in copies:
@@ -446,7 +496,7 @@
         in_specs=[far] * 2,
         out_specs=[whole] * 6,
         scratch_shapes=[
-            memory(2, FIELDS + 1, cells, LANES), memory(2, 64, LANES), memory(2, 64, LANES),
+            memory(2, FIELDS + 1, cells, LANES), memory(2, 72, LANES), memory(2, 72, LANES),
             pltpu.SemaphoreType.DMA((2, FIELDS + 1)),
         ],
         compiler_params=params,
@@ -468,7 +518,7 @@
         out_specs=[whole] * 4 + [far],
         scratch_shapes=solve_scratch(devices_x) + [
             memory(FIELDS, 2, cells, LANES), memory(FIELDS + 3, 2, cells, LANES),
-            memory(2, 64, LANES), memory(2, 64, LANES), memory(*pay_shape),
+            memory(2, 72, LANES), memory(2, 72, LANES), memory(*pay_shape),
             pltpu.SemaphoreType.DMA((devices_y,)),
         ],
         compiler_params=params,

time: 52.4 us -> 50.7 us (0.968)
  Pallas kernels: 10.4 us -> 8.61 us
    pallas_call x1, Pallas kernels: 2.72 us -> 1.71 us  [shards(): pl.pallas_call(functools.partial(last_kernel, count, devices_y), out_shap...]
    pallas_call x1, Pallas kernels: 3.51 us -> 2.85 us  [shards(): pl.pallas_call(functools.partial(x_kernel, count), out_shape=solved_shape...]
where the time goes in v3:
time: 50.7 us; the launch traced here: 50.5 us
  blocking collectives  41.9 us (83%)
  Pallas kernels  8.61 us (17%)
    all_gather x1, blocking collectives, shards(): x_all = lax.all_gather(x_pay, 'gx').reshape(devices_x * 2 * PAY_ROWS, LANES)  23.1 us
    all_to_all x1, blocking collectives, shards(): lax.all_to_all(copies, 'gy', 0, 0).reshape(devices_y * 2 * PAY_ROWS, LANES)  18.8 us
    pallas_call x1, Pallas kernels, shards(): pl.pallas_call(functools.partial(y_kernel, count, devices_x, devices_y),...  4.04 us
    pallas_call x1, Pallas kernels, shards(): pl.pallas_call(functools.partial(x_kernel, count), out_shape=solved_shape...  2.85 us
    pallas_call x1, Pallas kernels, shards(): pl.pallas_call(functools.partial(last_kernel, count, devices_y), out_shap...  1.71 us

profile of v3, /device:TPU:1, one launch (start us, length us, event | category | flops | bytes accessed | tf_op | source)
XLA Modules:
  0.0 50.5 jit_solution(9652135712334903692)
XLA Ops:
  0.0 2.9 %x_lines.1 = (f32[2,5,256,128]{3,2,1,0:T(8,128)S(1)}, f32[2,256,128]{2,1,0:T(8,128)S(1)}, f32[2,256,128]{2,1,0:T(8,128)S(1)}, f32[2,128,128]{2,1,0:T(8,128)S(1)}...) custom-call(f32[5,256,256]{2,1,0:T(8,128)} %bitcast.10, f32[256,256]{1,0:T(8,128)} %bitcast.11), custom_call_target="tpu_custom_call" | custom-call | tf_op jit(solution)/shard_map/x_lines/pallas_call | solution.py:493
  2.9 23.1 %all-gather = f32[32,40,128]{2,1,0:T(8,128)S(1)} all-gather(f32[2,40,128]{2,1,0:T(8,128)S(1)} %get-tuple-element.16), channel_id=2, replica_groups=mesh['gx'=16,'gy'=16] {'gx'}, dimensions={0}, use_global_device_ids=true | all-gather | bytes 696320 | tf_op jit(solution)/shard_map/all_gather | solution.py:508
  26.0 4.0 %y_lines.1 = (f32[2,5,256,128]{3,2,1,0:T(8,128)S(1)}, f32[2,256,128]{2,1,0:T(8,128)S(1)}, f32[2,256,128]{2,1,0:T(8,128)S(1)}, f32[2,128,128]{2,1,0:T(8,128)S(1)}, f32[16,2,40,128]{3,2,1,0:T(8,128)S(1)}) custom-call(s32[1]{0:T(128)} %bitcast.me_ref, f32[1280,128]{1,0:T(8,128)S(1)} %bitcast.8, f32[2,5,256,128]{3,2,1,0:T(8,128)S(1)} %get-tuple-element.17.x_part_ref, ...), custom_call_target="tpu_custom_call" | custom-call | tf_op jit(solution)/shard_map/y_lines/pallas_call | solution.py:514
  30.0 18.8 %all_to_all.5 = f32[16,2,40,128]{3,2,1,0:T(8,128)S(1)} all-to-all(f32[16,2,40,128]{3,2,1,0:T(8,128)S(1)} %get-tuple-element.22), channel_id=1, replica_groups=mesh['gx'=16,'gy'=16] {'gy'}, dimensions={0} | all-to-all | bytes 1310720 | tf_op jit(solution)/shard_map/all_to_all | solution.py:527
  48.8 1.7 %new_state.1 = f32[5,256,256]{2,1,0:T(8,128)} custom-call(s32[1]{0:T(128)} %bitcast.me_ref, f32[1280,128]{1,0:T(8,128)S(1)} %bitcast.9, f32[2,5,256,128]{3,2,1,0:T(8,128)S(1)} %get-tuple-element.23.part_ref, f32[2,256,128]{2,1,0:T(8,128)S(1)} %get-tuple-element.24.left_ref, f32[2,256,128]{2,1,0:T(8,128)S(1)} %get-tuple-element.25.right_ref, ...), custom_call_target="tpu_custom_call" | custom-call | tf_op jit(solution)/shard_map/new_state/pallas_call | solution.py:528

commit v4 on v3

--- a/solution.py
+++ b/solution.py
@@ -234,70 +234,110 @@
     return value
 
 
-def reduced_solve(me, devices, all_ref, coef_ref, out_ref):
-    def quantity(row):
-        return jnp.stack(
-            [all_ref[pl.ds(h * PAY_ROWS + row, devices, stride=2 * PAY_ROWS), :] for h in range(2)]
-        )
-
-    first_v, last_v = quantity(7), quantity(15)
-    hi_first, lo_last = quantity(ROW_HI), quantity(ROW_LO)
-    ids = sublane_ids(first_v.shape)
-    at_start, at_end = ids == 0, ids == devices - 1
-    v_below = jnp.where(at_start, 0.0, pltpu.roll(last_v, 1, 1))
-    v_above = jnp.where(at_end, 0.0, pltpu.roll(first_v, devices - 1, 1))
-    lo_first = 0.5 * (v_below + first_v)
-    hi_last = 0.5 * (last_v + v_above)
-    up_first = ONE_THIRD - hi_first
-    low_last = ONE_THIRD - lo_last
-    table = (
-        jnp.where(at_start, 0.0, ONE_THIRD - lo_first),
-        (1.0 + lo_first + hi_first) + up_first * quantity(5),
-        up_first * quantity(6),
-        low_last * quantity(13),
-        (1.0 + lo_last + hi_last) + low_last * quantity(14),
-        jnp.where(at_end, 0.0, ONE_THIRD - hi_last),
-        1.0 / up_first,
-        1.0 / low_last,
-    )
-    for i, value in enumerate(table):
-        coef_ref[:, i * devices : (i + 1) * devices, :] = value
-
-    def coef(i, d):
-        return coef_ref[:, i * devices + d : i * devices + d + 1, :]
-
-    def piece(d, row, size=8):
-        return jnp.stack([all_ref[pl.ds((2 * d + h) * PAY_ROWS + row, size), :] for h in range(2)])
-
-    def one(d, row):
-        return piece(d, row, 1)
-
-    chain, deltas = [], []
-    for d in range(devices):
-        rhs_first, rhs_last = piece(d, 0), piece(d, 8)
-        delta_second = delta_before = None
-        if d > 0:
-            delta_second = piece(d - 1, ROW_FLUX_RIGHT)
-            rhs_first = rhs_first + piece(d - 1, ROW_RIGHT) + one(d, 5) * delta_second
-            rhs_last = rhs_last + one(d, 6) * delta_second
-        if d < devices - 1:
-            delta_before = piece(d + 1, ROW_FLUX_LEFT)
-            rhs_first = rhs_first + one(d, 13) * delta_before
-            rhs_last = rhs_last + piece(d + 1, ROW_LEFT) + one(d, 14) * delta_before
-        deltas.append((delta_second, delta_before))
-        chain.append((coef(0, d), coef(1, d), coef(2, d), rhs_first))
-        chain.append((coef(3, d), coef(4, d), coef(5, d), rhs_last))
+def join(blocks, at_ends):
+    count = len(blocks)
+    one = lambda b, row: blocks[b](row, 1)
+    face = lambda b: 0.5 * (one(b, 15) + one(b + 1, 7))
+    chain, deltas, scales = [], [], []
+    for b in range(count):
+        rhs_first, rhs_last = blocks[b](0, 8), blocks[b](8, 8)
+        second = before = None
+        if b > 0:
+            second = blocks[b - 1](ROW_FLUX_RIGHT, 8)
+            rhs_first = rhs_first + blocks[b - 1](ROW_RIGHT, 8) + one(b, 5) * second
+            rhs_last = rhs_last + one(b, 6) * second
+        if b < count - 1:
+            before = blocks[b + 1](ROW_FLUX_LEFT, 8)
+            rhs_first = rhs_first + one(b, 13) * before
+            rhs_last = rhs_last + blocks[b + 1](ROW_LEFT, 8) + one(b, 14) * before
+        up, low = ONE_THIRD - one(b, ROW_HI), ONE_THIRD - one(b, ROW_LO)
+        lo_first = face(b - 1) if b > 0 else 0.5 * one(b, 7)
+        hi_last = face(b) if b < count - 1 else 0.5 * one(b, 15)
+        zero = jnp.zeros_like(up)
+        outer_low = ONE_THIRD - lo_first if b > 0 else zero
+        outer_up = ONE_THIRD - hi_last if b < count - 1 else zero
+        chain.append((outer_low, (1.0 + lo_first + one(b, ROW_HI)) + up * one(b, 5), up * one(b, 6), rhs_first))
+        chain.append((low * one(b, 13), (1.0 + one(b, ROW_LO) + hi_last) + low * one(b, 14), outer_up, rhs_last))
+        deltas.append((second, before))
+        scales.append((up, low))
+    return chain if at_ends else chain[1:-1], chain[0], chain[-1], deltas, scales
+
+
+def ordered(place, pay_refs, blocks_ref):
+    for k, pay_ref in enumerate(pay_refs):
+        blocks_ref[jnp.bitwise_xor(place, k)] = pay_ref[...]
+    return [lambda row, size, b=b: blocks_ref[b, :, row : row + size, :] for b in range(len(pay_refs))]
+
+
+def place_in(stage, me_ref):
+    first, size, _ = stage
+    return lax.rem(me_ref[0] // first, size)
+
+
+def merge_kernel(stage, me_ref, *refs):
+    size = stage[1]
+    pay_refs, (merged_ref, own_ref, blocks_ref, table_ref) = refs[:size], refs[size:]
+    place = place_in(stage, me_ref)
+    blocks = ordered(place, pay_refs, blocks_ref)
+    chain, first, last, deltas, scales = join(blocks, False)
+    eight = sublane_ids((2, 8, LANES))
+    is_field = eight < FIELDS
+    rhs = [jnp.where(is_field, value, 0.0) for _, _, _, value in chain]
+    rhs[0] = jnp.where(eight == 5, -chain[0][0], rhs[0])
+    rhs[-1] = jnp.where(eight == 6, -chain[-1][2], rhs[-1])
+    inner = solve_chain([(low, diag, up, value) for (low, diag, up, _), value in zip(chain, rhs)])
+
+    merged_ref[:, 0:8, :] = first[3] - first[2] * inner[0]
+    merged_ref[:, 8:16, :] = last[3] - last[0] * inner[-1]
+    merged_ref[:, 5:6, :] = blocks[0](5, 1) + blocks[0](6, 1) * inner[0][:, 5:6, :]
+    merged_ref[:, 6:7, :] = blocks[0](6, 1) * inner[0][:, 6:7, :]
+    merged_ref[:, 7:8, :] = blocks[0](7, 1)
+    merged_ref[:, 13:14, :] = blocks[-1](13, 1) * inner[-1][:, 5:6, :]
+    merged_ref[:, 14:15, :] = blocks[-1](14, 1) + blocks[-1](13, 1) * inner[-1][:, 6:7, :]
+    merged_ref[:, 15:16, :] = blocks[-1](15, 1)
+    for row, rows, block in (
+        (ROW_RIGHT, 5, -1), (ROW_HI, 1, 0), (ROW_FLUX_RIGHT, 5, -1), (ROW_LEFT, 10, 0), (ROW_LO, 1, -1)
+    ):
+        merged_ref[:, row : row + rows, :] = blocks[block](row, rows)
+    merged_ref[:, 38:40, :] = jnp.zeros((2, 2, LANES), jnp.float32)
+
+    for b in range(size):
+        zero = jnp.zeros((2, 8, LANES), jnp.float32)
+        own_first = jnp.where((eight == 5) | (eight == 7), 1.0, zero) if b == 0 else inner[2 * b - 1]
+        own_last = jnp.where((eight == 6) | (eight == 7), 1.0, zero) if b == size - 1 else inner[2 * b]
+        second, before = deltas[b]
+        second = zero if second is None else jnp.where(is_field, second / scales[b][0], 0.0)
+        before = zero if before is None else jnp.where(is_field, before / scales[b][1], 0.0)
+        for i, value in enumerate((own_first, own_last, second, before)):
+            table_ref[:, b * 32 + 8 * i : b * 32 + 8 * i + 8, :] = value
+    own_ref[...] = table_ref[:, pl.ds(pl.multiple_of(place * 32, 32), 32), :]
+
+
+def outer_solve(stage, me_ref, pay_refs, own_refs, blocks_ref, table_ref):
+    place = place_in(stage, me_ref)
+    chain, _, _, deltas, scales = join(ordered(place, pay_refs, blocks_ref), True)
     solved = solve_chain(chain)
-    for d in range(devices):
-        x_first, x_last = solved[2 * d], solved[2 * d + 1]
-        delta_second, delta_before = deltas[d]
-        seen_first = x_first if delta_second is None else x_first - delta_second * coef(6, d)
-        seen_last = x_last if delta_before is None else x_last - delta_before * coef(7, d)
+    for b in range(stage[1]):
+        x_first, x_last = solved[2 * b], solved[2 * b + 1]
+        second, before = deltas[b]
+        seen_first = x_first if second is None else x_first - second / scales[b][0]
+        seen_last = x_last if before is None else x_last - before / scales[b][1]
         for i, value in enumerate((x_first, x_last, seen_first, seen_last)):
-            out_ref[:, d * 32 + 8 * i : d * 32 + 8 * i + 8, :] = value
-    start = pl.multiple_of(me * 32, 32)
-    mine = out_ref[:, pl.ds(start, 32), :]
-    return [[mine[h, 8 * i : 8 * i + 8] for i in range(4)] for h in range(2)]
+            table_ref[:, b * 32 + 8 * i : b * 32 + 8 * i + 8, :] = value
+    mine = table_ref[:, pl.ds(pl.multiple_of(place * 32, 32), 32), :]
+    ends = [mine[:, 8 * i : 8 * i + 8] for i in range(4)]
+    for own_ref in own_refs:
+        x_first, x_last, seen_first, seen_last = ends
+        own_first, own_last, second, before = (own_ref[:, 8 * i : 8 * i + 8, :] for i in range(4))
+        first = own_first + own_first[:, 5:6] * seen_first + own_first[:, 6:7] * seen_last
+        last = own_last + own_last[:, 5:6] * seen_first + own_last[:, 6:7] * seen_last
+        ends = [
+            first + own_first[:, 7:8] * (x_first - seen_first),
+            last + own_last[:, 7:8] * (x_last - seen_last),
+            first - second,
+            last - before,
+        ]
+    return [[value[h] for value in ends] for h in range(2)]
 
 
 def rebuild(ends, count, part_ref, left_ref, right_ref, inner_ref, sol_ref):
@@ -395,12 +435,13 @@
     )
 
 
-def y_kernel(
-    count, devices, devices_y, me_ref, all_ref, x_part_ref, x_left_ref, x_right_ref, x_inner_ref, aux_ref,
-    part_ref, left_ref, right_ref, inner_ref, copies_ref,
-    coef_ref, out_ref, sol_ref, section_ref, turned_ref, first_ref, last_ref, pay_ref, sems,
-):
-    ends = reduced_solve(me_ref[0] // devices_y, devices, all_ref, coef_ref, out_ref)
+def y_kernel(count, stages, me_ref, *refs):
+    size, levels = stages[-1][1], len(stages) - 1
+    pay_refs, own_refs, refs = refs[:size], refs[size : size + levels], refs[size + levels :]
+    x_part_ref, x_left_ref, x_right_ref, x_inner_ref, aux_ref, *refs = refs
+    part_ref, left_ref, right_ref, inner_ref, pay_ref, *refs = refs
+    blocks_ref, table_ref, sol_ref, section_ref, turned_ref, first_ref, last_ref = refs
+    ends = outer_solve(stages[-1], me_ref, pay_refs, own_refs, blocks_ref, table_ref)
     for i in range(3):
         turn(count, aux_ref.at[:, i], turned_ref.at[FIELDS + i])
     halves = [
@@ -443,20 +484,14 @@
         lambda h: None, make_terms, viscous_at, count,
         part_ref, left_ref, right_ref, inner_ref, pay_ref, first_ref, last_ref,
     )
-    copies = [
-        pltpu.make_async_copy(pay_ref, copies_ref.at[d], sems.at[d]) for d in range(copies_ref.shape[0])
-    ]
-    for copy in copies:
-        copy.start()
-    for copy in copies:
-        copy.wait()
-
-
-def last_kernel(
-    count, devices, me_ref, all_ref, part_ref, left_ref, right_ref, inner_ref, new_ref,
-    coef_ref, out_ref, sol_ref, section_ref, turned_ref, sems,
-):
-    ends = reduced_solve(lax.rem(me_ref[0], devices), devices, all_ref, coef_ref, out_ref)
+
+
+def last_kernel(count, stages, me_ref, *refs):
+    size, levels = stages[-1][1], len(stages) - 1
+    pay_refs, own_refs, refs = refs[:size], refs[size : size + levels], refs[size + levels :]
+    part_ref, left_ref, right_ref, inner_ref, new_ref, *refs = refs
+    blocks_ref, table_ref, sol_ref, section_ref, turned_ref, sems = refs
+    ends = outer_solve(stages[-1], me_ref, pay_refs, own_refs, blocks_ref, table_ref)
     halves = [
         rebuild(ends[h], count, part_ref.at[h], left_ref.at[h], right_ref.at[h], inner_ref.at[h], sol_ref.at[h])
         for h in range(2)
@@ -505,38 +540,58 @@
         pltpu.with_memory_space_constraint(state.reshape(FIELDS, cells, cells), pltpu.HBM),
         pltpu.with_memory_space_constraint(viscous.reshape(cells, cells), pltpu.HBM),
     )
-    x_all = lax.all_gather(x_pay, "gx").reshape(devices_x * 2 * PAY_ROWS, LANES)
     me = (lax.axis_index("gx") * devices_y + lax.axis_index("gy")).astype(jnp.int32).reshape(1)
-
-    def solve_scratch(devices):
-        return [memory(2, 8 * devices, LANES), memory(2, 32 * devices, LANES), memory(2, 128, LANES)]
-
-    *y_parts, copies = pl.pallas_call(
-        functools.partial(y_kernel, count, devices_x, devices_y),
-        out_shape=solved_shapes + [float_of(devices_y, *pay_shape)],
-        in_specs=[scalar] + [whole] * 6,
-        out_specs=[whole] * 4 + [far],
-        scratch_shapes=solve_scratch(devices_x) + [
-            memory(FIELDS, 2, cells, LANES), memory(FIELDS + 3, 2, cells, LANES),
-            memory(2, 72, LANES), memory(2, 72, LANES), memory(*pay_shape),
-            pltpu.SemaphoreType.DMA((devices_y,)),
+    def merge_scratch(stage):
+        return [memory(stage[1], *pay_shape), memory(2, 32 * stage[1], LANES)]
+
+    def gather(pay, axis, stages):
+        owns = []
+        for stage in stages:
+            pays = [pay]
+            for mask in stage[2]:
+                pairs = [(i, i ^ mask) for i in range(lax.axis_size(axis))]
+                pays.append(lax.ppermute(pay, axis, pairs))
+            if stage is stages[-1]:
+                return pays + owns[::-1]
+            pay, own = pl.pallas_call(
+                functools.partial(merge_kernel, stage),
+                out_shape=[float_of(*pay_shape), float_of(2, 32, LANES)],
+                in_specs=[scalar] + [whole] * stage[1],
+                out_specs=[whole] * 2,
+                scratch_shapes=merge_scratch(stage),
+                compiler_params=params,
+                name="merge_" + axis,
+            )(me, *pays)
+            owns.append(own)
+
+    x_stages = ((devices_y, 2, (1,)), (2 * devices_y, 4, (2, 4, 6)), (8 * devices_y, 2, (14,)))
+    y_stages = ((1, 4, (1, 2, 3)), (4, 4, (4, 8, 12)))
+    x_ends = gather(x_pay, "gx", x_stages)
+    *y_parts, y_pay = pl.pallas_call(
+        functools.partial(y_kernel, count, x_stages),
+        out_shape=solved_shapes + [float_of(*pay_shape)],
+        in_specs=[scalar] + [whole] * (len(x_ends) + 5),
+        out_specs=[whole] * 5,
+        scratch_shapes=merge_scratch(x_stages[-1]) + [
+            memory(2, 128, LANES), memory(FIELDS, 2, cells, LANES), memory(FIELDS + 3, 2, cells, LANES),
+            memory(2, 72, LANES), memory(2, 72, LANES),
         ],
         compiler_params=params,
         name="y_lines",
-    )(me, x_all, *x_parts, aux)
-    y_all = lax.all_to_all(copies, "gy", 0, 0).reshape(devices_y * 2 * PAY_ROWS, LANES)
+    )(me, *x_ends, *x_parts, aux)
+    y_ends = gather(y_pay, "gy", y_stages)
     new = pl.pallas_call(
-        functools.partial(last_kernel, count, devices_y),
+        functools.partial(last_kernel, count, y_stages),
         out_shape=float_of(FIELDS, cells, cells),
-        in_specs=[scalar] + [whole] * 5,
+        in_specs=[scalar] + [whole] * (len(y_ends) + 4),
         out_specs=far,
-        scratch_shapes=solve_scratch(devices_y) + [
-            memory(FIELDS, 2, cells, LANES), memory(FIELDS, 2, cells, LANES),
+        scratch_shapes=merge_scratch(y_stages[-1]) + [
+            memory(2, 128, LANES), memory(FIELDS, 2, cells, LANES), memory(FIELDS, 2, cells, LANES),
             pltpu.SemaphoreType.DMA((FIELDS, 2)),
         ],
         compiler_params=params,
         name="new_state",
-    )(me, y_all, *y_parts)
+    )(me, *y_ends, *y_parts)
     return new.reshape(state.shape)
 
 

time: 50.7 us -> 41.2 us (0.81)
  the two profiles are of different devices: /device:TPU:1 before, /device:TPU:64 now
where the time goes in v4:
time: 41.2 us; the launch traced here: 41.1 us
  starting transfers between devices  16.9 us (41%)
  waiting for transfers between devices  16.8 us (41%)
  Pallas kernels  7.35 us (18%)
    ppermute x11, starting transfers between devices, gather(): pays.append(lax.ppermute(pay, axis, pairs))  16.9 us
    ppermute x11, waiting for transfers between devices, gather(): pays.append(lax.ppermute(pay, axis, pairs))  16.8 us
    pallas_call x1, Pallas kernels, shards(): pl.pallas_call(functools.partial(x_kernel, count), out_shape=solved_shape...  2.85 us
    pallas_call x1, Pallas kernels, shards(): pl.pallas_call(functools.partial(y_kernel, count, x_stages), out_shape=so...  2.81 us
    pallas_call x1, Pallas kernels, shards(): pl.pallas_call(functools.partial(last_kernel, count, y_stages), out_shape...  1.46 us
  transfers between devices with their start and end apart: 11, of which 8 were waited for; matrix products, arithmetic and copies ran while one was open for 0% of the time, Pallas kernels for 0%

profile of v4, /device:TPU:64, one launch (start us, length us, event | category | flops | bytes accessed | tf_op | source)
XLA Modules:
  0.0 41.1 jit_solution(5972194003180616892)
XLA Ops:
  0.0 2.9 %x_lines.1 = (f32[2,5,256,128]{3,2,1,0:T(8,128)S(1)}, f32[2,256,128]{2,1,0:T(8,128)S(1)}, f32[2,256,128]{2,1,0:T(8,128)S(1)}, f32[2,128,128]{2,1,0:T(8,128)S(1)}...) custom-call(f32[5,256,256]{2,1,0:T(8,128)} %bitcast.6, f32[256,256]{1,0:T(8,128)} %bitcast.7), custom_call_target="tpu_custom_call" | custom-call | tf_op jit(solution)/shard_map/x_lines/pallas_call | solution.py:528
  2.9 0.1 collective-permute-start
  3.0 1.2 %collective-permute-done.refs_1_ = f32[2,40,128]{2,1,0:T(8,128)S(1)} collective-permute-done((f32[2,40,128]{2,1,0:T(8,128)S(1)}, f32[2,40,128]{2,1,0:T(8,128)S(1)}, u32[]{:S(2)}, u32[]{:S(2)}) %collective-permute-start) | collective-permute-done | bytes 40992 | tf_op jit(solution)/shard_map/ppermute | solution.py:553
  4.2 0.1 merge_gx.2
  4.2 0.2 collective-permute-start.3
  4.4 4.2 %collective-permute-start.2 = (f32[2,40,128]{2,1,0:T(8,128)S(1)}, f32[2,40,128]{2,1,0:T(8,128)S(1)}, u32[]{:S(2)}, u32[]{:S(2)}) collective-permute-start(f32[2,40,128]{2,1,0:T(8,128)S(1)} %get-tuple-element.23.refs_0_), channel_id=1, source_target_pairs={{0,64},{16,80},{32,96},{48,112},{64,0},{80,16},{96,32},{112,48},{1... | collective-permute-start | bytes 122888 | tf_op jit(solution)/shard_map/ppermute | solution.py:553
  8.6 3.0 %collective-permute-done.2.refs_2_ = f32[2,40,128]{2,1,0:T(8,128)S(1)} collective-permute-done((f32[2,40,128]{2,1,0:T(8,128)S(1)}, f32[2,40,128]{2,1,0:T(8,128)S(1)}, u32[]{:S(2)}, u32[]{:S(2)}) %collective-permute-start.2) | collective-permute-done | bytes 40992 | tf_op jit(solution)/shard_map/ppermute | solution.py:553
  11.6 1.0 %collective-permute-done.1.refs_1_ = f32[2,40,128]{2,1,0:T(8,128)S(1)} collective-permute-done((f32[2,40,128]{2,1,0:T(8,128)S(1)}, f32[2,40,128]{2,1,0:T(8,128)S(1)}, u32[]{:S(2)}, u32[]{:S(2)}) %collective-permute-start.1) | collective-permute-done | bytes 40992 | tf_op jit(solution)/shard_map/ppermute | solution.py:553
  12.6 0.1 merge_gx.3
  12.7 4.1 %collective-permute-start.4 = (f32[2,40,128]{2,1,0:T(8,128)S(1)}, f32[2,40,128]{2,1,0:T(8,128)S(1)}, u32[]{:S(2)}, u32[]{:S(2)}) collective-permute-start(f32[2,40,128]{2,1,0:T(8,128)S(1)} %get-tuple-element.24.refs_0_), channel_id=1, source_target_pairs={{0,224},{16,240},{32,192},{48,208},{64,160},{80,176},{96,128},{112... | collective-permute-start | bytes 122888 | tf_op jit(solution)/shard_map/ppermute | solution.py:553
  16.8 3.0 %collective-permute-done.4.refs_1_ = f32[2,40,128]{2,1,0:T(8,128)S(1)} collective-permute-done((f32[2,40,128]{2,1,0:T(8,128)S(1)}, f32[2,40,128]{2,1,0:T(8,128)S(1)}, u32[]{:S(2)}, u32[]{:S(2)}) %collective-permute-start.4) | collective-permute-done | bytes 40992 | tf_op jit(solution)/shard_map/ppermute | solution.py:553
  19.8 2.8 %y_lines.1 = (f32[2,5,256,128]{3,2,1,0:T(8,128)S(1)}, f32[2,256,128]{2,1,0:T(8,128)S(1)}, f32[2,256,128]{2,1,0:T(8,128)S(1)}, f32[2,128,128]{2,1,0:T(8,128)S(1)}, f32[2,40,128]{2,1,0:T(8,128)S(1)}) custom-call(s32[1]{0:T(128)} %bitcast.me_ref, f32[2,40,128]{2,1,0:T(8,128)S(1)} %get-tuple-element.24.refs_0_, ...), custom_call_target="tpu_custom_call" | custom-call | tf_op jit(solution)/shard_map/y_lines/pallas_call | solution.py:570
  22.6 3.1 %collective-permute-start.7 = (f32[2,40,128]{2,1,0:T(8,128)S(1)}, f32[2,40,128]{2,1,0:T(8,128)S(1)}, u32[]{:S(2)}, u32[]{:S(2)}) collective-permute-start(f32[2,40,128]{2,1,0:T(8,128)S(1)} %get-tuple-element.32.refs_0_), channel_id=1, source_target_pairs={{0,3},{1,2},{2,1},{3,0},{4,7},{5,6},{6,5},{7,4},{8,11},{9,10},{10,... | collective-permute-start | bytes 122888 | tf_op jit(solution)/shard_map/ppermute | solution.py:553
  25.7 0.6 %collective-permute-start.6 = (f32[2,40,128]{2,1,0:T(8,128)S(1)}, f32[2,40,128]{2,1,0:T(8,128)S(1)}, u32[]{:S(2)}, u32[]{:S(2)}) collective-permute-start(f32[2,40,128]{2,1,0:T(8,128)S(1)} %get-tuple-element.32.refs_0_), channel_id=1, source_target_pairs={{0,2},{1,3},{2,0},{3,1},{4,6},{5,7},{6,4},{7,5},{8,10},{9,11},{10,... | collective-permute-start | bytes 122888 | tf_op jit(solution)/shard_map/ppermute | solution.py:553
  26.3 0.5 %collective-permute-start.5 = (f32[2,40,128]{2,1,0:T(8,128)S(1)}, f32[2,40,128]{2,1,0:T(8,128)S(1)}, u32[]{:S(2)}, u32[]{:S(2)}) collective-permute-start(f32[2,40,128]{2,1,0:T(8,128)S(1)} %get-tuple-element.32.refs_0_), channel_id=1, source_target_pairs={{0,1},{1,0},{2,3},{3,2},{4,5},{5,4},{6,7},{7,6},{8,9},{9,8},{10,11... | collective-permute-start | bytes 122888 | tf_op jit(solution)/shard_map/ppermute | solution.py:553
  26.8 1.3 %collective-permute-done.7.refs_3_ = f32[2,40,128]{2,1,0:T(8,128)S(1)} collective-permute-done((f32[2,40,128]{2,1,0:T(8,128)S(1)}, f32[2,40,128]{2,1,0:T(8,128)S(1)}, u32[]{:S(2)}, u32[]{:S(2)}) %collective-permute-start.7) | collective-permute-done | bytes 40992 | tf_op jit(solution)/shard_map/ppermute | solution.py:553
  28.1 3.1 %collective-permute-done.6.refs_2_ = f32[2,40,128]{2,1,0:T(8,128)S(1)} collective-permute-done((f32[2,40,128]{2,1,0:T(8,128)S(1)}, f32[2,40,128]{2,1,0:T(8,128)S(1)}, u32[]{:S(2)}, u32[]{:S(2)}) %collective-permute-start.6) | collective-permute-done | bytes 40992 | tf_op jit(solution)/shard_map/ppermute | solution.py:553
  31.2 0.1 merge_gy.1
  31.3 2.8 %collective-permute-start.10 = (f32[2,40,128]{2,1,0:T(8,128)S(1)}, f32[2,40,128]{2,1,0:T(8,128)S(1)}, u32[]{:S(2)}, u32[]{:S(2)}) collective-permute-start(f32[2,40,128]{2,1,0:T(8,128)S(1)} %get-tuple-element.33.refs_0_), channel_id=1, source_target_pairs={{0,12},{1,13},{2,14},{3,15},{4,8},{5,9},{6,10},{7,11},{8,4},{9,5},... | collective-permute-start | bytes 122888 | tf_op jit(solution)/shard_map/ppermute | solution.py:553
  34.1 0.8 %collective-permute-start.9 = (f32[2,40,128]{2,1,0:T(8,128)S(1)}, f32[2,40,128]{2,1,0:T(8,128)S(1)}, u32[]{:S(2)}, u32[]{:S(2)}) collective-permute-start(f32[2,40,128]{2,1,0:T(8,128)S(1)} %get-tuple-element.33.refs_0_), channel_id=1, source_target_pairs={{0,8},{1,9},{2,10},{3,11},{4,12},{5,13},{6,14},{7,15},{8,0},{9,1},... | collective-permute-start | bytes 122888 | tf_op jit(solution)/shard_map/ppermute | solution.py:553
  34.9 0.5 %collective-permute-start.8 = (f32[2,40,128]{2,1,0:T(8,128)S(1)}, f32[2,40,128]{2,1,0:T(8,128)S(1)}, u32[]{:S(2)}, u32[]{:S(2)}) collective-permute-start(f32[2,40,128]{2,1,0:T(8,128)S(1)} %get-tuple-element.33.refs_0_), channel_id=1, source_target_pairs={{0,4},{1,5},{2,6},{3,7},{4,0},{5,1},{6,2},{7,3},{8,12},{9,13},{10,... | collective-permute-start | bytes 122888 | tf_op jit(solution)/shard_map/ppermute | solution.py:553
  35.5 1.1 %collective-permute-done.10.refs_3_ = f32[2,40,128]{2,1,0:T(8,128)S(1)} collective-permute-done((f32[2,40,128]{2,1,0:T(8,128)S(1)}, f32[2,40,128]{2,1,0:T(8,128)S(1)}, u32[]{:S(2)}, u32[]{:S(2)}) %collective-permute-start.10) | collective-permute-done | bytes 40992 | tf_op jit(solution)/shard_map/ppermute | solution.py:553
  36.6 3.1 %collective-permute-done.9.refs_2_ = f32[2,40,128]{2,1,0:T(8,128)S(1)} collective-permute-done((f32[2,40,128]{2,1,0:T(8,128)S(1)}, f32[2,40,128]{2,1,0:T(8,128)S(1)}, u32[]{:S(2)}, u32[]{:S(2)}) %collective-permute-start.9) | collective-permute-done | bytes 40992 | tf_op jit(solution)/shard_map/ppermute | solution.py:553
  39.7 1.5 %new_state.1 = f32[5,256,256]{2,1,0:T(8,128)} custom-call(s32[1]{0:T(128)} %bitcast.me_ref, f32[2,40,128]{2,1,0:T(8,128)S(1)} %get-tuple-element.33.refs_0_, f32[2,40,128]{2,1,0:T(8,128)S(1)} %collective-permute-done.8.refs_1_, f32[2,40,128]{2,1,0:T(8,128)S(1)} %collective-permute-done.9.refs_2_, f32[2,40,128]{2,1,0:T(8,128)S(1)} %collective-permute-done.10.refs_3_, ...), custom_call_target="tpu_custom_call" | custom-call | tf_op jit(solution)/shard_map/new_state/pallas_call | solution.py:583
  (4 shorter events, 0.0 us)
Async XLA Ops:
  2.9 1.3 %collective-permute-start = (f32[2,40,128]{2,1,0:T(8,128)S(1)}, f32[2,40,128]{2,1,0:T(8,128)S(1)}, u32[]{:S(2)}, u32[]{:S(2)}) collective-permute-start(f32[2,40,128]{2,1,0:T(8,128)S(1)} %get-tuple-element.22.refs_0_), channel_id=1, source_target_pairs={{0,16},{16,0},{32,48},{48,32},{64,80},{80,64},{96,112},{112,96},{1... | collective-permute-start | bytes 122888 | tf_op jit(solution)/shard_map/ppermute | solution.py:553
  4.2 4.4 %collective-permute-start.3 = (f32[2,40,128]{2,1,0:T(8,128)S(1)}, f32[2,40,128]{2,1,0:T(8,128)S(1)}, u32[]{:S(2)}, u32[]{:S(2)}) collective-permute-start(f32[2,40,128]{2,1,0:T(8,128)S(1)} %get-tuple-element.23.refs_0_), channel_id=1, source_target_pairs={{0,96},{16,112},{32,64},{48,80},{64,32},{80,48},{96,0},{112,16},{1... | collective-permute-start | bytes 122888 | tf_op jit(solution)/shard_map/ppermute | solution.py:553
  4.4 7.1 %collective-permute-start.2 = (f32[2,40,128]{2,1,0:T(8,128)S(1)}, f32[2,40,128]{2,1,0:T(8,128)S(1)}, u32[]{:S(2)}, u32[]{:S(2)}) collective-permute-start(f32[2,40,128]{2,1,0:T(8,128)S(1)} %get-tuple-element.23.refs_0_), channel_id=1, source_target_pairs={{0,64},{16,80},{32,96},{48,112},{64,0},{80,16},{96,32},{112,48},{1... | collective-permute-start | bytes 122888 | tf_op jit(solution)/shard_map/ppermute | solution.py:553
  8.6 4.0 %collective-permute-start.1 = (f32[2,40,128]{2,1,0:T(8,128)S(1)}, f32[2,40,128]{2,1,0:T(8,128)S(1)}, u32[]{:S(2)}, u32[]{:S(2)}) collective-permute-start(f32[2,40,128]{2,1,0:T(8,128)S(1)} %get-tuple-element.23.refs_0_), channel_id=1, source_target_pairs={{0,32},{16,48},{32,0},{48,16},{64,96},{80,112},{96,64},{112,80},{1... | collective-permute-start | bytes 122888 | tf_op jit(solution)/shard_map/ppermute | solution.py:553
  12.7 7.1 %collective-permute-start.4 = (f32[2,40,128]{2,1,0:T(8,128)S(1)}, f32[2,40,128]{2,1,0:T(8,128)S(1)}, u32[]{:S(2)}, u32[]{:S(2)}) collective-permute-start(f32[2,40,128]{2,1,0:T(8,128)S(1)} %get-tuple-element.24.refs_0_), channel_id=1, source_target_pairs={{0,224},{16,240},{32,192},{48,208},{64,160},{80,176},{96,128},{112... | collective-permute-start | bytes 122888 | tf_op jit(solution)/shard_map/ppermute | solution.py:553
  22.6 5.5 %collective-permute-start.7 = (f32[2,40,128]{2,1,0:T(8,128)S(1)}, f32[2,40,128]{2,1,0:T(8,128)S(1)}, u32[]{:S(2)}, u32[]{:S(2)}) collective-permute-start(f32[2,40,128]{2,1,0:T(8,128)S(1)} %get-tuple-element.32.refs_0_), channel_id=1, source_target_pairs={{0,3},{1,2},{2,1},{3,0},{4,7},{5,6},{6,5},{7,4},{8,11},{9,10},{10,... | collective-permute-start | bytes 122888 | tf_op jit(solution)/shard_map/ppermute | solution.py:553
  25.7 5.5 %collective-permute-start.6 = (f32[2,40,128]{2,1,0:T(8,128)S(1)}, f32[2,40,128]{2,1,0:T(8,128)S(1)}, u32[]{:S(2)}, u32[]{:S(2)}) collective-permute-start(f32[2,40,128]{2,1,0:T(8,128)S(1)} %get-tuple-element.32.refs_0_), channel_id=1, source_target_pairs={{0,2},{1,3},{2,0},{3,1},{4,6},{5,7},{6,4},{7,5},{8,10},{9,11},{10,... | collective-permute-start | bytes 122888 | tf_op jit(solution)/shard_map/ppermute | solution.py:553
  26.3 4.9 %collective-permute-start.5 = (f32[2,40,128]{2,1,0:T(8,128)S(1)}, f32[2,40,128]{2,1,0:T(8,128)S(1)}, u32[]{:S(2)}, u32[]{:S(2)}) collective-permute-start(f32[2,40,128]{2,1,0:T(8,128)S(1)} %get-tuple-element.32.refs_0_), channel_id=1, source_target_pairs={{0,1},{1,0},{2,3},{3,2},{4,5},{5,4},{6,7},{7,6},{8,9},{9,8},{10,11... | collective-permute-start | bytes 122888 | tf_op jit(solution)/shard_map/ppermute | solution.py:553
  31.3 5.3 %collective-permute-start.10 = (f32[2,40,128]{2,1,0:T(8,128)S(1)}, f32[2,40,128]{2,1,0:T(8,128)S(1)}, u32[]{:S(2)}, u32[]{:S(2)}) collective-permute-start(f32[2,40,128]{2,1,0:T(8,128)S(1)} %get-tuple-element.33.refs_0_), channel_id=1, source_target_pairs={{0,12},{1,13},{2,14},{3,15},{4,8},{5,9},{6,10},{7,11},{8,4},{9,5},... | collective-permute-start | bytes 122888 | tf_op jit(solution)/shard_map/ppermute | solution.py:553
  34.1 5.5 %collective-permute-start.9 = (f32[2,40,128]{2,1,0:T(8,128)S(1)}, f32[2,40,128]{2,1,0:T(8,128)S(1)}, u32[]{:S(2)}, u32[]{:S(2)}) collective-permute-start(f32[2,40,128]{2,1,0:T(8,128)S(1)} %get-tuple-element.33.refs_0_), channel_id=1, source_target_pairs={{0,8},{1,9},{2,10},{3,11},{4,12},{5,13},{6,14},{7,15},{8,0},{9,1},... | collective-permute-start | bytes 122888 | tf_op jit(solution)/shard_map/ppermute | solution.py:553
  34.9 4.7 %collective-permute-start.8 = (f32[2,40,128]{2,1,0:T(8,128)S(1)}, f32[2,40,128]{2,1,0:T(8,128)S(1)}, u32[]{:S(2)}, u32[]{:S(2)}) collective-permute-start(f32[2,40,128]{2,1,0:T(8,128)S(1)} %get-tuple-element.33.refs_0_), channel_id=1, source_target_pairs={{0,4},{1,5},{2,6},{3,7},{4,0},{5,1},{6,2},{7,3},{8,12},{9,13},{10,... | collective-permute-start | bytes 122888 | tf_op jit(solution)/shard_map/ppermute | solution.py:553

commit v5 on v4

--- a/solution.py
+++ b/solution.py
@@ -36,48 +36,78 @@
     return jnp.where(sublane_ids(value.shape) == CHUNKS - 1, 0.0, pltpu.roll(value, CHUNKS - 1, value.ndim - 2))
 
 
-def local_solve(
-    ready, make_terms, viscous_at, count, part_ref, left_ref, right_ref, inner_ref, pay_ref, first_ref, last_ref
-):
-    final, middle = count - 1, count // 2
-    rows = lambda j: pl.ds(j * CHUNKS, CHUNKS)
-
-    @functools.cache
-    def viscous(j):
-        if j < 0:
-            return from_previous(viscous(j + count))
-        if j >= count:
-            return from_next(viscous(j - count))
-        return viscous_at(j)
-
-    face = functools.cache(lambda j: 0.5 * (viscous(j - 1) + viscous(j)))
-    coupling = functools.cache(lambda j: ONE_THIRD - face(j))
-
-    def diagonal(j):
-        return 1.0 + face(j) + face(j + 1)
-
-    inverse, tied, slope, reach = {}, {}, {}, {}
+class Matrix:
+    def __init__(self, viscous_at, count):
+        self.viscous_at, self.count, self.known = viscous_at, count, {}
+
+    def viscous(self, j):
+        if j not in self.known:
+            if j < 0:
+                value = from_previous(self.viscous(j + self.count))
+            elif j >= self.count:
+                value = from_next(self.viscous(j - self.count))
+            else:
+                value = self.viscous_at(j)
+            self.known[j] = value
+        return self.known[j]
+
+    def face(self, j):
+        return 0.5 * (self.viscous(j - 1) + self.viscous(j))
+
+    def coupling(self, j):
+        return ONE_THIRD - self.face(j)
+
+    def diagonal(self, j):
+        return 1.0 + self.face(j) + self.face(j + 1)
+
+
+class Rows:
+    def __init__(self, ref):
+        self.ref = ref
+
+    def __getitem__(self, j):
+        return self.ref[:, pl.ds(j * CHUNKS, CHUNKS), :]
+
+    def __setitem__(self, j, value):
+        self.ref[:, pl.ds(j * CHUNKS, CHUNKS), :] = value
+
+
+def eliminate_matrix(matrix, inverse, tied, slope, left, right):
+    final, middle = matrix.count - 1, matrix.count // 2
+    pivots, slopes, reach = {}, {}, {}
     for k in range(1, middle):
         for j, before, outer, inner in ((k, k - 1, k, k + 1), (final - k, final - k + 1, final - k + 1, final - k)):
-            pivot = diagonal(j)
+            pivot = matrix.diagonal(j)
             if k > 1:
-                pivot = pivot - coupling(outer) * slope[before]
-            inverse[j] = 1.0 / pivot
-            tied[j] = coupling(outer) * inverse[j]
-            slope[j] = coupling(inner) * inverse[j]
-            reach[j] = -tied[j] if k == 1 else -tied[j] * reach[before]
+                pivot = pivot - matrix.coupling(outer) * slopes[before]
+            pivots[j] = 1.0 / pivot
+            bound = matrix.coupling(outer) * pivots[j]
+            slopes[j] = matrix.coupling(inner) * pivots[j]
+            reach[j] = -bound if k == 1 else -bound * reach[before]
+            inverse[j], tied[j], slope[j] = pivots[j], bound, slopes[j]
     low, high = middle - 1, middle
-    meet = 1.0 / (1.0 - slope[low] * slope[high])
-    left, right = {}, {}
-    left[low], right[low] = reach[low] * meet, -(slope[low] * reach[high]) * meet
-    left[high], right[high] = -slope[high] * left[low], reach[high] - slope[high] * right[low]
+    meet = 1.0 / (1.0 - slopes[low] * slopes[high])
+    inverse[0] = meet
+    lefts, rights = {}, {}
+    lefts[low], rights[low] = reach[low] * meet, -(slopes[low] * reach[high]) * meet
+    lefts[high], rights[high] = -slopes[high] * lefts[low], reach[high] - slopes[high] * rights[low]
     for k in range(middle - 2, 0, -1):
-        left[k], right[k] = reach[k] - slope[k] * left[k + 1], -slope[k] * right[k + 1]
+        lefts[k], rights[k] = reach[k] - slopes[k] * lefts[k + 1], -slopes[k] * rights[k + 1]
         m = final - k
-        left[m], right[m] = -slope[m] * left[m - 1], reach[m] - slope[m] * right[m - 1]
+        lefts[m], rights[m] = -slopes[m] * lefts[m - 1], reach[m] - slopes[m] * rights[m - 1]
     for j in range(1, final):
-        left_ref[:, rows(j), :] = left[j]
-        right_ref[:, rows(j), :] = right[j]
+        left[j], right[j] = lefts[j], rights[j]
+
+
+def local_solve(ready, make_terms, matrix, factors, part_ref, inner_ref, pay_ref, first_ref, last_ref):
+    count = matrix.count
+    final, middle = count - 1, count // 2
+    low, high = middle - 1, middle
+    rows = lambda j: pl.ds(j * CHUNKS, CHUNKS)
+    viscous, face, coupling, diagonal = matrix.viscous, matrix.face, matrix.coupling, matrix.diagonal
+    inverse, tied, slope, all_left, all_right = factors
+    meet = inverse[0]
+    left, right = ({j: value[j] for j in (1, final - 1)} for value in (all_left, all_right))
 
     first = lambda value: value[..., 0:1, :]
     last = lambda value: value[..., CHUNKS - 1 : CHUNKS, :]
@@ -263,8 +293,8 @@
     return chain if at_ends else chain[1:-1], chain[0], chain[-1], deltas, scales
 
 
-def ordered(place, pay_refs, blocks_ref):
-    for k, pay_ref in enumerate(pay_refs):
+def ordered(stage, place, pay_refs, blocks_ref):
+    for k, pay_ref in zip((0,) + tuple(stage[2]), pay_refs):
         blocks_ref[jnp.bitwise_xor(place, k)] = pay_ref[...]
     return [lambda row, size, b=b: blocks_ref[b, :, row : row + size, :] for b in range(len(pay_refs))]
 
@@ -278,7 +308,7 @@
     size = stage[1]
     pay_refs, (merged_ref, own_ref, blocks_ref, table_ref) = refs[:size], refs[size:]
     place = place_in(stage, me_ref)
-    blocks = ordered(place, pay_refs, blocks_ref)
+    blocks = ordered(stage, place, pay_refs, blocks_ref)
     chain, first, last, deltas, scales = join(blocks, False)
     eight = sublane_ids((2, 8, LANES))
     is_field = eight < FIELDS
@@ -315,7 +345,7 @@
 
 def outer_solve(stage, me_ref, pay_refs, own_refs, blocks_ref, table_ref):
     place = place_in(stage, me_ref)
-    chain, _, _, deltas, scales = join(ordered(place, pay_refs, blocks_ref), True)
+    chain, _, _, deltas, scales = join(ordered(stage, place, pay_refs, blocks_ref), True)
     solved = solve_chain(chain)
     for b in range(stage[1]):
         x_first, x_last = solved[2 * b], solved[2 * b + 1]
@@ -430,20 +460,26 @@
         aux_ref[:, 2, pl.ds(j * CHUNKS, CHUNKS), :] = value
         return value
 
-    local_solve(
-        ready, make_terms, viscous_at, count, part_ref, left_ref, right_ref, inner_ref, pay_ref, first_ref, last_ref
-    )
+    matrix, factors = Matrix(viscous_at, count), ({}, {}, {}, Rows(left_ref), Rows(right_ref))
+    eliminate_matrix(matrix, *factors)
+    local_solve(ready, make_terms, matrix, factors, part_ref, inner_ref, pay_ref, first_ref, last_ref)
+
+
+def y_matrix_kernel(count, aux_ref, turned_ref, inverse_ref, tied_ref, slope_ref, left_ref, right_ref):
+    for i in range(3):
+        turn(count, aux_ref.at[:, i], turned_ref.at[i])
+    matrix = Matrix(lambda j: jnp.stack([strided(turned_ref.at[2, h], j, count) for h in range(2)]), count)
+    eliminate_matrix(matrix, *map(Rows, (inverse_ref, tied_ref, slope_ref, left_ref, right_ref)))
+    inverse_ref[:, (count - 1) * CHUNKS :, :] = jnp.zeros((2, CHUNKS, LANES), jnp.float32)
 
 
 def y_kernel(count, stages, me_ref, *refs):
     size, levels = stages[-1][1], len(stages) - 1
     pay_refs, own_refs, refs = refs[:size], refs[size : size + levels], refs[size + levels :]
     x_part_ref, x_left_ref, x_right_ref, x_inner_ref, aux_ref, *refs = refs
-    part_ref, left_ref, right_ref, inner_ref, pay_ref, *refs = refs
+    inverse_ref, tied_ref, slope_ref, left_ref, right_ref, part_ref, inner_ref, pay_ref, *refs = refs
     blocks_ref, table_ref, sol_ref, section_ref, turned_ref, first_ref, last_ref = refs
     ends = outer_solve(stages[-1], me_ref, pay_refs, own_refs, blocks_ref, table_ref)
-    for i in range(3):
-        turn(count, aux_ref.at[:, i], turned_ref.at[FIELDS + i])
     halves = [
         rebuild(
             ends[h], count, x_part_ref.at[h], x_left_ref.at[h], x_right_ref.at[h], x_inner_ref.at[h], sol_ref.at[h]
@@ -460,7 +496,7 @@
         return strided(turned_ref.at[q, h], j, count)
 
     def make_terms(h, j):
-        vel_y, press = value(FIELDS, h, j), value(FIELDS + 1, h, j)
+        vel_y, press = strided(aux_ref.at[0, h], j, count), strided(aux_ref.at[1, h], j, count)
         low, high, far = ONE_THIRD - vel_y, ONE_THIRD + vel_y, FAR_RATIO * vel_y
 
         def carried(u):
@@ -478,11 +514,12 @@
         )
 
     def viscous_at(j):
-        return jnp.stack([value(FIELDS + 2, h, j) for h in range(2)])
-
+        return jnp.stack([strided(aux_ref.at[2, h], j, count) for h in range(2)])
+
+    factors = tuple(map(Rows, (inverse_ref, tied_ref, slope_ref, left_ref, right_ref)))
     local_solve(
-        lambda h: None, make_terms, viscous_at, count,
-        part_ref, left_ref, right_ref, inner_ref, pay_ref, first_ref, last_ref,
+        lambda h: None, make_terms, Matrix(viscous_at, count), factors,
+        part_ref, inner_ref, pay_ref, first_ref, last_ref,
     )
 
 
@@ -548,7 +585,7 @@
         owns = []
         for stage in stages:
             pays = [pay]
-            for mask in stage[2]:
+            for mask in stage[2].values():
                 pairs = [(i, i ^ mask) for i in range(lax.axis_size(axis))]
                 pays.append(lax.ppermute(pay, axis, pairs))
             if stage is stages[-1]:
@@ -564,21 +601,35 @@
             )(me, *pays)
             owns.append(own)
 
-    x_stages = ((devices_y, 2, (1,)), (2 * devices_y, 4, (2, 4, 6)), (8 * devices_y, 2, (14,)))
-    y_stages = ((1, 4, (1, 2, 3)), (4, 4, (4, 8, 12)))
+    x_stages = (
+        (devices_y, 2, {1: 1}),
+        (2 * devices_y, 4, {1: 2, 2: 4, 3: 6}),
+        (8 * devices_y, 2, {1: 12}),
+    )
+    y_stages = ((1, 4, {1: 1, 3: 3, 2: 2}), (4, 4, {1: 4, 3: 12, 2: 8}))
     x_ends = gather(x_pay, "gx", x_stages)
-    *y_parts, y_pay = pl.pallas_call(
+    plane = float_of(2, cells, LANES)
+    y_aux, *y_factors = pl.pallas_call(
+        functools.partial(y_matrix_kernel, count),
+        out_shape=[float_of(3, 2, cells, LANES)] + [plane] * 5,
+        in_specs=[whole],
+        out_specs=[whole] * 6,
+        compiler_params=params,
+        cost_estimate=pl.CostEstimate(flops=4000000, bytes_accessed=2000000, transcendentals=0),
+        name="y_matrix",
+    )(aux)
+    y_part, y_inner, y_pay = pl.pallas_call(
         functools.partial(y_kernel, count, x_stages),
-        out_shape=solved_shapes + [float_of(*pay_shape)],
-        in_specs=[scalar] + [whole] * (len(x_ends) + 5),
-        out_specs=[whole] * 5,
+        out_shape=[solved_shapes[0], solved_shapes[3], float_of(*pay_shape)],
+        in_specs=[scalar] + [whole] * (len(x_ends) + 10),
+        out_specs=[whole] * 3,
         scratch_shapes=merge_scratch(x_stages[-1]) + [
-            memory(2, 128, LANES), memory(FIELDS, 2, cells, LANES), memory(FIELDS + 3, 2, cells, LANES),
+            memory(2, 128, LANES), memory(FIELDS, 2, cells, LANES), memory(FIELDS, 2, cells, LANES),
             memory(2, 72, LANES), memory(2, 72, LANES),
         ],
         compiler_params=params,
         name="y_lines",
-    )(me, *x_ends, *x_parts, aux)
+    )(me, *x_ends, *x_parts, y_aux, *y_factors)
     y_ends = gather(y_pay, "gy", y_stages)
     new = pl.pallas_call(
         functools.partial(last_kernel, count, y_stages),
@@ -591,7 +642,7 @@
         ],
         compiler_params=params,
         name="new_state",
-    )(me, *y_ends, *y_parts)
+    )(me, *y_ends, y_part, *y_factors[3:], y_inner)
     return new.reshape(state.shape)
 
 

time: 41.2 us -> 40.5 us (0.983)
  the two profiles are of different devices: /device:TPU:64 before, /device:TPU:6 now
where the time goes in v5:
time: 40.5 us; the launch traced here: 40.4 us
  starting transfers between devices  17.6 us (43%)
  waiting for transfers between devices  15.1 us (37%)
  Pallas kernels  7.62 us (19%)
    ppermute x11, starting transfers between devices, gather(): pays.append(lax.ppermute(pay, axis, pairs))  17.6 us
    ppermute x11, waiting for transfers between devices, gather(): pays.append(lax.ppermute(pay, axis, pairs))  15.1 us
    pallas_call x1, Pallas kernels, shards(): pl.pallas_call(functools.partial(x_kernel, count), out_shape=solved_shape...  2.86 us
    pallas_call x1, Pallas kernels, shards(): pl.pallas_call(functools.partial(y_kernel, count, x_stages), out_shape=[s...  2.52 us
    pallas_call x1, Pallas kernels, shards(): pl.pallas_call(functools.partial(last_kernel, count, y_stages), out_shape...  1.52 us
  transfers between devices with their start and end apart: 11, of which 9 were waited for; matrix products, arithmetic and copies ran while one was open for 0% of the time, Pallas kernels for 1%

profile of v5, /device:TPU:6, one launch (start us, length us, event | category | flops | bytes accessed | tf_op | source)
XLA Modules:
  0.0 40.4 jit_solution(18384188224182827827)
XLA Ops:
  0.0 2.9 %x_lines.1 = (f32[2,5,256,128]{3,2,1,0:T(8,128)S(1)}, f32[2,256,128]{2,1,0:T(8,128)S(1)}, f32[2,256,128]{2,1,0:T(8,128)S(1)}, f32[2,128,128]{2,1,0:T(8,128)S(1)}...) custom-call(f32[5,256,256]{2,1,0:T(8,128)} %bitcast.6, f32[256,256]{1,0:T(8,128)} %bitcast.7), custom_call_target="tpu_custom_call" | custom-call | tf_op jit(solution)/shard_map/x_lines/pallas_call | solution.py:565
  2.9 0.1 collective-permute-start
  3.0 1.2 %collective-permute-done.refs_1_ = f32[2,40,128]{2,1,0:T(8,128)S(1)} collective-permute-done((f32[2,40,128]{2,1,0:T(8,128)S(1)}, f32[2,40,128]{2,1,0:T(8,128)S(1)}, u32[]{:S(2)}, u32[]{:S(2)}) %collective-permute-start) | collective-permute-done | bytes 40992 | tf_op jit(solution)/shard_map/ppermute | solution.py:590
  4.2 0.1 merge_gx.2
  4.2 4.7 %collective-permute-start.3 = (f32[2,40,128]{2,1,0:T(8,128)S(1)}, f32[2,40,128]{2,1,0:T(8,128)S(1)}, u32[]{:S(2)}, u32[]{:S(2)}) collective-permute-start(f32[2,40,128]{2,1,0:T(8,128)S(1)} %get-tuple-element.27.refs_0_), channel_id=1, source_target_pairs={{0,96},{16,112},{32,64},{48,80},{64,32},{80,48},{96,0},{112,16},{1... | collective-permute-start | bytes 122888 | tf_op jit(solution)/shard_map/ppermute | solution.py:590
  8.9 0.7 %collective-permute-start.1 = (f32[2,40,128]{2,1,0:T(8,128)S(1)}, f32[2,40,128]{2,1,0:T(8,128)S(1)}, u32[]{:S(2)}, u32[]{:S(2)}) collective-permute-start(f32[2,40,128]{2,1,0:T(8,128)S(1)} %get-tuple-element.27.refs_0_), channel_id=1, source_target_pairs={{0,32},{16,48},{32,0},{48,16},{64,96},{80,112},{96,64},{112,80},{1... | collective-permute-start | bytes 122888 | tf_op jit(solution)/shard_map/ppermute | solution.py:590
  9.6 1.3 %collective-permute-done.3.refs_3_ = f32[2,40,128]{2,1,0:T(8,128)S(1)} collective-permute-done((f32[2,40,128]{2,1,0:T(8,128)S(1)}, f32[2,40,128]{2,1,0:T(8,128)S(1)}, u32[]{:S(2)}, u32[]{:S(2)}) %collective-permute-start.3) | collective-permute-done | bytes 40992 | tf_op jit(solution)/shard_map/ppermute | solution.py:590
  10.9 2.9 %collective-permute-done.2.refs_2_ = f32[2,40,128]{2,1,0:T(8,128)S(1)} collective-permute-done((f32[2,40,128]{2,1,0:T(8,128)S(1)}, f32[2,40,128]{2,1,0:T(8,128)S(1)}, u32[]{:S(2)}, u32[]{:S(2)}) %collective-permute-start.2) | collective-permute-done | bytes 40992 | tf_op jit(solution)/shard_map/ppermute | solution.py:590
  13.8 0.1 merge_gx.3
  13.9 4.2 %collective-permute-start.4 = (f32[2,40,128]{2,1,0:T(8,128)S(1)}, f32[2,40,128]{2,1,0:T(8,128)S(1)}, u32[]{:S(2)}, u32[]{:S(2)}) collective-permute-start(f32[2,40,128]{2,1,0:T(8,128)S(1)} %get-tuple-element.28.refs_0_), channel_id=1, source_target_pairs={{0,192},{16,208},{32,224},{48,240},{64,128},{80,144},{96,160},{112... | collective-permute-start | bytes 122888 | tf_op jit(solution)/shard_map/ppermute | solution.py:590
  18.2 0.5 %y_matrix.1 = (f32[3,2,256,128]{3,2,1,0:T(8,128)S(1)}, f32[2,256,128]{2,1,0:T(8,128)S(1)}, f32[2,256,128]{2,1,0:T(8,128)S(1)}, f32[2,256,128]{2,1,0:T(8,128)S(1)...) custom-call(f32[2,3,256,128]{3,2,1,0:T(8,128)S(1)} %get-tuple-element.35.aux_ref), custom_call_target="tpu_custom_call" | custom-call | flops 4000000 | bytes 2000000 | tf_op jit(solution)/shard_map/y_matrix/pallas_call | solution.py:612
  18.7 1.5 %collective-permute-done.4.refs_1_ = f32[2,40,128]{2,1,0:T(8,128)S(1)} collective-permute-done((f32[2,40,128]{2,1,0:T(8,128)S(1)}, f32[2,40,128]{2,1,0:T(8,128)S(1)}, u32[]{:S(2)}, u32[]{:S(2)}) %collective-permute-start.4) | collective-permute-done | bytes 40992 | tf_op jit(solution)/shard_map/ppermute | solution.py:590
  20.2 2.5 %y_lines.1 = (f32[2,5,256,128]{3,2,1,0:T(8,128)S(1)}, f32[2,128,128]{2,1,0:T(8,128)S(1)}, f32[2,40,128]{2,1,0:T(8,128)S(1)}) custom-call(s32[1]{0:T(128)} %bitcast.me_ref, f32[2,40,128]{2,1,0:T(8,128)S(1)} %get-tuple-element.28.refs_0_, f32[2,40,128]{2,1,0:T(8,128)S(1)} %collective-permute-done.4.refs_1_, f32[2,32,128]{2,1,0:T(8,128)S(1)} %get-tuple-element.29.refs_2_, ...), custom_call_target="tpu_custom_call" | custom-call | tf_op jit(solution)/shard_map/y_lines/pallas_call | solution.py:621
  22.7 3.3 %collective-permute-start.7 = (f32[2,40,128]{2,1,0:T(8,128)S(1)}, f32[2,40,128]{2,1,0:T(8,128)S(1)}, u32[]{:S(2)}, u32[]{:S(2)}) collective-permute-start(f32[2,40,128]{2,1,0:T(8,128)S(1)} %get-tuple-element.42.refs_0_), channel_id=1, source_target_pairs={{0,2},{1,3},{2,0},{3,1},{4,6},{5,7},{6,4},{7,5},{8,10},{9,11},{10,... | collective-permute-start | bytes 122888 | tf_op jit(solution)/shard_map/ppermute | solution.py:590
  26.0 1.1 %collective-permute-start.6 = (f32[2,40,128]{2,1,0:T(8,128)S(1)}, f32[2,40,128]{2,1,0:T(8,128)S(1)}, u32[]{:S(2)}, u32[]{:S(2)}) collective-permute-start(f32[2,40,128]{2,1,0:T(8,128)S(1)} %get-tuple-element.42.refs_0_), channel_id=1, source_target_pairs={{0,3},{1,2},{2,1},{3,0},{4,7},{5,6},{6,5},{7,4},{8,11},{9,10},{10,... | collective-permute-start | bytes 122888 | tf_op jit(solution)/shard_map/ppermute | solution.py:590
  27.0 1.3 %collective-permute-done.7.refs_3_ = f32[2,40,128]{2,1,0:T(8,128)S(1)} collective-permute-done((f32[2,40,128]{2,1,0:T(8,128)S(1)}, f32[2,40,128]{2,1,0:T(8,128)S(1)}, u32[]{:S(2)}, u32[]{:S(2)}) %collective-permute-start.7) | collective-permute-done | bytes 40992 | tf_op jit(solution)/shard_map/ppermute | solution.py:590
  28.3 2.9 %collective-permute-done.6.refs_2_ = f32[2,40,128]{2,1,0:T(8,128)S(1)} collective-permute-done((f32[2,40,128]{2,1,0:T(8,128)S(1)}, f32[2,40,128]{2,1,0:T(8,128)S(1)}, u32[]{:S(2)}, u32[]{:S(2)}) %collective-permute-start.6) | collective-permute-done | bytes 40992 | tf_op jit(solution)/shard_map/ppermute | solution.py:590
  31.2 0.1 merge_gy.1
  31.3 1.5 %collective-permute-start.10 = (f32[2,40,128]{2,1,0:T(8,128)S(1)}, f32[2,40,128]{2,1,0:T(8,128)S(1)}, u32[]{:S(2)}, u32[]{:S(2)}) collective-permute-start(f32[2,40,128]{2,1,0:T(8,128)S(1)} %get-tuple-element.43.refs_0_), channel_id=1, source_target_pairs={{0,8},{1,9},{2,10},{3,11},{4,12},{5,13},{6,14},{7,15},{8,0},{9,1},... | collective-permute-start | bytes 122888 | tf_op jit(solution)/shard_map/ppermute | solution.py:590
  32.8 2.1 %collective-permute-start.9 = (f32[2,40,128]{2,1,0:T(8,128)S(1)}, f32[2,40,128]{2,1,0:T(8,128)S(1)}, u32[]{:S(2)}, u32[]{:S(2)}) collective-permute-start(f32[2,40,128]{2,1,0:T(8,128)S(1)} %get-tuple-element.43.refs_0_), channel_id=1, source_target_pairs={{0,12},{1,13},{2,14},{3,15},{4,8},{5,9},{6,10},{7,11},{8,4},{9,5},... | collective-permute-start | bytes 122888 | tf_op jit(solution)/shard_map/ppermute | solution.py:590
  34.9 2.0 %collective-permute-done.10.refs_3_ = f32[2,40,128]{2,1,0:T(8,128)S(1)} collective-permute-done((f32[2,40,128]{2,1,0:T(8,128)S(1)}, f32[2,40,128]{2,1,0:T(8,128)S(1)}, u32[]{:S(2)}, u32[]{:S(2)}) %collective-permute-start.10) | collective-permute-done | bytes 40992 | tf_op jit(solution)/shard_map/ppermute | solution.py:590
  36.9 1.1 %collective-permute-done.9.refs_2_ = f32[2,40,128]{2,1,0:T(8,128)S(1)} collective-permute-done((f32[2,40,128]{2,1,0:T(8,128)S(1)}, f32[2,40,128]{2,1,0:T(8,128)S(1)}, u32[]{:S(2)}, u32[]{:S(2)}) %collective-permute-start.9) | collective-permute-done | bytes 40992 | tf_op jit(solution)/shard_map/ppermute | solution.py:590
  38.0 0.9 %collective-permute-done.8.refs_1_ = f32[2,40,128]{2,1,0:T(8,128)S(1)} collective-permute-done((f32[2,40,128]{2,1,0:T(8,128)S(1)}, f32[2,40,128]{2,1,0:T(8,128)S(1)}, u32[]{:S(2)}, u32[]{:S(2)}) %collective-permute-start.8) | collective-permute-done | bytes 40992 | tf_op jit(solution)/shard_map/ppermute | solution.py:590
  38.9 1.5 %new_state.1 = f32[5,256,256]{2,1,0:T(8,128)} custom-call(s32[1]{0:T(128)} %bitcast.me_ref, f32[2,40,128]{2,1,0:T(8,128)S(1)} %get-tuple-element.43.refs_0_, f32[2,40,128]{2,1,0:T(8,128)S(1)} %collective-permute-done.8.refs_1_, f32[2,40,128]{2,1,0:T(8,128)S(1)} %collective-permute-done.9.refs_2_, f32[2,40,128]{2,1,0:T(8,128)S(1)} %collective-permute-done.10.refs_3_, ...), custom_call_target="tpu_custom_call" | custom-call | tf_op jit(solution)/shard_map/new_state/pallas_call | solution.py:634
  (5 shorter events, 0.0 us)
Async XLA Ops:
  2.9 1.3 %collective-permute-start = (f32[2,40,128]{2,1,0:T(8,128)S(1)}, f32[2,40,128]{2,1,0:T(8,128)S(1)}, u32[]{:S(2)}, u32[]{:S(2)}) collective-permute-start(f32[2,40,128]{2,1,0:T(8,128)S(1)} %get-tuple-element.26.refs_0_), channel_id=1, source_target_pairs={{0,16},{16,0},{32,48},{48,32},{64,80},{80,64},{96,112},{112,96},{1... | collective-permute-start | bytes 122888 | tf_op jit(solution)/shard_map/ppermute | solution.py:590
  4.2 6.7 %collective-permute-start.3 = (f32[2,40,128]{2,1,0:T(8,128)S(1)}, f32[2,40,128]{2,1,0:T(8,128)S(1)}, u32[]{:S(2)}, u32[]{:S(2)}) collective-permute-start(f32[2,40,128]{2,1,0:T(8,128)S(1)} %get-tuple-element.27.refs_0_), channel_id=1, source_target_pairs={{0,96},{16,112},{32,64},{48,80},{64,32},{80,48},{96,0},{112,16},{1... | collective-permute-start | bytes 122888 | tf_op jit(solution)/shard_map/ppermute | solution.py:590
  8.9 4.9 %collective-permute-start.2 = (f32[2,40,128]{2,1,0:T(8,128)S(1)}, f32[2,40,128]{2,1,0:T(8,128)S(1)}, u32[]{:S(2)}, u32[]{:S(2)}) collective-permute-start(f32[2,40,128]{2,1,0:T(8,128)S(1)} %get-tuple-element.27.refs_0_), channel_id=1, source_target_pairs={{0,64},{16,80},{32,96},{48,112},{64,0},{80,16},{96,32},{112,48},{1... | collective-permute-start | bytes 122888 | tf_op jit(solution)/shard_map/ppermute | solution.py:590
  8.9 4.9 %collective-permute-start.1 = (f32[2,40,128]{2,1,0:T(8,128)S(1)}, f32[2,40,128]{2,1,0:T(8,128)S(1)}, u32[]{:S(2)}, u32[]{:S(2)}) collective-permute-start(f32[2,40,128]{2,1,0:T(8,128)S(1)} %get-tuple-element.27.refs_0_), channel_id=1, source_target_pairs={{0,32},{16,48},{32,0},{48,16},{64,96},{80,112},{96,64},{112,80},{1... | collective-permute-start | bytes 122888 | tf_op jit(solution)/shard_map/ppermute | solution.py:590
  13.9 6.2 %collective-permute-start.4 = (f32[2,40,128]{2,1,0:T(8,128)S(1)}, f32[2,40,128]{2,1,0:T(8,128)S(1)}, u32[]{:S(2)}, u32[]{:S(2)}) collective-permute-start(f32[2,40,128]{2,1,0:T(8,128)S(1)} %get-tuple-element.28.refs_0_), channel_id=1, source_target_pairs={{0,192},{16,208},{32,224},{48,240},{64,128},{80,144},{96,160},{112... | collective-permute-start | bytes 122888 | tf_op jit(solution)/shard_map/ppermute | solution.py:590
  22.7 5.6 %collective-permute-start.7 = (f32[2,40,128]{2,1,0:T(8,128)S(1)}, f32[2,40,128]{2,1,0:T(8,128)S(1)}, u32[]{:S(2)}, u32[]{:S(2)}) collective-permute-start(f32[2,40,128]{2,1,0:T(8,128)S(1)} %get-tuple-element.42.refs_0_), channel_id=1, source_target_pairs={{0,2},{1,3},{2,0},{3,1},{4,6},{5,7},{6,4},{7,5},{8,10},{9,11},{10,... | collective-permute-start | bytes 122888 | tf_op jit(solution)/shard_map/ppermute | solution.py:590
  26.0 5.2 %collective-permute-start.6 = (f32[2,40,128]{2,1,0:T(8,128)S(1)}, f32[2,40,128]{2,1,0:T(8,128)S(1)}, u32[]{:S(2)}, u32[]{:S(2)}) collective-permute-start(f32[2,40,128]{2,1,0:T(8,128)S(1)} %get-tuple-element.42.refs_0_), channel_id=1, source_target_pairs={{0,3},{1,2},{2,1},{3,0},{4,7},{5,6},{6,5},{7,4},{8,11},{9,10},{10,... | collective-permute-start | bytes 122888 | tf_op jit(solution)/shard_map/ppermute | solution.py:590
  27.0 4.2 %collective-permute-start.5 = (f32[2,40,128]{2,1,0:T(8,128)S(1)}, f32[2,40,128]{2,1,0:T(8,128)S(1)}, u32[]{:S(2)}, u32[]{:S(2)}) collective-permute-start(f32[2,40,128]{2,1,0:T(8,128)S(1)} %get-tuple-element.42.refs_0_), channel_id=1, source_target_pairs={{0,1},{1,0},{2,3},{3,2},{4,5},{5,4},{6,7},{7,6},{8,9},{9,8},{10,11... | collective-permute-start | bytes 122888 | tf_op jit(solution)/shard_map/ppermute | solution.py:590
  31.3 5.6 %collective-permute-start.10 = (f32[2,40,128]{2,1,0:T(8,128)S(1)}, f32[2,40,128]{2,1,0:T(8,128)S(1)}, u32[]{:S(2)}, u32[]{:S(2)}) collective-permute-start(f32[2,40,128]{2,1,0:T(8,128)S(1)} %get-tuple-element.43.refs_0_), channel_id=1, source_target_pairs={{0,8},{1,9},{2,10},{3,11},{4,12},{5,13},{6,14},{7,15},{8,0},{9,1},... | collective-permute-start | bytes 122888 | tf_op jit(solution)/shard_map/ppermute | solution.py:590
  32.8 5.2 %collective-permute-start.9 = (f32[2,40,128]{2,1,0:T(8,128)S(1)}, f32[2,40,128]{2,1,0:T(8,128)S(1)}, u32[]{:S(2)}, u32[]{:S(2)}) collective-permute-start(f32[2,40,128]{2,1,0:T(8,128)S(1)} %get-tuple-element.43.refs_0_), channel_id=1, source_target_pairs={{0,12},{1,13},{2,14},{3,15},{4,8},{5,9},{6,10},{7,11},{8,4},{9,5},... | collective-permute-start | bytes 122888 | tf_op jit(solution)/shard_map/ppermute | solution.py:590
  34.9 4.0 %collective-permute-start.8 = (f32[2,40,128]{2,1,0:T(8,128)S(1)}, f32[2,40,128]{2,1,0:T(8,128)S(1)}, u32[]{:S(2)}, u32[]{:S(2)}) collective-permute-start(f32[2,40,128]{2,1,0:T(8,128)S(1)} %get-tuple-element.43.refs_0_), channel_id=1, source_target_pairs={{0,4},{1,5},{2,6},{3,7},{4,0},{5,1},{6,2},{7,3},{8,12},{9,13},{10,... | collective-permute-start | bytes 122888 | tf_op jit(solution)/shard_map/ppermute | solution.py:590

commit v6 on v5

--- a/solution.py
+++ b/solution.py
@@ -138,7 +138,7 @@
             1: [from_previous(end[q][3]) for q in fields],
         }
         for j in range(count):
-            terms = make_terms(h, j)
+            terms = {final - 1: before, final: end}.get(j) or make_terms(h, j)
             if j == 0:
                 zero = terms
             if j == 1:

time: 40.5 us -> 40.5 us (level)
  no operation moved by 1% of the time
where the time goes in v6:
time: 40.5 us; the launch traced here: 40.4 us
  starting transfers between devices  17.6 us (43%)
  waiting for transfers between devices  15.1 us (37%)
  Pallas kernels  7.62 us (19%)
    ppermute x11, starting transfers between devices, gather(): pays.append(lax.ppermute(pay, axis, pairs))  17.6 us
    ppermute x11, waiting for transfers between devices, gather(): pays.append(lax.ppermute(pay, axis, pairs))  15.1 us
    pallas_call x1, Pallas kernels, shards(): pl.pallas_call(functools.partial(x_kernel, count), out_shape=solved_shape...  2.81 us
    pallas_call x1, Pallas kernels, shards(): pl.pallas_call(functools.partial(y_kernel, count, x_stages), out_shape=[s...  2.56 us
    pallas_call x1, Pallas kernels, shards(): pl.pallas_call(functools.partial(last_kernel, count, y_stages), out_shape...  1.52 us
  transfers between devices with their start and end apart: 11, of which 9 were waited for; matrix products, arithmetic and copies ran while one was open for 0% of the time, Pallas kernels for 1%

profile of v6, /device:TPU:6, one launch (start us, length us, event | category | flops | bytes accessed | tf_op | source)
XLA Modules:
  0.0 40.4 jit_solution(10116314716621637679)
XLA Ops:
  0.0 2.8 %x_lines.1 = (f32[2,5,256,128]{3,2,1,0:T(8,128)S(1)}, f32[2,256,128]{2,1,0:T(8,128)S(1)}, f32[2,256,128]{2,1,0:T(8,128)S(1)}, f32[2,128,128]{2,1,0:T(8,128)S(1)}...) custom-call(f32[5,256,256]{2,1,0:T(8,128)} %bitcast.6, f32[256,256]{1,0:T(8,128)} %bitcast.7), custom_call_target="tpu_custom_call" | custom-call | tf_op jit(solution)/shard_map/x_lines/pallas_call | solution.py:565
  2.8 0.1 collective-permute-start
  2.9 1.2 %collective-permute-done.refs_1_ = f32[2,40,128]{2,1,0:T(8,128)S(1)} collective-permute-done((f32[2,40,128]{2,1,0:T(8,128)S(1)}, f32[2,40,128]{2,1,0:T(8,128)S(1)}, u32[]{:S(2)}, u32[]{:S(2)}) %collective-permute-start) | collective-permute-done | bytes 40992 | tf_op jit(solution)/shard_map/ppermute | solution.py:590
  4.1 0.1 merge_gx.2
  4.2 4.7 %collective-permute-start.3 = (f32[2,40,128]{2,1,0:T(8,128)S(1)}, f32[2,40,128]{2,1,0:T(8,128)S(1)}, u32[]{:S(2)}, u32[]{:S(2)}) collective-permute-start(f32[2,40,128]{2,1,0:T(8,128)S(1)} %get-tuple-element.27.refs_0_), channel_id=1, source_target_pairs={{0,96},{16,112},{32,64},{48,80},{64,32},{80,48},{96,0},{112,16},{1... | collective-permute-start | bytes 122888 | tf_op jit(solution)/shard_map/ppermute | solution.py:590
  8.9 0.7 %collective-permute-start.1 = (f32[2,40,128]{2,1,0:T(8,128)S(1)}, f32[2,40,128]{2,1,0:T(8,128)S(1)}, u32[]{:S(2)}, u32[]{:S(2)}) collective-permute-start(f32[2,40,128]{2,1,0:T(8,128)S(1)} %get-tuple-element.27.refs_0_), channel_id=1, source_target_pairs={{0,32},{16,48},{32,0},{48,16},{64,96},{80,112},{96,64},{112,80},{1... | collective-permute-start | bytes 122888 | tf_op jit(solution)/shard_map/ppermute | solution.py:590
  9.6 1.3 %collective-permute-done.3.refs_3_ = f32[2,40,128]{2,1,0:T(8,128)S(1)} collective-permute-done((f32[2,40,128]{2,1,0:T(8,128)S(1)}, f32[2,40,128]{2,1,0:T(8,128)S(1)}, u32[]{:S(2)}, u32[]{:S(2)}) %collective-permute-start.3) | collective-permute-done | bytes 40992 | tf_op jit(solution)/shard_map/ppermute | solution.py:590
  10.9 2.9 %collective-permute-done.2.refs_2_ = f32[2,40,128]{2,1,0:T(8,128)S(1)} collective-permute-done((f32[2,40,128]{2,1,0:T(8,128)S(1)}, f32[2,40,128]{2,1,0:T(8,128)S(1)}, u32[]{:S(2)}, u32[]{:S(2)}) %collective-permute-start.2) | collective-permute-done | bytes 40992 | tf_op jit(solution)/shard_map/ppermute | solution.py:590
  13.8 0.1 merge_gx.3
  13.9 4.2 %collective-permute-start.4 = (f32[2,40,128]{2,1,0:T(8,128)S(1)}, f32[2,40,128]{2,1,0:T(8,128)S(1)}, u32[]{:S(2)}, u32[]{:S(2)}) collective-permute-start(f32[2,40,128]{2,1,0:T(8,128)S(1)} %get-tuple-element.28.refs_0_), channel_id=1, source_target_pairs={{0,192},{16,208},{32,224},{48,240},{64,128},{80,144},{96,160},{112... | collective-permute-start | bytes 122888 | tf_op jit(solution)/shard_map/ppermute | solution.py:590
  18.1 0.5 %y_matrix.1 = (f32[3,2,256,128]{3,2,1,0:T(8,128)S(1)}, f32[2,256,128]{2,1,0:T(8,128)S(1)}, f32[2,256,128]{2,1,0:T(8,128)S(1)}, f32[2,256,128]{2,1,0:T(8,128)S(1)...) custom-call(f32[2,3,256,128]{3,2,1,0:T(8,128)S(1)} %get-tuple-element.35.aux_ref), custom_call_target="tpu_custom_call" | custom-call | flops 4000000 | bytes 2000000 | tf_op jit(solution)/shard_map/y_matrix/pallas_call | solution.py:612
  18.6 1.5 %collective-permute-done.4.refs_1_ = f32[2,40,128]{2,1,0:T(8,128)S(1)} collective-permute-done((f32[2,40,128]{2,1,0:T(8,128)S(1)}, f32[2,40,128]{2,1,0:T(8,128)S(1)}, u32[]{:S(2)}, u32[]{:S(2)}) %collective-permute-start.4) | collective-permute-done | bytes 40992 | tf_op jit(solution)/shard_map/ppermute | solution.py:590
  20.1 2.6 %y_lines.1 = (f32[2,5,256,128]{3,2,1,0:T(8,128)S(1)}, f32[2,128,128]{2,1,0:T(8,128)S(1)}, f32[2,40,128]{2,1,0:T(8,128)S(1)}) custom-call(s32[1]{0:T(128)} %bitcast.me_ref, f32[2,40,128]{2,1,0:T(8,128)S(1)} %get-tuple-element.28.refs_0_, f32[2,40,128]{2,1,0:T(8,128)S(1)} %collective-permute-done.4.refs_1_, f32[2,32,128]{2,1,0:T(8,128)S(1)} %get-tuple-element.29.refs_2_, ...), custom_call_target="tpu_custom_call" | custom-call | tf_op jit(solution)/shard_map/y_lines/pallas_call | solution.py:621
  22.7 3.3 %collective-permute-start.7 = (f32[2,40,128]{2,1,0:T(8,128)S(1)}, f32[2,40,128]{2,1,0:T(8,128)S(1)}, u32[]{:S(2)}, u32[]{:S(2)}) collective-permute-start(f32[2,40,128]{2,1,0:T(8,128)S(1)} %get-tuple-element.42.refs_0_), channel_id=1, source_target_pairs={{0,2},{1,3},{2,0},{3,1},{4,6},{5,7},{6,4},{7,5},{8,10},{9,11},{10,... | collective-permute-start | bytes 122888 | tf_op jit(solution)/shard_map/ppermute | solution.py:590
  26.0 1.1 %collective-permute-start.6 = (f32[2,40,128]{2,1,0:T(8,128)S(1)}, f32[2,40,128]{2,1,0:T(8,128)S(1)}, u32[]{:S(2)}, u32[]{:S(2)}) collective-permute-start(f32[2,40,128]{2,1,0:T(8,128)S(1)} %get-tuple-element.42.refs_0_), channel_id=1, source_target_pairs={{0,3},{1,2},{2,1},{3,0},{4,7},{5,6},{6,5},{7,4},{8,11},{9,10},{10,... | collective-permute-start | bytes 122888 | tf_op jit(solution)/shard_map/ppermute | solution.py:590
  27.0 1.3 %collective-permute-done.7.refs_3_ = f32[2,40,128]{2,1,0:T(8,128)S(1)} collective-permute-done((f32[2,40,128]{2,1,0:T(8,128)S(1)}, f32[2,40,128]{2,1,0:T(8,128)S(1)}, u32[]{:S(2)}, u32[]{:S(2)}) %collective-permute-start.7) | collective-permute-done | bytes 40992 | tf_op jit(solution)/shard_map/ppermute | solution.py:590
  28.3 2.9 %collective-permute-done.6.refs_2_ = f32[2,40,128]{2,1,0:T(8,128)S(1)} collective-permute-done((f32[2,40,128]{2,1,0:T(8,128)S(1)}, f32[2,40,128]{2,1,0:T(8,128)S(1)}, u32[]{:S(2)}, u32[]{:S(2)}) %collective-permute-start.6) | collective-permute-done | bytes 40992 | tf_op jit(solution)/shard_map/ppermute | solution.py:590
  31.2 0.1 merge_gy.1
  31.3 1.5 %collective-permute-start.10 = (f32[2,40,128]{2,1,0:T(8,128)S(1)}, f32[2,40,128]{2,1,0:T(8,128)S(1)}, u32[]{:S(2)}, u32[]{:S(2)}) collective-permute-start(f32[2,40,128]{2,1,0:T(8,128)S(1)} %get-tuple-element.43.refs_0_), channel_id=1, source_target_pairs={{0,8},{1,9},{2,10},{3,11},{4,12},{5,13},{6,14},{7,15},{8,0},{9,1},... | collective-permute-start | bytes 122888 | tf_op jit(solution)/shard_map/ppermute | solution.py:590
  32.8 2.1 %collective-permute-start.9 = (f32[2,40,128]{2,1,0:T(8,128)S(1)}, f32[2,40,128]{2,1,0:T(8,128)S(1)}, u32[]{:S(2)}, u32[]{:S(2)}) collective-permute-start(f32[2,40,128]{2,1,0:T(8,128)S(1)} %get-tuple-element.43.refs_0_), channel_id=1, source_target_pairs={{0,12},{1,13},{2,14},{3,15},{4,8},{5,9},{6,10},{7,11},{8,4},{9,5},... | collective-permute-start | bytes 122888 | tf_op jit(solution)/shard_map/ppermute | solution.py:590
  34.9 2.0 %collective-permute-done.10.refs_3_ = f32[2,40,128]{2,1,0:T(8,128)S(1)} collective-permute-done((f32[2,40,128]{2,1,0:T(8,128)S(1)}, f32[2,40,128]{2,1,0:T(8,128)S(1)}, u32[]{:S(2)}, u32[]{:S(2)}) %collective-permute-start.10) | collective-permute-done | bytes 40992 | tf_op jit(solution)/shard_map/ppermute | solution.py:590
  36.9 1.1 %collective-permute-done.9.refs_2_ = f32[2,40,128]{2,1,0:T(8,128)S(1)} collective-permute-done((f32[2,40,128]{2,1,0:T(8,128)S(1)}, f32[2,40,128]{2,1,0:T(8,128)S(1)}, u32[]{:S(2)}, u32[]{:S(2)}) %collective-permute-start.9) | collective-permute-done | bytes 40992 | tf_op jit(solution)/shard_map/ppermute | solution.py:590
  38.0 0.9 %collective-permute-done.8.refs_1_ = f32[2,40,128]{2,1,0:T(8,128)S(1)} collective-permute-done((f32[2,40,128]{2,1,0:T(8,128)S(1)}, f32[2,40,128]{2,1,0:T(8,128)S(1)}, u32[]{:S(2)}, u32[]{:S(2)}) %collective-permute-start.8) | collective-permute-done | bytes 40992 | tf_op jit(solution)/shard_map/ppermute | solution.py:590
  38.9 1.5 %new_state.1 = f32[5,256,256]{2,1,0:T(8,128)} custom-call(s32[1]{0:T(128)} %bitcast.me_ref, f32[2,40,128]{2,1,0:T(8,128)S(1)} %get-tuple-element.43.refs_0_, f32[2,40,128]{2,1,0:T(8,128)S(1)} %collective-permute-done.8.refs_1_, f32[2,40,128]{2,1,0:T(8,128)S(1)} %collective-permute-done.9.refs_2_, f32[2,40,128]{2,1,0:T(8,128)S(1)} %collective-permute-done.10.refs_3_, ...), custom_call_target="tpu_custom_call" | custom-call | tf_op jit(solution)/shard_map/new_state/pallas_call | solution.py:634
  (5 shorter events, 0.0 us)
Async XLA Ops:
  2.8 1.3 %collective-permute-start = (f32[2,40,128]{2,1,0:T(8,128)S(1)}, f32[2,40,128]{2,1,0:T(8,128)S(1)}, u32[]{:S(2)}, u32[]{:S(2)}) collective-permute-start(f32[2,40,128]{2,1,0:T(8,128)S(1)} %get-tuple-element.26.refs_0_), channel_id=1, source_target_pairs={{0,16},{16,0},{32,48},{48,32},{64,80},{80,64},{96,112},{112,96},{1... | collective-permute-start | bytes 122888 | tf_op jit(solution)/shard_map/ppermute | solution.py:590
  4.2 6.7 %collective-permute-start.3 = (f32[2,40,128]{2,1,0:T(8,128)S(1)}, f32[2,40,128]{2,1,0:T(8,128)S(1)}, u32[]{:S(2)}, u32[]{:S(2)}) collective-permute-start(f32[2,40,128]{2,1,0:T(8,128)S(1)} %get-tuple-element.27.refs_0_), channel_id=1, source_target_pairs={{0,96},{16,112},{32,64},{48,80},{64,32},{80,48},{96,0},{112,16},{1... | collective-permute-start | bytes 122888 | tf_op jit(solution)/shard_map/ppermute | solution.py:590
  8.9 4.9 %collective-permute-start.2 = (f32[2,40,128]{2,1,0:T(8,128)S(1)}, f32[2,40,128]{2,1,0:T(8,128)S(1)}, u32[]{:S(2)}, u32[]{:S(2)}) collective-permute-start(f32[2,40,128]{2,1,0:T(8,128)S(1)} %get-tuple-element.27.refs_0_), channel_id=1, source_target_pairs={{0,64},{16,80},{32,96},{48,112},{64,0},{80,16},{96,32},{112,48},{1... | collective-permute-start | bytes 122888 | tf_op jit(solution)/shard_map/ppermute | solution.py:590
  8.9 4.9 %collective-permute-start.1 = (f32[2,40,128]{2,1,0:T(8,128)S(1)}, f32[2,40,128]{2,1,0:T(8,128)S(1)}, u32[]{:S(2)}, u32[]{:S(2)}) collective-permute-start(f32[2,40,128]{2,1,0:T(8,128)S(1)} %get-tuple-element.27.refs_0_), channel_id=1, source_target_pairs={{0,32},{16,48},{32,0},{48,16},{64,96},{80,112},{96,64},{112,80},{1... | collective-permute-start | bytes 122888 | tf_op jit(solution)/shard_map/ppermute | solution.py:590
  13.9 6.2 %collective-permute-start.4 = (f32[2,40,128]{2,1,0:T(8,128)S(1)}, f32[2,40,128]{2,1,0:T(8,128)S(1)}, u32[]{:S(2)}, u32[]{:S(2)}) collective-permute-start(f32[2,40,128]{2,1,0:T(8,128)S(1)} %get-tuple-element.28.refs_0_), channel_id=1, source_target_pairs={{0,192},{16,208},{32,224},{48,240},{64,128},{80,144},{96,160},{112... | collective-permute-start | bytes 122888 | tf_op jit(solution)/shard_map/ppermute | solution.py:590
  22.7 5.6 %collective-permute-start.7 = (f32[2,40,128]{2,1,0:T(8,128)S(1)}, f32[2,40,128]{2,1,0:T(8,128)S(1)}, u32[]{:S(2)}, u32[]{:S(2)}) collective-permute-start(f32[2,40,128]{2,1,0:T(8,128)S(1)} %get-tuple-element.42.refs_0_), channel_id=1, source_target_pairs={{0,2},{1,3},{2,0},{3,1},{4,6},{5,7},{6,4},{7,5},{8,10},{9,11},{10,... | collective-permute-start | bytes 122888 | tf_op jit(solution)/shard_map/ppermute | solution.py:590
  26.0 5.2 %collective-permute-start.6 = (f32[2,40,128]{2,1,0:T(8,128)S(1)}, f32[2,40,128]{2,1,0:T(8,128)S(1)}, u32[]{:S(2)}, u32[]{:S(2)}) collective-permute-start(f32[2,40,128]{2,1,0:T(8,128)S(1)} %get-tuple-element.42.refs_0_), channel_id=1, source_target_pairs={{0,3},{1,2},{2,1},{3,0},{4,7},{5,6},{6,5},{7,4},{8,11},{9,10},{10,... | collective-permute-start | bytes 122888 | tf_op jit(solution)/shard_map/ppermute | solution.py:590
  27.0 4.2 %collective-permute-start.5 = (f32[2,40,128]{2,1,0:T(8,128)S(1)}, f32[2,40,128]{2,1,0:T(8,128)S(1)}, u32[]{:S(2)}, u32[]{:S(2)}) collective-permute-start(f32[2,40,128]{2,1,0:T(8,128)S(1)} %get-tuple-element.42.refs_0_), channel_id=1, source_target_pairs={{0,1},{1,0},{2,3},{3,2},{4,5},{5,4},{6,7},{7,6},{8,9},{9,8},{10,11... | collective-permute-start | bytes 122888 | tf_op jit(solution)/shard_map/ppermute | solution.py:590
  31.3 5.6 %collective-permute-start.10 = (f32[2,40,128]{2,1,0:T(8,128)S(1)}, f32[2,40,128]{2,1,0:T(8,128)S(1)}, u32[]{:S(2)}, u32[]{:S(2)}) collective-permute-start(f32[2,40,128]{2,1,0:T(8,128)S(1)} %get-tuple-element.43.refs_0_), channel_id=1, source_target_pairs={{0,8},{1,9},{2,10},{3,11},{4,12},{5,13},{6,14},{7,15},{8,0},{9,1},... | collective-permute-start | bytes 122888 | tf_op jit(solution)/shard_map/ppermute | solution.py:590
  32.8 5.2 %collective-permute-start.9 = (f32[2,40,128]{2,1,0:T(8,128)S(1)}, f32[2,40,128]{2,1,0:T(8,128)S(1)}, u32[]{:S(2)}, u32[]{:S(2)}) collective-permute-start(f32[2,40,128]{2,1,0:T(8,128)S(1)} %get-tuple-element.43.refs_0_), channel_id=1, source_target_pairs={{0,12},{1,13},{2,14},{3,15},{4,8},{5,9},{6,10},{7,11},{8,4},{9,5},... | collective-permute-start | bytes 122888 | tf_op jit(solution)/shard_map/ppermute | solution.py:590
  34.9 4.0 %collective-permute-start.8 = (f32[2,40,128]{2,1,0:T(8,128)S(1)}, f32[2,40,128]{2,1,0:T(8,128)S(1)}, u32[]{:S(2)}, u32[]{:S(2)}) collective-permute-start(f32[2,40,128]{2,1,0:T(8,128)S(1)} %get-tuple-element.43.refs_0_), channel_id=1, source_target_pairs={{0,4},{1,5},{2,6},{3,7},{4,0},{5,1},{6,2},{7,3},{8,12},{9,13},{10,... | collective-permute-start | bytes 122888 | tf_op jit(solution)/shard_map/ppermute | solution.py:590
